TPU v7x, 32 devices: a whole 2x2x4 slice. The times are simulated.
32 devices in a mesh: wide: 8 (over y, x, core), narrow: 4 (over z).
Axes of the slice: x: 2, y: 2, z: 4, core: 2. Of those that a mesh axis runs over, the one named last changes fastest.
Arguments:
- tokens: bfloat16 [8, 2048, 768], P('wide', 'narrow'), may hold values from -6 to 6
- segment: int32 [8, 2048], P('wide'), may hold values from 0 to 10, as said below
- padding: int32 [8, 2048], P('wide'), may hold values from 0 to 1, as said below
- coords: int32 [2, 8, 2048], P(None, 'wide'), may hold values from 0 to 23, as said below
- ln1_gain: float32 [768], replicated, may hold values from 0.5 to 1.5
- ln1_shift: float32 [768], replicated, may hold values from -1 to 1
- query_key_value_weight: bfloat16 [768, 2304], replicated, may hold values from -0.21875 to 0.21875
- b_qkv: float32 [2304], replicated, may hold values from -3 to 3
- output_weight: bfloat16 [768, 768], replicated, may hold values from -0.875 to 0.875
- b_out: float32 [768], replicated, may hold values from -3 to 3
- rope_freqs: float32 [2, 12, 32], replicated, may hold values from -3 to 3
- ln2_gain: float32 [768], replicated, may hold values from 0.5 to 1.5
- ln2_shift: float32 [768], replicated, may hold values from -1 to 1
- w_up: bfloat16 [768, 3072], P(None, 'narrow'), may hold values from -0.21875 to 0.21875
- b_up: float32 [3072], P('narrow'), may hold values from -3 to 3
- w_down: bfloat16 [3072, 768], P('narrow')
- b_down: float32 [768], replicated, may hold values from -3 to 3
- cotangent: bfloat16 [8, 2048, 768], P('wide', 'narrow'), may hold values from -6 to 6
Outputs:
- activations: bfloat16 [8, 2048, 768], P('wide', 'narrow')
- input_grad: float32 [8, 2048, 768], P('wide', 'narrow')
- grad_ln1_gain: float32 [768], replicated
- grad_ln1_shift: float32 [768], replicated
- grad_w_qkv: float32 [768, 2304], replicated
- grad_b_qkv: float32 [2304], replicated
- grad_w_out: float32 [768, 768], replicated
- grad_b_out: float32 [768], replicated
- grad_freqs: float32 [2, 12, 32], replicated
- grad_ln2_gain: float32 [768], replicated
- grad_ln2_shift: float32 [768], replicated
- grad_w_up: float32 [768, 3072], P(None, 'narrow')
- grad_b_up: float32 [3072], P('narrow')
- grad_w_down: float32 [3072, 768], P('narrow')
- grad_b_down: float32 [768], replicated
- rot_sq: float32 [], replicated
- other_sq: float32 [], replicated
Inputs may be any that keep to these rules, and one draw needn't show every extreme that they name: `segment`: each sequence packs whole images of 14, 20 or 24 patches on a side in order while they fit; slots of one image carry its number, counted from 0; padding slots at the end carry the number after the last image. One sequence holds only 14-side images. `padding`: 1 exactly on the slots after the last image of a sequence. `coords`: row and column of a patch in its image, row by row; 0 on padding.
All inputs are finite; a program needn't handle non-finite values.
Results may differ from a plain program's by a relative error of at most 0.009.
The roundings to bfloat16 on the way count: a program that leaves them out, or rounds other values in their place, can miss the bound.
Values may be sent and summed in bfloat16 or wider, within the bound.
No kernel may reach another device: no remote copies, remote signals or barrier semaphores. Data moves between devices by JAX's collectives and lax.ppermute only.
A program may use at most 384 MiB of HBM per device.

v0:
```python
import jax
import jax.numpy as jnp
from jax import lax
from jax.sharding import PartitionSpec as P

QB = 512


EPS = 1e-06
MASKED = -1e30


def layer_norm(inputs, scales, token_shift):
    mean = jnp.mean(inputs, -1, keepdims=True)
    centred = inputs - mean
    variance = jnp.mean(centred * centred, -1, keepdims=True)
    return centred * lax.rsqrt(variance + EPS) * scales + token_shift


def rotate(tensor, angle):
    half_size = tensor.shape[-1] // 2
    first = tensor[..., :half_size]
    second = tensor[..., half_size:]
    cosine = jnp.cos(angle)
    sine_val = jnp.sin(angle)
    return jnp.concatenate(
        [first * cosine - second * sine_val, first * sine_val + second * cosine], -1
    )


def gelu_exact(inputs):
    return jax.nn.gelu(inputs, approximate=False)


def flat_dot(left, right):
    return lax.dot_general(
        left.reshape(-1, left.shape[-1]),
        right.reshape(-1, right.shape[-1]),
        (((0,), (0,)), ((), ())),
        preferred_element_type=jnp.float32,
    )


def row_total(tensor):
    return jnp.sum(tensor.astype(jnp.float32).reshape(-1, tensor.shape[-1]), 0)


def squares(tensor):
    return jnp.sum(tensor * tensor)


def on_device(
    tokens,
    segment,
    padding,
    coords,
    ln1_gain,
    ln1_shift,
    query_key_value_weight,
    b_qkv,
    output_weight,
    b_out,
    rope_freqs,
    ln2_gain,
    ln2_shift,
    w_up,
    b_up,
    w_down,
    b_down,
    cotangent,
):
    narrow_size = lax.axis_size("narrow")
    narrow_index = lax.axis_index("narrow")
    seq_count, own_len, model_width = tokens.shape
    seq_length = own_len * narrow_size
    head_count = rope_freqs.shape[1]
    head_size = model_width // head_count
    score_scale = head_size ** (-0.5)
    block_count = seq_length // QB
    position = jnp.arange(seq_length)
    grid_rows = coords[0].astype(jnp.float32)[..., None, None]
    grid_cols = coords[1].astype(jnp.float32)[..., None, None]

    def rotate_both(queries, keys_pre, freq_table):
        angle = grid_rows * freq_table[0] + grid_cols * freq_table[1]
        return (rotate(queries, angle), rotate(keys_pre, angle))

    def split_heads(tensor):
        return tensor.reshape(seq_count, seq_length, head_count, head_size)

    whole = lax.all_gather(tokens, "narrow", axis=1, tiled=True).astype(jnp.float32)
    norm1, ln1_pull = jax.vjp(layer_norm, whole, ln1_gain, ln1_shift)
    norm1_low = norm1.astype(jnp.bfloat16)
    proj_qkv = (
        jnp.dot(norm1_low, query_key_value_weight, preferred_element_type=jnp.float32) + b_qkv
    )
    queries = split_heads(proj_qkv[..., :model_width])
    keys_pre = split_heads(proj_qkv[..., model_width : 2 * model_width])
    values_low = split_heads(proj_qkv[..., 2 * model_width :]).astype(jnp.bfloat16)
    (rot_q, rot_k), rope_pull = jax.vjp(rotate_both, queries, keys_pre, rope_freqs)
    rot_q_low = rot_q.astype(jnp.bfloat16)
    rot_k_low = rot_k.astype(jnp.bfloat16)

    def masked_scores(start, q_block):
        seg_rows = lax.dynamic_slice_in_dim(segment, start, QB, 1)
        allowed = (seg_rows[:, :, None] == segment[:, None, :]) & (padding[:, None, :] == 0)
        allowed = allowed | ((start + jnp.arange(QB))[:, None] == position[None, :])[None]
        scores = (
            jnp.einsum("sqhd,skhd->shqk", q_block, rot_k_low, preferred_element_type=jnp.float32)
            * score_scale
        )
        return jnp.where(allowed[:, None], scores, MASKED)

    def forward_block(state_in, blk_index):
        start = blk_index * QB
        q_block = lax.dynamic_slice_in_dim(rot_q_low, start, QB, 1)
        scores = masked_scores(start, q_block)
        row_max = jnp.max(scores, -1, keepdims=True)
        shifted = jnp.exp(scores - row_max)
        row_sum = jnp.sum(shifted, -1, keepdims=True)
        prob_low = (shifted / row_sum).astype(jnp.bfloat16)
        attended = jnp.einsum(
            "shqk,skhd->sqhd", prob_low, values_low, preferred_element_type=jnp.float32
        )
        return (state_in, (attended, row_max + jnp.log(row_sum)))

    unused, (head_blocks, log_norm) = lax.scan(forward_block, None, jnp.arange(block_count))
    mixed_low = (
        jnp.moveaxis(head_blocks, 0, 1)
        .reshape(seq_count, seq_length, model_width)
        .astype(jnp.bfloat16)
    )
    out_partial = jnp.dot(mixed_low, output_weight, preferred_element_type=jnp.float32)
    attended = out_partial + b_out
    hidden = whole + attended
    norm2, ln2_pull = jax.vjp(layer_norm, hidden, ln2_gain, ln2_shift)
    norm2_low = norm2.astype(jnp.bfloat16)
    pre_act = jnp.dot(norm2_low, w_up, preferred_element_type=jnp.float32) + b_up
    activated, gelu_pull = jax.vjp(gelu_exact, pre_act)
    act_low = activated.astype(jnp.bfloat16)
    partial_out = jnp.dot(act_low, w_down, preferred_element_type=jnp.float32)
    mlp_out = lax.psum_scatter(
        partial_out.astype(jnp.bfloat16), "narrow", scatter_dimension=1, tiled=True
    ).astype(jnp.float32)
    own_hidden = lax.dynamic_slice_in_dim(hidden, narrow_index * own_len, own_len, 1)
    activations = (own_hidden + mlp_out + b_down).astype(jnp.bfloat16)
    grad_full = lax.all_gather(cotangent, "narrow", axis=1, tiled=True)
    grad_w_down = flat_dot(act_low, grad_full)
    grad_b_down = row_total(grad_full)
    d_act = jnp.einsum("slc,fc->slf", grad_full, w_down, preferred_element_type=jnp.float32)
    d_pre = gelu_pull(d_act)[0].astype(jnp.bfloat16)
    grad_w_up = flat_dot(norm2_low, d_pre)
    grad_b_up = row_total(d_pre)
    d_norm2_part = jnp.einsum("slf,cf->slc", d_pre, w_up, preferred_element_type=jnp.float32)
    d_norm2 = lax.psum(d_norm2_part, "narrow")
    d_from_ln2, grad_ln2_gain, grad_ln2_shift = ln2_pull(d_norm2)
    d_hidden = grad_full.astype(jnp.float32) + d_from_ln2
    mlp_small = jnp.concatenate([grad_ln2_gain, grad_ln2_shift, grad_b_down])
    attention_gradient = d_hidden.astype(jnp.bfloat16)
    grad_w_out = flat_dot(mixed_low, attention_gradient)
    grad_b_out = row_total(attention_gradient)
    d_heads = split_heads(
        jnp.einsum(
            "tym,vm->tyv", attention_gradient, output_weight, preferred_element_type=jnp.float32
        ).astype(jnp.bfloat16)
    )

    def backward_block(state_in, blk_index):
        d_keys, d_values = state_in
        start = blk_index * QB
        q_block = lax.dynamic_slice_in_dim(rot_q_low, start, QB, 1)
        grad_block = lax.dynamic_slice_in_dim(d_heads, start, QB, 1)
        attn_prob = jnp.exp(masked_scores(start, q_block) - log_norm[blk_index])
        prob_low = attn_prob.astype(jnp.bfloat16)
        d_values = d_values + jnp.einsum(
            "shqk,sqhd->skhd", prob_low, grad_block, preferred_element_type=jnp.float32
        )
        d_probs = jnp.einsum(
            "sqhd,skhd->shqk", grad_block, values_low, preferred_element_type=jnp.float32
        )
        row_dot = jnp.sum(attn_prob * d_probs, -1, keepdims=True)
        d_scores = (attn_prob * (d_probs - row_dot)).astype(jnp.bfloat16)
        d_query = (
            jnp.einsum("shqk,skhd->sqhd", d_scores, rot_k_low, preferred_element_type=jnp.float32)
            * score_scale
        )
        d_keys = (
            d_keys
            + jnp.einsum("shqk,sqhd->skhd", d_scores, q_block, preferred_element_type=jnp.float32)
            * score_scale
        )
        return ((d_keys, d_values), d_query)

    zero_heads = jnp.zeros((seq_count, seq_length, head_count, head_size), jnp.float32)
    (d_keys, d_values), query_blocks = lax.scan(
        backward_block, (zero_heads, zero_heads), jnp.arange(block_count)
    )
    d_queries = jnp.moveaxis(query_blocks, 0, 1).reshape(
        seq_count, seq_length, head_count, head_size
    )
    d_q_pre, d_k_pre, grad_rope = rope_pull((d_queries, d_keys))
    query_key_value_gradient = jnp.concatenate(
        [
            d_q_pre.reshape(seq_count, seq_length, model_width),
            d_k_pre.reshape(seq_count, seq_length, model_width),
            d_values.reshape(seq_count, seq_length, model_width),
        ],
        -1,
    ).astype(jnp.bfloat16)
    grad_w_qkv = flat_dot(norm1_low, query_key_value_gradient)
    grad_b_qkv = row_total(query_key_value_gradient)
    first_norm_gradient = jnp.einsum(
        "tym,vm->tyv",
        query_key_value_gradient,
        query_key_value_weight,
        preferred_element_type=jnp.float32,
    )
    d_from_ln1, grad_ln1_gain, grad_ln1_shift = ln1_pull(first_norm_gradient)
    input_full = d_hidden + d_from_ln1
    input_grad = lax.dynamic_slice_in_dim(input_full, narrow_index * own_len, own_len, 1)
    attn_small = jnp.concatenate([grad_ln1_gain, grad_ln1_shift, grad_b_out])
    summed = lax.psum(
        (
            grad_w_qkv,
            grad_w_out,
            grad_b_qkv,
            grad_rope,
            attn_small,
            grad_w_up,
            grad_b_up,
            grad_w_down,
            mlp_small,
        ),
        "wide",
    )
    attn_sums = (summed[0], summed[1], summed[2], summed[3], summed[4])
    mlp_sums = (summed[5], summed[6], summed[7], summed[8])
    total_w_qkv = attn_sums[0]
    total_w_out = attn_sums[1]
    total_b_qkv = attn_sums[2]
    total_freqs = attn_sums[3]
    small_total = attn_sums[4]
    total_ln1_gain = small_total[:model_width]
    total_ln1_shift = small_total[model_width : 2 * model_width]
    total_b_out = small_total[2 * model_width :]
    total_w_up = mlp_sums[0]
    total_b_up = mlp_sums[1]
    total_w_down = mlp_sums[2]
    total_ln2_gain = mlp_sums[3][:model_width]
    total_ln2_shift = mlp_sums[3][model_width : 2 * model_width]
    total_b_down = mlp_sums[3][2 * model_width :]
    rot_sq = squares(total_freqs)
    shared_sq = (
        squares(total_ln1_gain)
        + squares(total_ln1_shift)
        + squares(total_w_qkv)
        + squares(total_b_qkv)
    )
    shared_sq = (
        shared_sq
        + squares(total_w_out)
        + squares(total_b_out)
        + squares(total_ln2_gain)
        + squares(total_ln2_shift)
        + squares(total_b_down)
    )
    local_sq = (
        shared_sq / narrow_size + squares(total_w_up) + squares(total_b_up) + squares(total_w_down)
    )
    other_sq = lax.psum(local_sq, "narrow")
    return (
        activations,
        input_grad,
        total_ln1_gain,
        total_ln1_shift,
        total_w_qkv,
        total_b_qkv,
        total_w_out,
        total_b_out,
        total_freqs,
        total_ln2_gain,
        total_ln2_shift,
        total_w_up,
        total_b_up,
        total_w_down,
        total_b_down,
        rot_sq,
        other_sq,
    )


def solution(mesh):
    placed = (
        P("wide", "narrow", None),
        P("wide", None),
        P("wide", None),
        P(None, "wide", None),
        P(),
        P(),
        P(),
        P(),
        P(),
        P(),
        P(),
        P(),
        P(),
        P(None, "narrow"),
        P("narrow"),
        P("narrow", None),
        P(),
        P("wide", "narrow", None),
    )
    return jax.shard_map(
        on_device,
        mesh=mesh,
        in_specs=placed,
        out_specs=(
            P("wide", "narrow", None),
            P("wide", "narrow", None),
            P(),
            P(),
            P(),
            P(),
            P(),
            P(),
            P(),
            P(),
            P(),
            P(None, "narrow"),
            P("narrow"),
            P("narrow", None),
            P(),
            P(),
            P(),
        ),
        check_vma=False,
    )
```

profile of v0, /device:TPU:1, one launch (start us, length us, event | category | flops | bytes accessed | tf_op | source)
XLA Modules:
  0.0 1835.5 jit_solution(14922016407411045034)
XLA Ops:
  14.3 61.5 %all-gather.3.cloned.1.call-done = bf16[1,2048,768]{1,2,0:T(8,128)(2,1)} async-done(((bf16[1,512,768]{1,2,0:T(8,128)(2,1)}), bf16[1,2048,768]{1,2,0:T(8,128)(2,1)}) %all-gather.3.cloned.1.call-update) | async-done | bytes 3145744 | tf_op jit(solution)/shard_map/all_gather | solution.py:91
  126.1 15.1 subtract_convert_fusion
  145.8 290.7 %while.28 = (s32[]{:T(128)}, bf16[4,1,512,12,64]{2,4,3,1,0:T(8,128)(2,1)}, f32[4,1,12,512,1]{3,2,4,1,0:T(8,128)}, s32[4]{0:T(128)}, s32[1,2048]{1,0:T(1,128)S(1)...) while((s32[]{:T(128)}, ...), condition=%wide.region_5.6_spmd.clone, body=%wide.region_2.5_spmd.clone.sunk | while | flops 3376411136 | bytes 168368400 | solution.py:127
  150.1 23.1 %fusion.128 = (f32[12,512]{1,0:T(8,128)}, f32[12,512,2048]{2,1,0:T(8,128)}) fusion(pred[512,2048]{1,0:T(8,128)(4,1)} %fusion.127, bf16[1,2048,12,64]{1,3,2,0:T(8,128)(2,1)} %get-tuple-element.544, bf16[1,2048,12,64]{1,3,2,0:T(8,128)(2,1)} %get-tuple-element.543, s32[]{:T(128)S(6)} %select_n.65), kind=kOutput, calls=%fused_computation.5.clone.1 | convolution fusion | flops 1648355328 | bytes 55336964 | tf_op jit(solution)/shard_map/while/body/eval_jaxpr/sqhd,skhd->shqk/dot_general | solution.py:109
  173.2 22.9 %fusion.129 = f32[12,512]{1,0:T(8,128)S(1)} fusion(f32[12,512,2048]{2,1,0:T(8,128)} %get-tuple-element.495, f32[12,512]{1,0:T(8,128)} %get-tuple-element.496, pred[512,2048]{1,0:T(8,128)(4,1)} %fusion.127), kind=kLoop, calls=%fused_computation.6.clone.1 | loop fusion | flops 50325504 | bytes 51429376 | tf_op jit(solution)/shard_map/while/body/eval_jaxpr/reduce_sum | solution.py:120
  196.1 21.7 %bitcast_dynamic-update-slice_fusion.4 = bf16[4,1,512,12,64]{2,4,3,1,0:T(8,128)(2,1)} fusion(bf16[4,1,512,12,64]{2,4,3,1,0:T(8,128)(2,1)} %get-tuple-element.525, s32[]{:T(128)S(6)} %copy.119, bf16[1,2048,12,64]{1,3,2,0:T(8,128)(2,1)} %get-tuple-element.545, f32[12,512,2048]{2,1,0:T(8,128)} %get-tuple-element.495, f32[12,512]{1,0:T(8,128)S(1)} %fusion.129, ...), kind=kOutput, calls=%fused_computation.13.clone.1 | convolution fusion | flops 1673527296 | bytes 56147972 | tf_op jit(solution)/shard_map/while/body/eval_jaxpr/shqk,skhd->sqhd/dot_general | solution.py:122
  222.7 23.1 %fusion.128 = (f32[12,512]{1,0:T(8,128)}, f32[12,512,2048]{2,1,0:T(8,128)}) fusion(pred[512,2048]{1,0:T(8,128)(4,1)} %fusion.127, bf16[1,2048,12,64]{1,3,2,0:T(8,128)(2,1)} %get-tuple-element.544, bf16[1,2048,12,64]{1,3,2,0:T(8,128)(2,1)} %get-tuple-element.543, s32[]{:T(128)S(6)} %select_n.65), kind=kOutput, calls=%fused_computation.5.clone.1 | convolution fusion | flops 1648355328 | bytes 55336964 | tf_op jit(solution)/shard_map/while/body/eval_jaxpr/sqhd,skhd->shqk/dot_general | solution.py:109
  245.8 22.9 %fusion.129 = f32[12,512]{1,0:T(8,128)S(1)} fusion(f32[12,512,2048]{2,1,0:T(8,128)} %get-tuple-element.495, f32[12,512]{1,0:T(8,128)} %get-tuple-element.496, pred[512,2048]{1,0:T(8,128)(4,1)} %fusion.127), kind=kLoop, calls=%fused_computation.6.clone.1 | loop fusion | flops 50325504 | bytes 51429376 | tf_op jit(solution)/shard_map/while/body/eval_jaxpr/reduce_sum | solution.py:120
  268.7 21.7 %bitcast_dynamic-update-slice_fusion.4 = bf16[4,1,512,12,64]{2,4,3,1,0:T(8,128)(2,1)} fusion(bf16[4,1,512,12,64]{2,4,3,1,0:T(8,128)(2,1)} %get-tuple-element.525, s32[]{:T(128)S(6)} %copy.119, bf16[1,2048,12,64]{1,3,2,0:T(8,128)(2,1)} %get-tuple-element.545, f32[12,512,2048]{2,1,0:T(8,128)} %get-tuple-element.495, f32[12,512]{1,0:T(8,128)S(1)} %fusion.129, ...), kind=kOutput, calls=%fused_computation.13.clone.1 | convolution fusion | flops 1673527296 | bytes 56147972 | tf_op jit(solution)/shard_map/while/body/eval_jaxpr/shqk,skhd->sqhd/dot_general | solution.py:122
  295.2 23.1 %fusion.128 = (f32[12,512]{1,0:T(8,128)}, f32[12,512,2048]{2,1,0:T(8,128)}) fusion(pred[512,2048]{1,0:T(8,128)(4,1)} %fusion.127, bf16[1,2048,12,64]{1,3,2,0:T(8,128)(2,1)} %get-tuple-element.544, bf16[1,2048,12,64]{1,3,2,0:T(8,128)(2,1)} %get-tuple-element.543, s32[]{:T(128)S(6)} %select_n.65), kind=kOutput, calls=%fused_computation.5.clone.1 | convolution fusion | flops 1648355328 | bytes 55336964 | tf_op jit(solution)/shard_map/while/body/eval_jaxpr/sqhd,skhd->shqk/dot_general | solution.py:109
  318.4 22.9 %fusion.129 = f32[12,512]{1,0:T(8,128)S(1)} fusion(f32[12,512,2048]{2,1,0:T(8,128)} %get-tuple-element.495, f32[12,512]{1,0:T(8,128)} %get-tuple-element.496, pred[512,2048]{1,0:T(8,128)(4,1)} %fusion.127), kind=kLoop, calls=%fused_computation.6.clone.1 | loop fusion | flops 50325504 | bytes 51429376 | tf_op jit(solution)/shard_map/while/body/eval_jaxpr/reduce_sum | solution.py:120
  341.2 21.7 %bitcast_dynamic-update-slice_fusion.4 = bf16[4,1,512,12,64]{2,4,3,1,0:T(8,128)(2,1)} fusion(bf16[4,1,512,12,64]{2,4,3,1,0:T(8,128)(2,1)} %get-tuple-element.525, s32[]{:T(128)S(6)} %copy.119, bf16[1,2048,12,64]{1,3,2,0:T(8,128)(2,1)} %get-tuple-element.545, f32[12,512,2048]{2,1,0:T(8,128)} %get-tuple-element.495, f32[12,512]{1,0:T(8,128)S(1)} %fusion.129, ...), kind=kOutput, calls=%fused_computation.13.clone.1 | convolution fusion | flops 1673527296 | bytes 56147972 | tf_op jit(solution)/shard_map/while/body/eval_jaxpr/shqk,skhd->sqhd/dot_general | solution.py:122
  367.8 23.1 %fusion.128 = (f32[12,512]{1,0:T(8,128)}, f32[12,512,2048]{2,1,0:T(8,128)}) fusion(pred[512,2048]{1,0:T(8,128)(4,1)} %fusion.127, bf16[1,2048,12,64]{1,3,2,0:T(8,128)(2,1)} %get-tuple-element.544, bf16[1,2048,12,64]{1,3,2,0:T(8,128)(2,1)} %get-tuple-element.543, s32[]{:T(128)S(6)} %select_n.65), kind=kOutput, calls=%fused_computation.5.clone.1 | convolution fusion | flops 1648355328 | bytes 55336964 | tf_op jit(solution)/shard_map/while/body/eval_jaxpr/sqhd,skhd->shqk/dot_general | solution.py:109
  390.9 22.9 %fusion.129 = f32[12,512]{1,0:T(8,128)S(1)} fusion(f32[12,512,2048]{2,1,0:T(8,128)} %get-tuple-element.495, f32[12,512]{1,0:T(8,128)} %get-tuple-element.496, pred[512,2048]{1,0:T(8,128)(4,1)} %fusion.127), kind=kLoop, calls=%fused_computation.6.clone.1 | loop fusion | flops 50325504 | bytes 51429376 | tf_op jit(solution)/shard_map/while/body/eval_jaxpr/reduce_sum | solution.py:120
  413.8 21.7 %bitcast_dynamic-update-slice_fusion.4 = bf16[4,1,512,12,64]{2,4,3,1,0:T(8,128)(2,1)} fusion(bf16[4,1,512,12,64]{2,4,3,1,0:T(8,128)(2,1)} %get-tuple-element.525, s32[]{:T(128)S(6)} %copy.119, bf16[1,2048,12,64]{1,3,2,0:T(8,128)(2,1)} %get-tuple-element.545, f32[12,512,2048]{2,1,0:T(8,128)} %get-tuple-element.495, f32[12,512]{1,0:T(8,128)S(1)} %fusion.129, ...), kind=kOutput, calls=%fused_computation.13.clone.1 | convolution fusion | flops 1673527296 | bytes 56147972 | tf_op jit(solution)/shard_map/while/body/eval_jaxpr/shqk,skhd->sqhd/dot_general | solution.py:122
  450.1 18.9 %multiply_convert_fusion.1 = (bf16[2048,768]{1,0:T(8,128)(2,1)}, f32[2048,768]{1,0:T(8,128)}, f32[2048,768]{1,0:T(8,128)}) fusion(f32[768]{0:T(1024)S(1)} %copy-done.63, bf16[2048,768]{0,1:T(8,128)(2,1)S(1)} %fusion.64, bf16[768,768]{1,0:T(8,128)(2,1)S(1)} %copy-done.57), kind=kOutput, calls=%fused_computation.90 | convolution fusion | flops 2519728128 | bytes 20057088 | tf_op jit(solution)/shard_map/dot_general | solution.py:138
  507.8 200.8 %all-reduce.11.cloned.1.call-done = f32[1,2048,768]{1,2,0:T(8,128)} async-done(((f32[1,2048,768]{1,2,0:T(8,128)}), f32[1,2048,768]{1,2,0:T(8,128)}) %all-reduce.11.cloned.1.call-update) | async-done | bytes 6291472 | tf_op jit(solution)/shard_map/psum | solution.py:155
  730.5 795.3 %while.29 = (s32[]{:T(128)}, f32[1,2048,12,64]{1,3,2,0:T(8,128)}, f32[1,2048,12,64]{1,3,2,0:T(8,128)}, f32[4,1,512,12,64]{2,0,4,3,1:T(4,128)}, s32[4]{0:T(128)},...) while((s32[]{:T(128)}, f32[1,2048,12,64]{1,3,2,0:T(8,128)}, ...), condition=%wide.region_14.15_spmd.clone, body=%wide.region_12.14_spmd.clone.sunk | while | flops 8254255616 | bytes 433805600 | solution.py:195
  738.2 21.6 %fusion.138 = f32[12,512,2048]{2,1,0:T(8,128)} fusion(bf16[1,2048,12,64]{1,3,2,0:T(8,128)(2,1)} %get-tuple-element.592, bf16[1,2048,12,64]{1,3,2,0:T(8,128)(2,1)} %get-tuple-element.589, s32[]{:T(128)S(6)} %select_n.69), kind=kOutput, calls=%fused_computation.37.clone.1 | convolution fusion | flops 1610612736 | bytes 54263812 | tf_op jit(solution)/shard_map/while/body/eval_jaxpr/sqhd,skhd->shqk/dot_general | solution.py:109
  759.8 24.2 %bitcast_add_fusion.5 = f32[1,2048,12,64]{1,3,2,0:T(8,128)} fusion(f32[1,2048,12,64]{1,3,2,0:T(8,128)} %get-tuple-element.569, f32[12,512,2048]{2,1,0:T(8,128)} %fusion.138, f32[12,512]{1,0:T(8,128)} %dynamic-slice_bitcast_fusion.2, pred[512,2048]{1,0:T(8,128)(4,1)} %fusion.139, pred[]{:T(512)S(6)} %compare.9, ...), kind=kOutput, calls=%fused_computation.29.clone.1 | convolution fusion | flops 1664090112 | bytes 64782340 | tf_op jit(solution)/shard_map/while/body/eval_jaxpr/shqk,sqhd->skhd/dot_general | solution.py:175
  784.0 38.1 %multiply_reduce_fusion.20 = (f32[12,512]{1,0:T(8,128)}, f32[12,512,2048]{2,1,0:T(8,128)}) fusion(f32[12,512,2048]{2,1,0:T(8,128)} %fusion.138, f32[12,512]{1,0:T(8,128)} %dynamic-slice_bitcast_fusion.2, pred[512,2048]{1,0:T(8,128)(4,1)} %fusion.139, bf16[1,2048,12,64]{1,3,2,0:T(8,128)(2,1)} %get-tuple-element.595, ...), kind=kOutput, calls=%fused_computation.24.clone.1 | convolution fusion | flops 1673521152 | bytes 105701376 | tf_op jit(solution)/shard_map/while/body/eval_jaxpr/sqhd,skhd->shqk/dot_general | solution.py:178
  822.1 41.5 %multiply_convert_fusion.3 = bf16[12,512,2048]{2,1,0:T(8,128)(2,1)} fusion(f32[12,512,2048]{2,1,0:T(8,128)} %get-tuple-element.509, f32[12,512,2048]{2,1,0:T(8,128)} %fusion.138, f32[12,512]{1,0:T(8,128)} %get-tuple-element.510, f32[12,512]{1,0:T(8,128)} %dynamic-slice_bitcast_fusion.2, pred[512,2048]{1,0:T(8,128)(4,1)} %fusion.139), kind=kLoop, calls=%fused_computation.23.clone.1 | loop fusion | flops 75497472 | bytes 126926848 | tf_op jit(solution)/shard_map/while/body/eval_jaxpr/convert_element_type | solution.py:182
  863.6 14.2 multiply_bitcast_fusion.2
  877.8 15.6 bitcast_add_fusion.4
  896.2 31.1 %dynamic_update_slice.21 = f32[4,1,512,12,64]{2,0,4,3,1:T(4,128)} dynamic-update-slice(f32[4,1,512,12,64]{2,0,4,3,1:T(4,128)} %get-tuple-element.570, f32[1,1,512,12,64]{2,0,4,3,1:T(1,128)} %copy.112, s32[]{:T(128)S(6)} %copy.130, s32[]{:T(128)} %constant.75.clone.1..sunk.1, s32[]{:T(128)} %constant.75.clone.1..sunk.1, s32[]{:T(128)} %constant.75.clone.1..sunk.1, s32[]{:T(128)} %constant.75.clone.1..sunk.1) | dynamic-update-slice | bytes 3145732 | tf_op jit(solution)/shard_map/while/body/jit(dynamic_update_index_in_dim)/dynamic_update_slice | solution.py:127
  934.8 21.4 %fusion.138 = f32[12,512,2048]{2,1,0:T(8,128)} fusion(bf16[1,2048,12,64]{1,3,2,0:T(8,128)(2,1)} %get-tuple-element.592, bf16[1,2048,12,64]{1,3,2,0:T(8,128)(2,1)} %get-tuple-element.589, s32[]{:T(128)S(6)} %select_n.69), kind=kOutput, calls=%fused_computation.37.clone.1 | convolution fusion | flops 1610612736 | bytes 54263812 | tf_op jit(solution)/shard_map/while/body/eval_jaxpr/sqhd,skhd->shqk/dot_general | solution.py:109
  956.2 25.4 %bitcast_add_fusion.5 = f32[1,2048,12,64]{1,3,2,0:T(8,128)} fusion(f32[1,2048,12,64]{1,3,2,0:T(8,128)} %get-tuple-element.569, f32[12,512,2048]{2,1,0:T(8,128)} %fusion.138, f32[12,512]{1,0:T(8,128)} %dynamic-slice_bitcast_fusion.2, pred[512,2048]{1,0:T(8,128)(4,1)} %fusion.139, pred[]{:T(512)S(6)} %compare.9, ...), kind=kOutput, calls=%fused_computation.29.clone.1 | convolution fusion | flops 1664090112 | bytes 64782340 | tf_op jit(solution)/shard_map/while/body/eval_jaxpr/shqk,sqhd->skhd/dot_general | solution.py:175
  981.6 38.1 %multiply_reduce_fusion.20 = (f32[12,512]{1,0:T(8,128)}, f32[12,512,2048]{2,1,0:T(8,128)}) fusion(f32[12,512,2048]{2,1,0:T(8,128)} %fusion.138, f32[12,512]{1,0:T(8,128)} %dynamic-slice_bitcast_fusion.2, pred[512,2048]{1,0:T(8,128)(4,1)} %fusion.139, bf16[1,2048,12,64]{1,3,2,0:T(8,128)(2,1)} %get-tuple-element.595, ...), kind=kOutput, calls=%fused_computation.24.clone.1 | convolution fusion | flops 1673521152 | bytes 105701376 | tf_op jit(solution)/shard_map/while/body/eval_jaxpr/sqhd,skhd->shqk/dot_general | solution.py:178
  1019.7 41.5 %multiply_convert_fusion.3 = bf16[12,512,2048]{2,1,0:T(8,128)(2,1)} fusion(f32[12,512,2048]{2,1,0:T(8,128)} %get-tuple-element.509, f32[12,512,2048]{2,1,0:T(8,128)} %fusion.138, f32[12,512]{1,0:T(8,128)} %get-tuple-element.510, f32[12,512]{1,0:T(8,128)} %dynamic-slice_bitcast_fusion.2, pred[512,2048]{1,0:T(8,128)(4,1)} %fusion.139), kind=kLoop, calls=%fused_computation.23.clone.1 | loop fusion | flops 75497472 | bytes 126926848 | tf_op jit(solution)/shard_map/while/body/eval_jaxpr/convert_element_type | solution.py:182
  1075.4 17.4 bitcast_add_fusion.4
  1095.6 31.1 %dynamic_update_slice.21 = f32[4,1,512,12,64]{2,0,4,3,1:T(4,128)} dynamic-update-slice(f32[4,1,512,12,64]{2,0,4,3,1:T(4,128)} %get-tuple-element.570, f32[1,1,512,12,64]{2,0,4,3,1:T(1,128)} %copy.112, s32[]{:T(128)S(6)} %copy.130, s32[]{:T(128)} %constant.75.clone.1..sunk.1, s32[]{:T(128)} %constant.75.clone.1..sunk.1, s32[]{:T(128)} %constant.75.clone.1..sunk.1, s32[]{:T(128)} %constant.75.clone.1..sunk.1) | dynamic-update-slice | bytes 3145732 | tf_op jit(solution)/shard_map/while/body/jit(dynamic_update_index_in_dim)/dynamic_update_slice | solution.py:127
  1134.2 21.4 %fusion.138 = f32[12,512,2048]{2,1,0:T(8,128)} fusion(bf16[1,2048,12,64]{1,3,2,0:T(8,128)(2,1)} %get-tuple-element.592, bf16[1,2048,12,64]{1,3,2,0:T(8,128)(2,1)} %get-tuple-element.589, s32[]{:T(128)S(6)} %select_n.69), kind=kOutput, calls=%fused_computation.37.clone.1 | convolution fusion | flops 1610612736 | bytes 54263812 | tf_op jit(solution)/shard_map/while/body/eval_jaxpr/sqhd,skhd->shqk/dot_general | solution.py:109
  1155.6 25.4 %bitcast_add_fusion.5 = f32[1,2048,12,64]{1,3,2,0:T(8,128)} fusion(f32[1,2048,12,64]{1,3,2,0:T(8,128)} %get-tuple-element.569, f32[12,512,2048]{2,1,0:T(8,128)} %fusion.138, f32[12,512]{1,0:T(8,128)} %dynamic-slice_bitcast_fusion.2, pred[512,2048]{1,0:T(8,128)(4,1)} %fusion.139, pred[]{:T(512)S(6)} %compare.9, ...), kind=kOutput, calls=%fused_computation.29.clone.1 | convolution fusion | flops 1664090112 | bytes 64782340 | tf_op jit(solution)/shard_map/while/body/eval_jaxpr/shqk,sqhd->skhd/dot_general | solution.py:175
  1181.0 38.1 %multiply_reduce_fusion.20 = (f32[12,512]{1,0:T(8,128)}, f32[12,512,2048]{2,1,0:T(8,128)}) fusion(f32[12,512,2048]{2,1,0:T(8,128)} %fusion.138, f32[12,512]{1,0:T(8,128)} %dynamic-slice_bitcast_fusion.2, pred[512,2048]{1,0:T(8,128)(4,1)} %fusion.139, bf16[1,2048,12,64]{1,3,2,0:T(8,128)(2,1)} %get-tuple-element.595, ...), kind=kOutput, calls=%fused_computation.24.clone.1 | convolution fusion | flops 1673521152 | bytes 105701376 | tf_op jit(solution)/shard_map/while/body/eval_jaxpr/sqhd,skhd->shqk/dot_general | solution.py:178
  1219.1 41.5 %multiply_convert_fusion.3 = bf16[12,512,2048]{2,1,0:T(8,128)(2,1)} fusion(f32[12,512,2048]{2,1,0:T(8,128)} %get-tuple-element.509, f32[12,512,2048]{2,1,0:T(8,128)} %fusion.138, f32[12,512]{1,0:T(8,128)} %get-tuple-element.510, f32[12,512]{1,0:T(8,128)} %dynamic-slice_bitcast_fusion.2, pred[512,2048]{1,0:T(8,128)(4,1)} %fusion.139), kind=kLoop, calls=%fused_computation.23.clone.1 | loop fusion | flops 75497472 | bytes 126926848 | tf_op jit(solution)/shard_map/while/body/eval_jaxpr/convert_element_type | solution.py:182
  1274.8 17.4 bitcast_add_fusion.4
  1295.0 31.1 %dynamic_update_slice.21 = f32[4,1,512,12,64]{2,0,4,3,1:T(4,128)} dynamic-update-slice(f32[4,1,512,12,64]{2,0,4,3,1:T(4,128)} %get-tuple-element.570, f32[1,1,512,12,64]{2,0,4,3,1:T(1,128)} %copy.112, s32[]{:T(128)S(6)} %copy.130, s32[]{:T(128)} %constant.75.clone.1..sunk.1, s32[]{:T(128)} %constant.75.clone.1..sunk.1, s32[]{:T(128)} %constant.75.clone.1..sunk.1, s32[]{:T(128)} %constant.75.clone.1..sunk.1) | dynamic-update-slice | bytes 3145732 | tf_op jit(solution)/shard_map/while/body/jit(dynamic_update_index_in_dim)/dynamic_update_slice | solution.py:127
  1333.6 21.4 %fusion.138 = f32[12,512,2048]{2,1,0:T(8,128)} fusion(bf16[1,2048,12,64]{1,3,2,0:T(8,128)(2,1)} %get-tuple-element.592, bf16[1,2048,12,64]{1,3,2,0:T(8,128)(2,1)} %get-tuple-element.589, s32[]{:T(128)S(6)} %select_n.69), kind=kOutput, calls=%fused_computation.37.clone.1 | convolution fusion | flops 1610612736 | bytes 54263812 | tf_op jit(solution)/shard_map/while/body/eval_jaxpr/sqhd,skhd->shqk/dot_general | solution.py:109
  1355.0 25.4 %bitcast_add_fusion.5 = f32[1,2048,12,64]{1,3,2,0:T(8,128)} fusion(f32[1,2048,12,64]{1,3,2,0:T(8,128)} %get-tuple-element.569, f32[12,512,2048]{2,1,0:T(8,128)} %fusion.138, f32[12,512]{1,0:T(8,128)} %dynamic-slice_bitcast_fusion.2, pred[512,2048]{1,0:T(8,128)(4,1)} %fusion.139, pred[]{:T(512)S(6)} %compare.9, ...), kind=kOutput, calls=%fused_computation.29.clone.1 | convolution fusion | flops 1664090112 | bytes 64782340 | tf_op jit(solution)/shard_map/while/body/eval_jaxpr/shqk,sqhd->skhd/dot_general | solution.py:175
  1380.4 38.1 %multiply_reduce_fusion.20 = (f32[12,512]{1,0:T(8,128)}, f32[12,512,2048]{2,1,0:T(8,128)}) fusion(f32[12,512,2048]{2,1,0:T(8,128)} %fusion.138, f32[12,512]{1,0:T(8,128)} %dynamic-slice_bitcast_fusion.2, pred[512,2048]{1,0:T(8,128)(4,1)} %fusion.139, bf16[1,2048,12,64]{1,3,2,0:T(8,128)(2,1)} %get-tuple-element.595, ...), kind=kOutput, calls=%fused_computation.24.clone.1 | convolution fusion | flops 1673521152 | bytes 105701376 | tf_op jit(solution)/shard_map/while/body/eval_jaxpr/sqhd,skhd->shqk/dot_general | solution.py:178
  1418.5 41.5 %multiply_convert_fusion.3 = bf16[12,512,2048]{2,1,0:T(8,128)(2,1)} fusion(f32[12,512,2048]{2,1,0:T(8,128)} %get-tuple-element.509, f32[12,512,2048]{2,1,0:T(8,128)} %fusion.138, f32[12,512]{1,0:T(8,128)} %get-tuple-element.510, f32[12,512]{1,0:T(8,128)} %dynamic-slice_bitcast_fusion.2, pred[512,2048]{1,0:T(8,128)(4,1)} %fusion.139), kind=kLoop, calls=%fused_computation.23.clone.1 | loop fusion | flops 75497472 | bytes 126926848 | tf_op jit(solution)/shard_map/while/body/eval_jaxpr/convert_element_type | solution.py:182
  1460.0 14.2 multiply_bitcast_fusion.2
  1474.2 17.4 bitcast_add_fusion.4
  1494.4 31.1 %dynamic_update_slice.21 = f32[4,1,512,12,64]{2,0,4,3,1:T(4,128)} dynamic-update-slice(f32[4,1,512,12,64]{2,0,4,3,1:T(4,128)} %get-tuple-element.570, f32[1,1,512,12,64]{2,0,4,3,1:T(1,128)} %copy.112, s32[]{:T(128)S(6)} %copy.130, s32[]{:T(128)} %constant.75.clone.1..sunk.1, s32[]{:T(128)} %constant.75.clone.1..sunk.1, s32[]{:T(128)} %constant.75.clone.1..sunk.1, s32[]{:T(128)} %constant.75.clone.1..sunk.1) | dynamic-update-slice | bytes 3145732 | tf_op jit(solution)/shard_map/while/body/jit(dynamic_update_index_in_dim)/dynamic_update_slice | solution.py:127
  1539.5 18.5 %multiply_add_fusion = (f32[1,2048,12,32]{1,3,2,0:T(8,128)S(1)}, f32[1,2048,12,32]{1,3,2,0:T(8,128)S(1)}, f32[1,2048,12,32]{1,3,2,0:T(8,128)S(1)}, f32[1,2048,12,32]{1,3,2,0:T(8,128)S(1)}) fusion(f32[1,2048,12,64]{1,3,2,0:T(8,128)} %reshape_transpose.4, f32[1,2048,12,64]{1,3,2,0:T(8,128)} %bitcast.202, f32[1,2048,12,64]{1,3,2,0:T(8,128)} %bitcast.204, ...), kind=kLoop, calls=%fused_computation.122 | loop fusion | flops 27525120 | bytes 37768192 | tf_op jit(solution)/shard_map/transpose(jvp())/add_any | solution.py:24
  1581.0 15.5 fusion.83
  1637.4 25.1 %all-reduce.6 = (f32[2304]{0:T(1024)}, f32[2304]{0:T(1024)}, f32[2,12,32]{2,1,0:T(8,128)}, f32[2304]{0:T(1024)}, f32[768]{0:T(1024)}) all-reduce(f32[2304]{0:T(1024)} %pad_maximum_fusion.3, f32[2304]{0:T(1024)} %convert_reduce_fusion, f32[2,12,32]{2,1,0:T(8,128)S(1)} %pad_add_fusion, ...), channel_id=1, replica_groups=mesh['wide'=8,'narrow'=4] {'wide'}, use_global_device_ids=true, to_apply=%region_20.21 | all-reduce | flops 8448 | bytes 67584 | tf_op jit(solution)/shard_map/psum | solution.py:222
  1676.6 110.6 %all-reduce.13.cloned.1.call-done = (f32[768,2304]{1,0:T(8,128)}, f32[768,768]{1,0:T(8,128)}, f32[768,768]{1,0:T(8,128)}, f32[768,768]{1,0:T(8,128)}) async-done(((f32[768,2304]{1,0:T(8,128)}, f32[768,768]{1,0:T(8,128)}, f32[768,768]{1,0:T(8,128)}, f32[768,768]{1,0:T(8,128)}), (f32[768,2304]{1,0:T(8,128)}, f32[768,768]{1,0:T(8,128)}, f32[768,768]{1,0:T(8,128)}, ...) | async-done | bytes 14155792 | tf_op jit(solution)/shard_map/psum | solution.py:222
  (311 shorter events, 337.3 us)
Async XLA Ops:
  7.2 73.9 %copy-start = (bf16[768,2304]{1,0:T(8,128)(2,1)S(1)}, bf16[768,2304]{1,0:T(8,128)(2,1)}, u32[]{:S(2)}) copy-start(bf16[768,2304]{1,0:T(8,128)(2,1)} %param.28) | copy-start | bytes 10616836
  7.2 68.6 %all-gather.3.cloned.1.call-start = ((), (), s32[]{:S(2)}) async-start(), calls=%async_computation.1 | async-start | bytes 3932160 | tf_op jit(solution)/shard_map/all_gather | solution.py:91
  9.7 459.3 %all-gather.5.cloned.1.call-start = ((), (), s32[]{:S(2)}) async-start(), calls=%async_computation.3 | async-start | bytes 3932160 | tf_op jit(solution)/shard_map/all_gather | solution.py:147
  12.1 696.5 %all-reduce.11.cloned.1.call-start = ((), (), s32[]{:S(2)}) async-start(), calls=%async_computation.4 | async-start | bytes 12582912 | tf_op jit(solution)/shard_map/psum | solution.py:155
  14.3 111.8 %copy-start.32 = (f32[12,32]{1,0:T(8,128)}, f32[12,32]{1,0:T(8,128)S(1)}, u32[]{:S(2)}) copy-start(f32[12,32]{1,0:T(8,128)S(1)} %get-tuple-element.373) | copy-start | bytes 4612
  14.3 111.8 %copy-start.34 = (f32[12,32]{1,0:T(8,128)}, f32[12,32]{1,0:T(8,128)S(1)}, u32[]{:S(2)}) copy-start(f32[12,32]{1,0:T(8,128)S(1)} %get-tuple-element.374) | copy-start | bytes 4612
  78.3 10.9 copy-start.28
  81.1 8.1 copy-start.40
  81.1 8.1 copy-start.38
  89.2 6.5 copy-start.11
  173.2 22.9 %copy-start.1 = (pred[512,2048]{1,0:T(8,128)(4,1)S(1)}, pred[512,2048]{1,0:T(8,128)(4,1)}, u32[]{:S(2)}) copy-start(pred[512,2048]{1,0:T(8,128)(4,1)} %fusion.127) | copy-start | bytes 3145732 | tf_op jit(solution)/shard_map/while
  173.2 22.9 %copy-start.19 = (f32[12,512]{1,0:T(8,128)S(1)}, f32[12,512]{1,0:T(8,128)}, u32[]{:S(2)}) copy-start(f32[12,512]{1,0:T(8,128)} %get-tuple-element.496) | copy-start | bytes 73732 | tf_op jit(solution)/shard_map/while
  245.8 22.9 %copy-start.1 = (pred[512,2048]{1,0:T(8,128)(4,1)S(1)}, pred[512,2048]{1,0:T(8,128)(4,1)}, u32[]{:S(2)}) copy-start(pred[512,2048]{1,0:T(8,128)(4,1)} %fusion.127) | copy-start | bytes 3145732 | tf_op jit(solution)/shard_map/while
  245.8 22.9 %copy-start.19 = (f32[12,512]{1,0:T(8,128)S(1)}, f32[12,512]{1,0:T(8,128)}, u32[]{:S(2)}) copy-start(f32[12,512]{1,0:T(8,128)} %get-tuple-element.496) | copy-start | bytes 73732 | tf_op jit(solution)/shard_map/while
  318.3 22.9 %copy-start.1 = (pred[512,2048]{1,0:T(8,128)(4,1)S(1)}, pred[512,2048]{1,0:T(8,128)(4,1)}, u32[]{:S(2)}) copy-start(pred[512,2048]{1,0:T(8,128)(4,1)} %fusion.127) | copy-start | bytes 3145732 | tf_op jit(solution)/shard_map/while
  318.4 22.9 %copy-start.19 = (f32[12,512]{1,0:T(8,128)S(1)}, f32[12,512]{1,0:T(8,128)}, u32[]{:S(2)}) copy-start(f32[12,512]{1,0:T(8,128)} %get-tuple-element.496) | copy-start | bytes 73732 | tf_op jit(solution)/shard_map/while
  390.9 22.9 %copy-start.1 = (pred[512,2048]{1,0:T(8,128)(4,1)S(1)}, pred[512,2048]{1,0:T(8,128)(4,1)}, u32[]{:S(2)}) copy-start(pred[512,2048]{1,0:T(8,128)(4,1)} %fusion.127) | copy-start | bytes 3145732 | tf_op jit(solution)/shard_map/while
  390.9 22.9 %copy-start.19 = (f32[12,512]{1,0:T(8,128)S(1)}, f32[12,512]{1,0:T(8,128)}, u32[]{:S(2)}) copy-start(f32[12,512]{1,0:T(8,128)} %get-tuple-element.496) | copy-start | bytes 73732 | tf_op jit(solution)/shard_map/while
  469.1 13.3 copy-start.58
  486.9 1109.7 %reduce-scatter.2.cloned.1.call-start = ((), (), s32[]{:S(2)}) async-start(), calls=%async_computation.2 | async-start | bytes 3932160 | tf_op jit(solution)/shard_map/reduce_scatter | solution.py:142
  500.5 1286.7 %all-reduce.13.cloned.1.call-start = ((), (), s32[]{:S(2)}) async-start(), calls=%async_computation.5 | async-start | bytes 28311552 | tf_op jit(solution)/shard_map/psum | solution.py:222
  708.6 5.7 copy-start.43
  708.6 6.4 copy-start.4
  708.6 6.4 copy-start.27
  708.6 6.4 copy-start.31
  708.6 6.4 copy-start.45
  708.6 12.9 slice-start
  715.0 6.5 slice-start.1
  715.0 6.5 copy-start.23
  877.8 15.6 copy-start.9
  1075.4 17.4 copy-start.9
  1274.8 17.4 copy-start.9
  1474.2 17.4 copy-start.9
  1534.3 23.7 %slice-start.2 = ((s8[6291456]{0:T(1024)(128)(4,1)}), s8[4194304]{0:T(1024)(128)(4,1)S(1)}, s32[]{:S(2)}) async-start(s8[6291456]{0:T(1024)(128)(4,1)} %bitcast.199), calls=%async_computation.8 | async-start | bytes 8388608
  1539.5 18.6 %slice-start.3 = ((s8[6291456]{0:T(1024)(128)(4,1)}), s8[2097152]{0:T(1024)(128)(4,1)S(1)}, s32[]{:S(2)}) async-start(s8[6291456]{0:T(1024)(128)(4,1)} %bitcast.199), calls=%async_computation.9 | async-start | bytes 4194304
  1621.2 6.1 copy-start.5
  1621.2 7.0 copy-start.8
  1621.2 7.0 copy-start.52
  1628.3 5.7 copy-start.53
  1628.3 5.7 copy-start.56
  1628.3 6.3 copy-start.46
  1628.3 6.3 copy-start.47
  1628.3 6.3 copy-start.12
  1628.3 6.3 copy-start.13
  1628.3 7.0 copy-start.14
  1787.1 8.8 copy-start.10
  1817.9 6.6 copy-start.18
  1817.9 8.0 copy-start.17
  (39 other events, 157.6 us)
Sparse Core Ops, SparseCore 0:
  10.2 65.5 all-gather.2
  77.9 62.1 all-gather.4
  487.0 221.5 all-reduce.10
  710.8 59.0 reduce-scatter.1
  1596.7 190.4 all-reduce.12
where the time goes:
time: 1860 us; the launch traced here: 1840 us
  matrix products  746 us (40%)
  other arithmetic  401 us (22%)
  waiting for transfers between devices  373 us (20%)
  local copies, waits for them, and re-layouts  243 us (13%)
  blocking collectives  35.2 us (2%)
  between operations  22.4 us (1%)
    psum x1, waiting for transfers between devices, on_device(): d_norm2 = lax.psum(d_norm2_part, 'narrow')  201 us
    dot_general x8, matrix products, masked_scores(): jnp.einsum('sqhd,skhd->shqk', q_block, rot_k_low, preferred_element_type=...  178 us
    convert_element_type x4, other arithmetic, backward_block(): d_scores = (attn_prob * (d_probs - row_dot)).astype(jnp.bfloat16)  166 us
    dot_general x4, matrix products, backward_block(): jnp.einsum('sqhd,skhd->shqk', grad_block, values_low, preferred_element_t...  153 us
    dynamic_update_slice x8, local copies, waits for them, and re-layouts, on_device(): lax.scan(forward_block, None, jnp.arange(block_count))  135 us
    psum x1, waiting for transfers between devices, on_device(): lax.psum((grad_w_qkv, grad_w_out, grad_b_qkv, grad_rope, attn_small, grad...  111 us
    dot_general x4, matrix products, backward_block(): jnp.einsum('shqk,sqhd->skhd', prob_low, grad_block, preferred_element_typ...  100 us
    reduce_sum x4, other arithmetic, forward_block(): row_sum = jnp.sum(shifted, -1, keepdims=True)  91.5 us
  transfers between devices with their start and end apart: 5, of which 3 were waited for; matrix products, arithmetic and copies ran while one was open for 72% of the time, Pallas kernels for 0%

commit v1 on v0

v1 whole, which is shorter than its diff:
```python
import functools

import jax
import jax.numpy as jnp
import numpy as np
from jax import lax
from jax.experimental import pallas as pl
from jax.experimental.pallas import tpu as pltpu
from jax.sharding import Mesh, PartitionSpec as P

EPS = 1e-06
MASKED = -1e30
BLK = 128
CHUNK = 256
GROUP = 4
REACH = 64
STAT_ROWS = 6
STAT_PAD = 16
SIDE = 32
LN1_GAIN, LN1_SHIFT, B_OUT, LN2_GAIN, LN2_SHIFT, B_DOWN = (slice(n, n + 1) for n in range(6))
BF = jnp.bfloat16
F32 = jnp.float32
PLANE = ("a", "b", "c")
SWAP = [(0, 1), (1, 0)]
VMEM_LIMIT = 56 * 1024 * 1024


def dot(left, right):
    return lax.dot_general(left, right, (((1,), (0,)), ((), ())), preferred_element_type=F32)


def dot_nt(left, right):
    return lax.dot_general(left, right, (((1,), (1,)), ((), ())), preferred_element_type=F32)


def dot_tn(left, right):
    return lax.dot_general(left, right, (((0,), (0,)), ((), ())), preferred_element_type=F32)


def params(**kw):
    return pltpu.CompilerParams(vmem_limit_bytes=VMEM_LIMIT, **kw)


def cost(us):
    return pl.CostEstimate(
        flops=int(us * 1.15e9), bytes_accessed=int(us * 3.0e6), transcendentals=0
    )


def whole(shape):
    return pl.BlockSpec(shape, lambda *_: (0,) * len(shape))


ANY = pl.BlockSpec(memory_space=pl.ANY)
SMEM = pl.BlockSpec(memory_space=pltpu.SMEM)


def rounded(x):
    return lax.reduce_precision(x, exponent_bits=8, mantissa_bits=7)


def turn_table(rope_freqs):
    lanes = rope_freqs.shape[1] * rope_freqs.shape[2]
    freq = rope_freqs.reshape(2, 1, lanes)
    angle = jnp.arange(SIDE, dtype=F32)[None, :, None] * freq
    cosine, sine = jnp.cos(angle), jnp.sin(angle)

    def halves(x):
        return jnp.concatenate([x.astype(BF), (x - rounded(x)).astype(BF)], 0)

    zero = jnp.zeros((2 * SIDE, 2 * lanes), BF)
    rows = jnp.concatenate([halves(cosine[0]), halves(sine[0]), zero], 1)
    cols = jnp.concatenate([zero, halves(cosine[1]), halves(sine[1])], 1)
    return jnp.concatenate([rows, cols], 0)


def cos_sin(onehot, table, lanes):
    parts = dot(onehot, table)
    cr, sr = parts[:, :lanes], parts[:, lanes : 2 * lanes]
    cc, sc = parts[:, 2 * lanes : 3 * lanes], parts[:, 3 * lanes :]
    return cr * cc - sr * sc, sr * cc + cr * sc


def layer_norm_low(x, gain, shift):
    centred = x - jnp.mean(x, -1, keepdims=True)
    var = jnp.mean(centred * centred, -1, keepdims=True)
    return (centred * lax.rsqrt(var + EPS) * gain + shift).astype(BF)


def project(norm, cosine, sine, weights, b_ref, q_out, k_out, v_ref, exact):
    width = norm.shape[1]
    for n, out in enumerate((q_out, k_out)):
        for g in range(width // 256):
            lo = n * width + 256 * g
            proj = dot(norm, weights[:, lo : lo + 256]) + b_ref[:, lo : lo + 256]
            c, s = cosine[:, 128 * g : 128 * g + 128], sine[:, 128 * g : 128 * g + 128]
            for half, turned in enumerate(
                (proj[:, :128] * c - proj[:, 128:] * s, proj[:, :128] * s + proj[:, 128:] * c)
            ):
                at = slice(256 * g + 128 * half, 256 * g + 128 * half + 128)
                out[:, at] = turned.astype(BF)
                if exact:
                    exact[n][:, at] = turned
    for g in range(width // 256):
        lo = 2 * width + 256 * g
        v_ref[:, 256 * g : 256 * g + 256] = (
            dot(norm, weights[:, lo : lo + 256]) + b_ref[:, lo : lo + 256]
        ).astype(BF)


def qkv_own_kernel(
    x_ref, hot_ref, vec_ref, w_ref, b_ref, order_ref, table_ref,
    q_ref, k_ref, v_ref, pq_ref, pk_ref, w_turned,
):
    width = x_ref.shape[1]

    @pl.when(pl.program_id(0) == 0)
    def _():
        for g in range(2 * width // 256):
            at = slice(256 * g, 256 * g + 256)
            w_turned[:, at] = dot(w_ref[:, at], order_ref[...]).astype(BF)
        w_turned[:, 2 * width :] = w_ref[:, 2 * width :]

    norm = layer_norm_low(x_ref[...].astype(F32), vec_ref[LN1_GAIN], vec_ref[LN1_SHIFT])
    cosine, sine = cos_sin(hot_ref[...], table_ref[...], width // 2)
    project(norm, cosine, sine, w_turned, b_ref, q_ref, k_ref, v_ref, (pq_ref, pk_ref))


def qkv_own_call(x, onehot, vectors, weight, bias, order, table, first):
    own, width = x.shape
    rows = onehot.shape[0]
    tile = 256
    shape = jax.ShapeDtypeStruct((rows, width), BF)
    exact = jax.ShapeDtypeStruct((own, width), F32)
    row = lambda w: pl.BlockSpec((tile, w), lambda i: (i, 0))
    inside = lambda w: pl.BlockSpec(
        (pl.Element(tile), pl.Element(w)), lambda i: (pl.multiple_of(first + tile * i, BLK), 0)
    )
    return pl.pallas_call(
        qkv_own_kernel,
        grid=(own // tile,),
        in_specs=[
            row(width),
            inside(onehot.shape[1]),
            whole(vectors.shape),
            whole(weight.shape),
            whole((1, 3 * width)),
            whole(order.shape),
            whole(table.shape),
        ],
        out_specs=[inside(width)] * 3 + [row(width)] * 2 + [whole(weight.shape)],
        out_shape=[shape] * 3 + [exact] * 2 + [jax.ShapeDtypeStruct(weight.shape, BF)],
        compiler_params=params(),
        cost_estimate=cost(8),
        name="qkv_own",
    )(x, onehot, vectors, weight, bias[None], order, table)


def qkv_halo_kernel(
    far_l, near_l, near_r, far_r, hot_ref, vec_ref, w_ref, b_ref, table_ref,
    q_in, k_in, v_in, q_ref, k_ref, v_ref, x_all, sem,
):
    width = x_all.shape[1]
    step = pl.program_id(0)
    tile = q_ref.shape[0]

    @pl.when(step == 0)
    def _():
        own, reach = near_l.shape[0], far_l.shape[0]
        total = x_all.shape[0]
        blank = total // 2 - own - reach
        copies = []
        at = blank
        for n, ref in enumerate((far_l, near_l, near_r, far_r)):
            copies.append(
                pltpu.make_async_copy(ref, x_all.at[at : at + ref.shape[0], :], sem.at[n])
            )
            copies[-1].start()
            at += ref.shape[0]
        x_all[:blank, :] = jnp.zeros((blank, width), BF)
        x_all[total - blank :, :] = jnp.zeros((blank, width), BF)
        for copy in copies:
            copy.wait()

    x = x_all[pl.ds(pl.multiple_of(step * tile, tile), tile), :].astype(F32)
    norm = layer_norm_low(x, vec_ref[LN1_GAIN], vec_ref[LN1_SHIFT])
    cosine, sine = cos_sin(hot_ref[...], table_ref[...], width // 2)
    project(norm, cosine, sine, w_ref, b_ref, q_ref, k_ref, v_ref, ())


def qkv_halo_call(pieces, onehot, vectors, weight, bias, table, q, k, v, first):
    rows, width = q.shape
    own = pieces[1].shape[0]
    tile = first // 2
    shape = jax.ShapeDtypeStruct((rows, width), BF)
    at = lambda w: pl.BlockSpec(
        (pl.Element(tile), pl.Element(w)), lambda i: (pl.multiple_of(tile * i + jnp.where(i >= 2, own, 0), 64), 0)
    )
    return pl.pallas_call(
        qkv_halo_kernel,
        grid=(4,),
        in_specs=[ANY] * 4
        + [
            at(onehot.shape[1]),
            whole(vectors.shape),
            whole(weight.shape),
            whole((1, 3 * width)),
            whole(table.shape),
        ]
        + [ANY] * 3,
        out_specs=[at(width)] * 3,
        out_shape=[shape] * 3,
        input_output_aliases={9: 0, 10: 1, 11: 2},
        scratch_shapes=[pltpu.VMEM((2 * first, width), BF), pltpu.SemaphoreType.DMA((4,))],
        compiler_params=params(),
        cost_estimate=cost(11.5),
        name="qkv_halo",
    )(*pieces, onehot, vectors, weight, bias[None], table, q, k, v)


def head_stack(block, turned, scale=None):
    lane = lax.broadcasted_iota(jnp.int32, block.shape, 1)
    head = (lane % 128) // 32 if turned else lane // 64
    if scale is not None:
        block = block * scale
    zero = jnp.zeros_like(block)
    return jnp.concatenate([jnp.where(head == h, block, zero) for h in range(GROUP)], 0)


def fold8(x, op):
    return op(x.reshape(x.shape[0] // 8, 8, x.shape[1]), axis=0)


def forward_kernel(
    bound_ref, q_ref, k_ref, v_ref, bias_ref, o_ref, low_ref, lse_ref, s_ref
):
    blocks = q_ref.shape[0] // BLK
    lanes = GROUP * BLK

    def one_block(i, _):
        rows = pl.ds(pl.multiple_of(i * BLK, BLK), BLK)
        q4 = head_stack(q_ref[rows, :], True, jnp.asarray(0.125, BF))
        start, count = bound_ref[i, 0], bound_ref[i, 1]

        def scores(c, top):
            at = pl.ds(pl.multiple_of((start + 2 * c) * BLK, BLK), CHUNK)
            s = dot_nt(k_ref[at, :], q4)
            here = pl.ds(pl.multiple_of(c * CHUNK, CHUNK), CHUNK)
            tops = []
            for h in range(GROUP):
                lo = h * BLK
                masked = s[:, lo : lo + BLK] + bias_ref[at, rows_lane(i)]
                s_ref[here, lo : lo + BLK] = masked
                tops.append(fold8(masked, jnp.max))
            return jnp.maximum(top, jnp.concatenate(tops, 1))

        top = lax.fori_loop(0, count, scores, jnp.full((8, lanes), -3e38, F32))
        top = jnp.max(top, 0, keepdims=True)

        def mix(c, state):
            total, acc = state
            at = pl.ds(pl.multiple_of((start + 2 * c) * BLK, BLK), CHUNK)
            here = pl.ds(pl.multiple_of(c * CHUNK, CHUNK), CHUNK)
            e = jnp.exp(s_ref[here, :] - top)
            return total + fold8(e, jnp.sum), acc + dot_tn(v_ref[at, :], e.astype(BF))

        total, acc = lax.fori_loop(
            0, count, mix, (jnp.zeros((8, lanes), F32), jnp.zeros((256, lanes), F32))
        )
        total = jnp.sum(total, 0, keepdims=True)
        lse_ref[0, pl.ds(i, 1), :] = top + jnp.log(total)
        acc = acc / total
        out = jnp.concatenate(
            [acc[64 * h : 64 * h + 64, BLK * h : BLK * h + BLK] for h in range(GROUP)], 0
        )
        out = out.T
        o_ref[rows, :] = out
        low_ref[rows, :] = out.astype(BF)
        return 0

    def rows_lane(i):
        return pl.ds(pl.multiple_of(i * BLK, BLK), BLK)

    lax.fori_loop(0, blocks, one_block, 0)


def own_rows(own, first, base=0):
    return pl.BlockSpec((pl.Element(own), pl.Element(256)), lambda g: (first, 256 * (base + g)))


def forward_call(bounds, q_win, k_win, v_win, bias, first):
    win, width = k_win.shape
    own = bias.shape[1]
    groups = width // 256
    blocks = own // BLK
    tile = lambda n: pl.BlockSpec((n, 256), lambda g: (0, g))
    return pl.pallas_call(
        forward_kernel,
        grid=(groups,),
        in_specs=[SMEM, own_rows(own, first), tile(win), tile(win), whole(bias.shape)],
        out_specs=[tile(own), tile(own), pl.BlockSpec((1, blocks, GROUP * BLK), lambda g: (g, 0, 0))],
        out_shape=[
            jax.ShapeDtypeStruct((own, width), F32),
            jax.ShapeDtypeStruct((own, width), BF),
            jax.ShapeDtypeStruct((groups, blocks, GROUP * BLK), F32),
        ],
        scratch_shapes=[pltpu.VMEM((win, GROUP * BLK), F32)],
        compiler_params=params(),
        cost_estimate=cost(17.5),
        name="attention_forward",
    )(bounds, q_win, k_win, v_win, bias)


def backward_own_kernel(
    bound_ref, q_ref, do_ref, k_ref, v_ref, bias_ref, lse_ref, delta_ref,
    dq_ref, dk_ref, dv_ref, dk_acc, dv_acc, *, first,
):
    blocks = q_ref.shape[0] // BLK
    lanes = GROUP * BLK
    dk_acc[...] = jnp.zeros_like(dk_acc)
    dv_acc[...] = jnp.zeros_like(dv_acc)

    def one_block(i, _):
        rows = pl.ds(pl.multiple_of(i * BLK, BLK), BLK)
        q4 = head_stack(q_ref[rows, :], True, jnp.asarray(0.125, BF))
        do4 = head_stack(do_ref[rows, :], False)
        lse = lse_ref[0, pl.ds(i, 1), :]
        delta = delta_ref[0, pl.ds(i, 1), :]
        start, count = bound_ref[i, 0], bound_ref[i, 1]

        def step(c, acc):
            block = start + 2 * c
            at = pl.ds(pl.multiple_of(block * BLK, BLK), CHUNK)
            keys = k_ref[at, :]
            s = dot_nt(keys, q4)
            dp = dot_nt(v_ref[at, :], do4)
            bias = bias_ref[at, rows]
            low_p, low_ds = [], []
            for h in range(GROUP):
                lo = h * BLK
                p = jnp.exp(s[:, lo : lo + BLK] + bias - lse[:, lo : lo + BLK])
                low_p.append(p.astype(BF))
                low_ds.append((p * (dp[:, lo : lo + BLK] - delta[:, lo : lo + BLK])).astype(BF))
            low_p, low_ds = jnp.concatenate(low_p, 1), jnp.concatenate(low_ds, 1)

            @pl.when((block + 1 >= first) & (block < first + blocks))
            def _():
                dk_acc[at, :] += dot(low_ds, q4)
                dv_acc[at, :] += dot(low_p, do4)

            return acc + dot_tn(keys, low_ds)

        acc = lax.fori_loop(0, count, step, jnp.zeros((256, lanes), F32))
        parts = [acc[32 * h : 32 * h + 32, BLK * h : BLK * h + BLK] for h in range(GROUP)]
        parts += [acc[128 + 32 * h : 160 + 32 * h, BLK * h : BLK * h + BLK] for h in range(GROUP)]
        dq_ref[rows, :] = (jnp.concatenate(parts, 0) * 0.125).T
        return 0

    lax.fori_loop(0, blocks, one_block, 0)
    dk_ref[...] = dk_acc[first * BLK : (first + blocks) * BLK, :]
    dv_ref[...] = dv_acc[first * BLK : (first + blocks) * BLK, :]


def backward_own_call(bounds, q_win, do_own, k_win, v_win, bias, lse, delta, first, base, groups):
    own, width = bias.shape[1], 256 * groups
    win = k_win.shape[0]
    blocks = own // BLK
    tile = lambda n: pl.BlockSpec((n, 256), lambda g: (0, base + g))
    out = pl.BlockSpec((own, 256), lambda g: (0, g))
    stat = pl.BlockSpec((1, blocks, GROUP * BLK), lambda g: (base + g, 0, 0))
    return pl.pallas_call(
        functools.partial(backward_own_kernel, first=first // BLK),
        grid=(groups,),
        in_specs=[SMEM, own_rows(own, first, base), tile(own), tile(win), tile(win)]
        + [whole(bias.shape), stat, stat],
        out_specs=[out] * 3,
        out_shape=[jax.ShapeDtypeStruct((own, width), F32)] * 3,
        scratch_shapes=[pltpu.VMEM((win, 256), F32)] * 2,
        compiler_params=params(),
        cost_estimate=cost(9.5 * groups),
        name="attention_backward_own",
    )(bounds, q_win, do_own, k_win, v_win, bias, lse, delta)


def backward_halo_kernel(
    bound_ref, q_ref, far_l, near_l, near_r, far_r, k_ref, v_ref, bias_ref, *refs, first, splits
):
    d_in = refs[: 2 * splits]
    dk_ref, dv_ref, stat_ref = refs[2 * splits :]
    own, reach = k_ref.shape[0], far_l.shape[0] - STAT_PAD
    group = pl.program_id(0)
    base = 0
    for n in range(splits):
        size = (1, 2)[n]

        @pl.when((group >= base) & (group < base + size))
        def _():
            dk_ref[...] = d_in[n][...]
            dv_ref[...] = d_in[splits + n][...]

        base += size

    def stats(ref, row):
        parts = ref[row : row + 2 * STAT_ROWS, :].astype(F32)
        whole_row = parts[0:4] + parts[4:8] + parts[8:12]
        return [
            jnp.concatenate([whole_row[2 * n : 2 * n + 1], whole_row[2 * n + 1 : 2 * n + 2]], 1)
            for n in range(2)
        ]

    def one_block(j, block, ref, row, low, high):
        start, count = bound_ref[j, 0], bound_ref[j, 1]

        @pl.when(count > 0)
        def _():
            q4 = head_stack(q_ref[j * BLK : (j + 1) * BLK, :], True, jnp.asarray(0.125, BF))
            gone = jnp.zeros((BLK - (high - low), 256), BF)
            here = ref[row : row + high - low, :]
            if low:
                here = jnp.concatenate([gone, here], 0)
            elif high < BLK:
                here = jnp.concatenate([here, gone], 0)
            do4 = head_stack(here, False)
            size = ref.shape[0] - (STAT_PAD if high - low < BLK else own // BLK * 2 * STAT_ROWS)
            lse, delta = stats(ref, size + (block * 2 * STAT_ROWS))

            def step(c, _):
                at = pl.ds(pl.multiple_of((start + 2 * c) * BLK, BLK), CHUNK)
                s = dot_nt(k_ref[at, :], q4)
                dp = dot_nt(v_ref[at, :], do4)
                bias = bias_ref[at, j * BLK : (j + 1) * BLK]
                low_p, low_ds = [], []
                for h in range(GROUP):
                    lo = h * BLK
                    p = jnp.exp(s[:, lo : lo + BLK] + bias - lse[:, lo : lo + BLK])
                    low_p.append(p.astype(BF))
                    low_ds.append((p * (dp[:, lo : lo + BLK] - delta[:, lo : lo + BLK])).astype(BF))
                dk_ref[at, :] += dot(jnp.concatenate(low_ds, 1), q4)
                dv_ref[at, :] += dot(jnp.concatenate(low_p, 1), do4)
                return 0

            lax.fori_loop(0, count, step, 0)

    blocks = own // BLK
    one_block(0, 0, far_l, 0, BLK - reach, BLK)
    for i in range(blocks):
        one_block(1 + i, i, near_l, i * BLK, 0, BLK)
        one_block(first + blocks + i, i, near_r, i * BLK, 0, BLK)
    one_block(first + 2 * blocks, 0, far_r, 0, 0, reach)


def backward_halo_call(bounds, q_win, pieces, k_win, v_win, bias, dks, dvs, first):
    own = dks[0].shape[0]
    win, width = q_win.shape
    groups = width // 256
    tile = lambda n: pl.BlockSpec((n, 256), lambda g: (0, g))
    splits = len(dks)
    d_spec = [
        pl.BlockSpec((own, 256), lambda g: (0, 0)),
        pl.BlockSpec((own, 256), lambda g: (0, jnp.maximum(g - 1, 0))),
    ]
    return pl.pallas_call(
        functools.partial(backward_halo_kernel, first=first // BLK, splits=splits),
        grid=(groups,),
        in_specs=[SMEM, tile(win)]
        + [tile(p.shape[0]) for p in pieces]
        + [own_rows(own, first)] * 2
        + [whole(bias.shape)]
        + d_spec * 2,
        out_specs=[tile(own)] * 2,
        out_shape=[jax.ShapeDtypeStruct((own, width), F32)] * 2,
        scratch_shapes=[pltpu.VMEM((8, 128), F32)],
        compiler_params=params(),
        cost_estimate=cost(9),
        name="attention_backward_halo",
    )(bounds, q_win, *pieces, k_win, v_win, bias, *dks, *dvs)


def norm_parts(x):
    centred = x - jnp.mean(x, -1, keepdims=True)
    inverse = lax.rsqrt(jnp.mean(centred * centred, -1, keepdims=True) + EPS)
    return centred * inverse, inverse


def norm_back(grad, xhat, inverse, gain):
    scaled = grad * gain
    return inverse * (
        scaled
        - jnp.mean(scaled, -1, keepdims=True)
        - xhat * jnp.mean(scaled * xhat, -1, keepdims=True)
    )


def columns_sum(x):
    return jnp.sum(x, 0, keepdims=True)


def slices_out(place, source, keep, away, lead, sem, slices, rows):
    for n in range(slices):
        rel = place ^ n
        for target, odd in ((keep, 0), (away, 1)):

            @pl.when(rel % 2 == odd)
            def _():
                pltpu.make_async_copy(
                    source.at[n * rows : (n + 1) * rows, :],
                    target.at[rel // 2, pl.ds(lead, rows), :],
                    sem.at[n],
                ).start()


def slices_wait(source, keep, sem, slices, rows):
    for n in range(slices):
        pltpu.make_async_copy(
            source.at[n * rows : (n + 1) * rows, :], keep.at[0, 0:rows, :], sem.at[n]
        ).wait()


def one_quarter(q, w_all, norm_ref, dy_ref, bu_ref, dbu_ref, out_acc, dn_acc, g_all, fresh):
    own, width = norm_ref.shape
    tile = 256
    for t in range((w_all.shape[1] - width) // tile):
        cols = slice(tile * t, tile * t + tile)
        down = slice(width + tile * t, width + tile * t + tile)
        norm, dy = norm_ref[...], dy_ref[...]
        up_w = w_all[q, :width, cols]
        down_w = w_all[q, down, :]
        pre = dot(norm, up_w) + bu_ref[pl.ds(q, 1), cols]
        cdf = 0.5 * (1.0 + lax.erf(pre * np.float32(0.7071067811865476)))
        density = jnp.exp(-0.5 * pre * pre) * np.float32(0.3989422804014327)
        act = (pre * cdf).astype(BF)
        d_pre = (dot_nt(dy, down_w) * (cdf + pre * density)).astype(BF)
        dbu_ref[pl.ds(q, 1), cols] = columns_sum(d_pre.astype(F32))
        if fresh and t == 0:
            out_acc[...] = dot(act, down_w)
            dn_acc[...] = dot_nt(d_pre, up_w)
        else:
            out_acc[...] += dot(act, down_w)
            dn_acc[...] += dot_nt(d_pre, up_w)
        g_all[q, :width, cols] = dot_tn(norm, d_pre).astype(BF)
        g_all[q, down, :] = dot_tn(act, dy).astype(BF)


def middle_own_kernel(
    place_ref, x_ref, low_ref, wo_ref, vec_ref, dy_ref, bu_ref, up_ref, down_ref,
    hid_ref, norm_ref, out_ref, dn_ref, dbu_ref, keep_ref, send_ref, w_all, g_all, w_sem, g_sem,
    *, slices,
):
    width = x_ref.shape[1]
    rows = w_all.shape[1] // slices
    copies = [
        pltpu.make_async_copy(up_ref, w_all.at[0, :width, :], w_sem.at[0]),
        pltpu.make_async_copy(down_ref, w_all.at[0, width:, :], w_sem.at[1]),
    ]
    for copy in copies:
        copy.start()
    hidden_in = x_ref[...].astype(F32) + dot(low_ref[...], wo_ref[...]) + vec_ref[B_OUT]
    hid_ref[...] = hidden_in
    norm_ref[...] = layer_norm_low(hidden_in, vec_ref[LN2_GAIN], vec_ref[LN2_SHIFT])
    for copy in copies:
        copy.wait()
    one_quarter(0, w_all, norm_ref, dy_ref, bu_ref, dbu_ref, out_ref, dn_ref, g_all, True)
    slices_out(place_ref[0], g_all.at[0], keep_ref, send_ref, 0, g_sem, slices, rows)
    slices_wait(g_all.at[0], keep_ref, g_sem, slices, rows)


def middle_own_call(place, x, low, w_out, vectors, dy, b_up, w_up, w_down, slices):
    own, width = x.shape
    hidden = b_up.shape[1]
    rows = width + hidden
    vmem = pl.BlockSpec(memory_space=pltpu.VMEM)
    sds = jax.ShapeDtypeStruct
    return pl.pallas_call(
        functools.partial(middle_own_kernel, slices=slices),
        in_specs=[SMEM] + [vmem] * 6 + [ANY] * 2,
        out_specs=[vmem] * 5 + [ANY] * 2,
        out_shape=[
            sds((own, width), F32),
            sds((own, width), BF),
            sds((own, width), F32),
            sds((own, width), F32),
            sds((1, hidden), F32),
        ]
        + [sds((slices // 2, rows // slices, width), BF)] * 2,
        scratch_shapes=[
            pltpu.VMEM((1, rows, width), BF),
            pltpu.VMEM((1, rows, width), BF),
            pltpu.SemaphoreType.DMA((2,)),
            pltpu.SemaphoreType.DMA((slices,)),
        ],
        compiler_params=params(),
        cost_estimate=cost(12),
        name="middle_own",
    )(place, x, low, w_out, vectors, dy, b_up, w_up, w_down)


def middle_kernel(
    place_ref, hid_ref, norm_ref, out_in, dn_in, low_ref, mixed_ref, wo_ref, vec_ref, dy_ref,
    bu_ref, lse_ref, *refs, slices,
):
    piece_refs = refs[:10]
    (
        act_ref, dh_ref, dheads_ref, head_ref, tail_ref, delta_ref, small_ref, dbu_ref,
        keep_ref, send_ref, w_all, g_all, go_all, out_acc, dn_acc, w_sem, g_sem,
    ) = refs[10:]
    place = place_ref[0]
    own, width = norm_ref.shape
    quarters = w_all.shape[0]
    rows = w_all.shape[1] // slices
    part = rows // 2

    def fetches(q):
        copies = []
        for n in range(slices):
            for half in range(2):
                at = pl.multiple_of((place ^ n) * rows + half * part, part)
                copies.append(
                    pltpu.make_async_copy(
                        pieces_of(piece_refs, n, half).at[q],
                        w_all.at[q, pl.ds(at, part), :],
                        w_sem.at[q, 2 * n + half],
                    )
                )
        return copies

    for q in range(quarters):
        for copy in fetches(q):
            copy.start()
    out_acc[...] = out_in[...]
    dn_acc[...] = dn_in[...]

    def quarter(q, _):
        for copy in fetches(q):
            copy.wait()
        one_quarter(q, w_all, norm_ref, dy_ref, bu_ref, dbu_ref, out_acc, dn_acc, g_all, False)
        slices_out(
            place, g_all.at[q], keep_ref, send_ref, pl.multiple_of(q * rows, rows), g_sem.at[q],
            slices, rows,
        )
        return 0

    lax.fori_loop(0, quarters, quarter, 0)

    hidden_in = hid_ref[...]
    act_ref[...] = (hidden_in + out_acc[...] + vec_ref[B_DOWN]).astype(BF)
    xhat, inverse = norm_parts(hidden_in)
    dn = dn_acc[...]
    dy = dy_ref[...].astype(F32)
    d_hidden = dy + norm_back(dn, xhat, inverse, vec_ref[LN2_GAIN])
    dh_ref[...] = d_hidden
    d_att = d_hidden.astype(BF)
    small_ref[0:1, :] = columns_sum(dn * xhat)
    small_ref[1:2, :] = columns_sum(dn)
    small_ref[2:3, :] = columns_sum(dy)
    small_ref[3:4, :] = columns_sum(d_att.astype(F32))
    d_heads = dot_nt(d_att, wo_ref[...]).astype(BF)
    dheads_ref[:own, :] = d_heads
    spread = d_heads.astype(F32) * mixed_ref[...]
    pick = lax.broadcasted_iota(jnp.int32, (8, 256), 0)
    pick = (pick == lax.broadcasted_iota(jnp.int32, (8, 256), 1) // 64).astype(F32)
    for g in range(width // 256):
        for i in range(own // BLK):
            block = spread[BLK * i : BLK * i + BLK, 256 * g : 256 * g + 256]
            sums = lax.dot_general(
                pick, block, (((1,), (1,)), ((), ())),
                preferred_element_type=F32, precision=lax.Precision.HIGHEST,
            )
            delta = jnp.concatenate([sums[h : h + 1, :] for h in range(GROUP)], 1)
            delta_ref[g, i : i + 1, :] = delta
            lse = lse_ref[g, i : i + 1, :]
            left = jnp.concatenate(
                [lse[:, :256], lse[:, 256:], delta[:, :256], delta[:, 256:]], 0
            )
            parts = []
            for _ in range(3):
                parts.append(left.astype(BF))
                left = left - parts[-1].astype(F32)
            parts = jnp.concatenate(parts, 0)
            at = slice(256 * g, 256 * g + 256)
            lo = own + 2 * STAT_ROWS * i
            dheads_ref[lo : lo + 2 * STAT_ROWS, at] = parts
            for target, row in ((head_ref, 0), (tail_ref, own // BLK - 1)):
                if i == row:
                    target[REACH : REACH + 2 * STAT_ROWS, at] = parts
    blank = jnp.zeros((STAT_PAD - 2 * STAT_ROWS, width), BF)
    head_ref[REACH + 2 * STAT_ROWS :, :] = blank
    tail_ref[REACH + 2 * STAT_ROWS :, :] = blank
    head_ref[:REACH, :] = d_heads[:REACH, :]
    tail_ref[:REACH, :] = d_heads[own - REACH :, :]
    go_all[...] = dot_tn(low_ref[...], d_att).astype(BF)
    few = width // slices
    slices_out(place, go_all, keep_ref, send_ref, quarters * rows, g_sem.at[quarters], slices, few)
    for q in range(quarters):
        slices_wait(g_all.at[q], keep_ref, g_sem.at[q], slices, rows)
    slices_wait(go_all, keep_ref, g_sem.at[quarters], slices, few)


def middle_call(
    place, hidden_in, norm, out, dn, low, mixed, w_out, vectors, dy, b_up, lse, pieces, slices
):
    own, width = norm.shape
    quarters, hidden = b_up.shape
    rows = width + hidden
    vmem = pl.BlockSpec(memory_space=pltpu.VMEM)
    sds = jax.ShapeDtypeStruct
    grads = sds((slices // 2, (quarters * rows + width) // slices, width), BF)
    return pl.pallas_call(
        functools.partial(middle_kernel, slices=slices),
        in_specs=[SMEM] + [vmem] * 11 + [ANY] * len(pieces),
        out_specs=[vmem] * 8 + [ANY] * 2,
        out_shape=[
            sds((own, width), BF),
            sds((own, width), F32),
            sds((own + own // BLK * 2 * STAT_ROWS, width), BF),
            sds((REACH + STAT_PAD, width), BF),
            sds((REACH + STAT_PAD, width), BF),
            sds((width // 256, own // BLK, GROUP * BLK), F32),
            sds((4, width), F32),
            sds((quarters, hidden), F32),
            grads,
            grads,
        ],
        scratch_shapes=[
            pltpu.VMEM((quarters, rows, width), BF),
            pltpu.VMEM((quarters, rows, width), BF),
            pltpu.VMEM((width, width), BF),
            pltpu.VMEM((own, width), F32),
            pltpu.VMEM((own, width), F32),
            pltpu.SemaphoreType.DMA((quarters, 2 * slices)),
            pltpu.SemaphoreType.DMA((quarters + 1, slices)),
        ],
        compiler_params=params(),
        cost_estimate=cost(26),
        name="middle",
    )(place, hidden_in, norm, out, dn, low, mixed, w_out, vectors, dy, b_up, lse, *pieces)


def turn_back_kernel(
    place_ref, x_ref, vec_ref, dq0_ref, dq1_ref, dk_ref, dv_ref, q_ref, k_ref, hot_ref,
    table_ref, grid_ref, back_ref,
    d_ref, db_ref, freq_ref, keep_ref, send_ref, g_all, sem, *, slices,
):
    rows, width = dk_ref.shape
    norm = layer_norm_low(x_ref[...].astype(F32), vec_ref[LN1_GAIN], vec_ref[LN1_SHIFT])
    cosine, sine = cos_sin(hot_ref[...], table_ref[...], width // 2)

    def gradient(at, low):
        d_ref[:, at] = low
        db_ref[:, at] = columns_sum(low.astype(F32))
        g_all[:, at] = dot_tn(norm, low).astype(BF)

    for g in range(width // 256):
        c, s = cosine[:, 128 * g : 128 * g + 128], sine[:, 128 * g : 128 * g + 128]
        d_angle = jnp.zeros((rows, 128), F32)
        for n, (grad, turned_ref) in enumerate(((dq1_ref if g else dq0_ref, q_ref), (dk_ref, k_ref))):
            lo = 256 * (g - 1) if g and n == 0 else 256 * g
            g1, g2 = grad[:, lo : lo + 128], grad[:, lo + 128 : lo + 256]
            p1 = turned_ref[:, 256 * g : 256 * g + 128]
            p2 = turned_ref[:, 256 * g + 128 : 256 * g + 256]
            d_angle = d_angle + (g2 * p1 - g1 * p2)
            back = jnp.concatenate([g1 * c + g2 * s, g2 * c - g1 * s], 1).astype(BF)
            at = slice(n * width + 256 * g, n * width + 256 * g + 256)
            gradient(at, dot(back, back_ref[...]).astype(BF))
        freq_ref[:, 128 * g : 128 * g + 128] = lax.dot_general(
            grid_ref[...], d_angle, (((1,), (0,)), ((), ())),
            preferred_element_type=F32, precision=lax.Precision.HIGHEST,
        )
        at = slice(256 * g, 256 * g + 256)
        gradient(slice(2 * width + 256 * g, 2 * width + 256 * g + 256), dv_ref[:, at].astype(BF))
    slices_out(place_ref[0], g_all, keep_ref, send_ref, 0, sem, slices, width // slices)
    slices_wait(g_all, keep_ref, sem, slices, width // slices)


def turn_back_call(
    place, x, vectors, dqs, dk, dv, q_exact, k_exact, onehot, table, grid8, back, first, slices
):
    rows, width = dk.shape
    vmem = pl.BlockSpec(memory_space=pltpu.VMEM)
    sds = jax.ShapeDtypeStruct
    return pl.pallas_call(
        functools.partial(turn_back_kernel, slices=slices),
        in_specs=[SMEM] + [vmem] * 12,
        out_specs=[vmem] * 3 + [ANY] * 2,
        out_shape=[
            sds((rows, 3 * width), BF),
            sds((1, 3 * width), F32),
            sds((8, width // 2), F32),
        ]
        + [sds((slices // 2, width // slices, 3 * width), BF)] * 2,
        scratch_shapes=[
            pltpu.VMEM((width, 3 * width), BF),
            pltpu.SemaphoreType.DMA((slices,)),
        ],
        compiler_params=params(),
        cost_estimate=cost(11),
        name="turn_back",
    )(
        place, x, vectors, *dqs, dk, dv, q_exact, k_exact,
        onehot[first : first + rows], table, grid8, back,
    )


def input_grad_kernel(x_ref, vec_ref, d_ref, w_ref, dh_ref, out_ref, small_ref):
    d_norm = dot_nt(d_ref[...], w_ref[...])
    xhat, inverse = norm_parts(x_ref[...].astype(F32))
    small_ref[0:1, :] = columns_sum(d_norm * xhat)
    small_ref[1:2, :] = columns_sum(d_norm)
    out_ref[...] = dh_ref[...] + norm_back(d_norm, xhat, inverse, vec_ref[LN1_GAIN])


def input_grad_call(x, vectors, d_qkv, weight, d_hidden):
    rows, width = x.shape
    return pl.pallas_call(
        input_grad_kernel,
        out_shape=[
            jax.ShapeDtypeStruct((rows, width), F32),
            jax.ShapeDtypeStruct((2, width), F32),
        ],
        compiler_params=params(),
        cost_estimate=cost(7),
        name="input_grad",
    )(x, vectors, d_qkv, weight, d_hidden)


def assemble_kernel(place_ref, *refs, split, outs):
    piece_refs, out_refs = refs[:10], refs[10 : 10 + len(outs)]
    held, sem = refs[10 + len(outs) :]
    place, depth = place_ref[0], place_ref[1]
    pieces = held.shape[0]
    slot = pl.program_id(0)

    def copy(n, half, target):
        return pltpu.make_async_copy(
            pieces_of(piece_refs, n, half), held.at[target, half], sem.at[target, half]
        )

    @pl.when(slot == 0)
    def _():
        for n in range(pieces):
            for half in range(2):
                copy(n, half, place ^ n).start()

    for half in range(2):
        copy(0, half, slot).wait()
    rows = held.shape[-2]
    if split:
        for rel in range(split):
            block = held[slot, rel // (split // 2), rel % (split // 2)].astype(F32)
            at = ((depth - rel + split) % split) * rows
            lo = 0
            for ref in out_refs:
                ref[pl.ds(pl.multiple_of(at, 8), rows), :] = block[:, lo : lo + ref.shape[1]]
                lo += ref.shape[1]
    else:
        each = pieces // len(out_refs)
        for n, ref in enumerate(out_refs):

            @pl.when(slot // each == n)
            def _():
                for half in range(2):
                    ref[half * rows : half * rows + rows, :] = held[slot, half].astype(F32)


def assemble_call(place, arrays, shapes, split):
    pieces = 8
    rows = arrays[0].shape[-2] * max(split, 2)
    each = pieces if split else pieces // len(shapes)

    def spec(n, shape):
        lead = 0 if split else n * each
        return pl.BlockSpec((rows, shape[1]), lambda i: (jnp.clip(i - lead, 0, each - 1), 0))

    return pl.pallas_call(
        functools.partial(assemble_kernel, split=split, outs=shapes),
        grid=(pieces,),
        in_specs=[SMEM] + [ANY] * len(arrays),
        out_specs=[spec(n, shape) for n, shape in enumerate(shapes)],
        out_shape=[jax.ShapeDtypeStruct(s, F32) for s in shapes],
        scratch_shapes=[
            pltpu.VMEM((pieces,) + arrays[0].shape, BF),
            pltpu.SemaphoreType.DMA((pieces, 2)),
        ],
        compiler_params=params(),
        cost_estimate=cost(6),
        name="assemble",
    )(place, *arrays)


def send(x, axis, pairs):
    return lax.ppermute(x, axis, pairs)


def plane_gather(halves):
    over_b = send(halves, "b", SWAP)
    over_a = send(halves, "a", SWAP)
    near = [halves, over_b, over_a, send(over_b[0], "a", SWAP), send(over_a[1], "b", SWAP)]
    return near + [send(x, "c", SWAP) for x in near]


def pieces_of(refs, rel, half):
    refs = refs[5 * (rel % 2) : 5 * (rel % 2) + 5]
    return refs[3 + half] if rel // 2 == 3 else refs[rel // 2].at[half]


def wide_sum(x, extra):
    return lax.psum(x, "e") if extra > 1 else x


def sum_low(*terms):
    return functools.reduce(lambda x, y: x + y, [t.astype(F32) for t in terms])


def plane_scatter(kept, far, extra):
    chip = [sum_low(kept[n], far[n]).astype(BF) for n in range(4)]
    over_b = send(chip[1], "b", SWAP)
    over_a = send(chip[2], "a", SWAP)
    diagonal = send(chip[3], ("a", "b"), [(0, 3), (1, 2), (2, 1), (3, 0)])
    return chip, (chip[0], over_b, over_a, diagonal)


def split_scatter(kept, far):
    mid = kept.shape[1] // 2
    part = lambda n, half: sum_low(*(x[n, half * mid : half * mid + mid] for x in (kept, far)))
    over_b = jnp.stack([part(1, 0), part(3, 0)]).astype(BF)
    over_a = jnp.stack([part(2, 1), part(3, 1)]).astype(BF)
    rest = [part(0, 0), part(2, 0), part(0, 1), part(1, 1)]
    rest = [x.astype(BF) for x in rest]
    return (over_b, over_a, rest), (send(over_b, "b", SWAP), send(over_a, "a", SWAP))


def split_scatter_on(rest, got_b, got_a):
    on_a = sum_low(rest[1], got_b[1]).astype(BF)
    on_b = sum_low(rest[3], got_a[1]).astype(BF)
    return (on_a, on_b), (send(on_a, "a", SWAP), send(on_b, "b", SWAP))


def split_scatter_end(rest, got_b, got_a, got2_a, got2_b):
    return jnp.concatenate(
        [sum_low(rest[0], got_b[0], got2_a), sum_low(rest[2], got_a[0], got2_b)], 0
    )


def after(x, *others):
    return lax.optimization_barrier((x, others))[0]


def ring(size, step):
    return [(i, (i + step) % size) for i in range(size)]


def sum_all(vector, depth, extra):
    for axis in ("c", "b", "a"):
        vector = vector + send(vector, axis, SWAP)
    if extra > 1:
        vector = lax.psum(vector, "e")
    reach = 1
    while reach < depth:
        vector = vector + send(vector, "n", [(i, i ^ reach) for i in range(depth)])
        reach *= 2
    return vector


def on_device(
    tokens,
    segment,
    padding,
    coords,
    ln1_gain,
    ln1_shift,
    query_key_value_weight,
    b_qkv,
    output_weight,
    b_out,
    rope_freqs,
    ln2_gain,
    ln2_shift,
    w_up,
    b_up,
    w_down,
    b_down,
    cotangent,
    *,
    extra,
    depth,
):
    tokens, cotangent = tokens[0], cotangent[0]
    own, width = tokens.shape
    length = own * depth
    heads = rope_freqs.shape[1]
    half = width // heads // 2
    groups = heads // GROUP
    slices = 8
    outer = BLK
    side = own + outer
    win = own + 2 * side
    blocks = own // BLK
    z = lax.axis_index("n")
    plane = lax.axis_index("a") * 4 + lax.axis_index("b") * 2 + lax.axis_index("c")
    place = jnp.stack([plane, z]).astype(jnp.int32)
    up = [(i, i + 1) for i in range(depth - 1)]
    down = [(i + 1, i) for i in range(depth - 1)]
    up2 = [(i, i + 2) for i in range(depth - 2)]
    down2 = [(i + 2, i) for i in range(depth - 2)]

    def around(x, head, tail):
        before2 = send(tail, "n", up2)
        before = send(x, "n", up)
        after_ = send(x, "n", down)
        after2 = send(head, "n", down2)
        return [before2, before, after_, after2]

    position = jnp.arange(length, dtype=jnp.int32)
    ident = jnp.where(padding[0] == 0, segment[0], 1000 + position)
    ident = jnp.pad(ident, (side, side), constant_values=-1)
    ident_win = lax.dynamic_slice_in_dim(ident, z * own, win, 0)
    near = lax.broadcasted_iota(jnp.int32, (win,), 0)
    ident_win = jnp.where((near < outer - REACH) | (near >= win - outer + REACH), -1, ident_win)
    ident_own = lax.dynamic_slice_in_dim(ident, z * own + side, own, 0)
    seen = ident_win[:, None] == ident_own[None, :]
    bias_fwd = jnp.where(seen, 0.0, MASKED).astype(F32)
    bias_bwd = jnp.where(ident_own[:, None] == ident_win[None, :], 0.0, MASKED).astype(F32)
    touch = jnp.any(seen.reshape(win // BLK, BLK, blocks, BLK), (1, 3))

    def bounds(hit):
        size = hit.shape[1]
        lo = jnp.argmax(hit, 1).astype(jnp.int32)
        hi = size - jnp.argmax(hit[:, ::-1], 1).astype(jnp.int32)
        count = jnp.where(jnp.any(hit, 1), (hi - lo + 1) // 2, 0)
        return jnp.stack([jnp.minimum(lo, size - 2 * count), count], 1).astype(jnp.int32)

    bounds_fwd = bounds(touch.T)
    outside = (jnp.arange(win // BLK) < side // BLK) | (jnp.arange(win // BLK) >= side // BLK + blocks)
    bounds_bwd = bounds(touch) * outside[:, None].astype(jnp.int32)

    grid = jnp.pad(coords[:, 0], ((0, 0), (side, side)))
    grid_win = lax.dynamic_slice_in_dim(grid, z * own, win, 1)
    grid_own = lax.dynamic_slice_in_dim(grid, z * own + side, own, 1)
    lane = jnp.arange(4 * SIDE)
    picked = jnp.where(lane[None, :] < 2 * SIDE, grid_win[0][:, None], grid_win[1][:, None])
    onehot = (picked == (lane % SIDE)[None, :]).astype(BF)
    table = turn_table(rope_freqs)

    local = np.arange(256)
    order = np.zeros((256, 256), np.float32)
    order[(local % 128) // 32 * 64 + local // 128 * 32 + local % 32, local] = 1.0
    order = jnp.asarray(order, BF)
    qk_bias = b_qkv[: 2 * width].reshape(2 * groups, GROUP, 2, half).swapaxes(1, 2)
    bias_turned = jnp.concatenate([qk_bias.reshape(-1), b_qkv[2 * width :]])

    x_parts = around(tokens, tokens[:REACH], tokens[own - REACH :])
    vectors = jnp.stack([ln1_gain, ln1_shift, b_out, ln2_gain, ln2_shift, b_down])
    rot_q, rot_k, values, q_exact, k_exact, weight_turned = qkv_own_call(
        tokens, onehot, vectors, query_key_value_weight, bias_turned, order, table, side
    )

    rows = (width + w_down.shape[0]) // slices
    eighth = jnp.where(
        plane < width // rows,
        lax.dynamic_slice_in_dim(w_up, jnp.minimum(plane * rows, width - rows), rows, 0),
        lax.dynamic_slice_in_dim(w_down, jnp.maximum(plane * rows - width, 0), rows, 0),
    )
    left, bias_rows = b_up, []
    for _ in range(3):
        bias_rows.append(left.astype(BF))
        left = left - rounded(left)
    bias_rows = jnp.pad(jnp.stack(bias_rows), ((0, 13), (0, 0)))
    eighth = jnp.concatenate([eighth, bias_rows], 0)
    others = [send(eighth, "n", ring(depth, k)) for k in range(1, depth)]
    ready = (bias_fwd, bias_bwd, bounds_fwd, bounds_bwd, rot_q)
    x_parts, ready = lax.optimization_barrier((x_parts, ready))
    bias_fwd, bias_bwd, bounds_fwd, bounds_bwd, rot_q = ready
    rot_q, rot_k, values = qkv_halo_call(
        x_parts, onehot, vectors, weight_turned, bias_turned, table, rot_q, rot_k, values, side
    )
    others, rot_q = lax.optimization_barrier((others, rot_q))
    up_biases = jnp.concatenate(
        [jnp.sum(x[rows : rows + 3].astype(F32), 0, keepdims=True) for x in others]
    )
    part = rows // 2
    own_w = jnp.stack([x[half * part : half * part + part] for half in range(2) for x in others])
    own_w = own_w.reshape(2, depth - 1, part, width)
    over_b = send(own_w, "b", SWAP)
    over_a = send(own_w, "a", SWAP)
    mixed, mixed_low, lse = forward_call(bounds_fwd, rot_q, rot_k, values, bias_fwd, side)
    over_b, over_a, mixed_low = lax.optimization_barrier((over_b, over_a, mixed_low))
    diagonal = (send(over_b[0], "a", SWAP), send(over_a[1], "b", SWAP))
    hidden_in, norm2, out0, dn0, up_sum0, kept_own, sent_own = middle_own_call(
        place, tokens, mixed_low, output_weight, vectors, cotangent, b_up[None], w_up, w_down,
        slices,
    )
    far_own = send(sent_own, "c", SWAP)
    diagonal, norm2 = lax.optimization_barrier((diagonal, norm2))
    near = [own_w, over_b, over_a, *diagonal]
    pieces = near + [send(x, "c", SWAP) for x in near]
    chip_own, parts_own = plane_scatter(kept_own, far_own, extra)
    norm2 = after(norm2, chip_own)
    (
        activations, d_hidden, d_heads, d_head, d_tail, delta, small_mid, up_sums, kept_mid,
        sent_mid,
    ) = middle_call(
        place, hidden_in, norm2, out0, dn0, mixed_low, mixed, output_weight, vectors, cotangent,
        up_biases, lse, pieces, slices,
    )
    far_mid = send(sent_mid, "c", SWAP)
    do_parts = around(d_heads, d_head, d_tail)

    own_args = (bounds_fwd, rot_q, d_heads, rot_k, values, bias_fwd, lse, delta, side)
    dq0, dk0, dv0 = backward_own_call(*own_args, 0, 1)
    far_mid, dq0 = lax.optimization_barrier((far_mid, dq0))
    (sent_b, sent_a, rest), round_1 = split_scatter(kept_mid, far_mid)
    own_args = own_args[:-2] + (after(delta, dq0, sent_b, sent_a, rest), side)
    dq1, dk1, dv1 = backward_own_call(*own_args, 1, groups - 1)
    do_parts, dq1 = lax.optimization_barrier((do_parts, dq1))
    dk, dv = backward_halo_call(
        bounds_bwd, rot_q, do_parts, rot_k, values, bias_bwd, [dk0, dk1], [dv0, dv1], side
    )
    round_1, dk = lax.optimization_barrier((round_1, dk))
    crossing, round_2 = split_scatter_on(rest, *round_1)
    dk = after(dk, crossing)

    grid8 = jnp.pad(grid_own.astype(F32), ((0, 6), (0, 0)))
    d_qkv, grad_b_qkv, freqs8, kept_qkv, sent_qkv = turn_back_call(
        place, tokens, vectors, (dq0, dq1), dk, dv, q_exact, k_exact, onehot, table, grid8,
        order.T, side, slices,
    )
    far_qkv = send(sent_qkv, "c", SWAP)
    round_2, d_qkv = lax.optimization_barrier((round_2, d_qkv))
    plane_mid = wide_sum(split_scatter_end(rest, *round_1, *round_2), extra)
    ff_sent = [plane_mid[k * rows - rows : k * rows].astype(BF) for k in range(1, depth)]
    ff_got = [send(ff_sent[k - 1], "n", ring(depth, -k)) for k in range(1, depth)]
    input_grad, small_in = input_grad_call(
        tokens, vectors, after(d_qkv, ff_sent), query_key_value_weight, d_hidden
    )
    far_qkv, small_in = lax.optimization_barrier((far_qkv, small_in))
    (_, _, rest_qkv), round_1 = split_scatter(kept_qkv, far_qkv)
    _, round_2 = split_scatter_on(rest_qkv, *round_1)
    plane_qkv = wide_sum(split_scatter_end(rest_qkv, *round_1, *round_2), extra)

    ff_total = wide_sum(sum_low(*parts_own), extra) + sum_low(*ff_got)
    ff_square = jnp.sum(ff_total * ff_total)
    gathered = plane_gather(ff_total.astype(BF).reshape(2, rows // 2, width))
    total_w_up, total_w_down = assemble_call(place, gathered, [w_up.shape, w_down.shape], 0)

    part = jnp.concatenate([plane_qkv, plane_mid[(depth - 1) * rows :]], 1).astype(BF)
    thin = part.shape[0] // depth
    cut = lambda k: lax.dynamic_slice_in_dim(part, ((z + k) % depth) * thin, thin, 0)
    total = cut(0).astype(F32)
    for k in range(1, depth):
        total = total + send(cut(k), "n", ring(depth, k)).astype(F32)
    proj_square = jnp.sum(total * total)
    low = total.astype(BF)
    strip = jnp.stack([low] + [send(low, "n", ring(depth, k)) for k in range(1, depth)])
    gathered = plane_gather(strip.reshape((2, depth // 2) + low.shape))
    total_w_qkv, total_w_out = assemble_call(
        place, gathered, [query_key_value_weight.shape, output_weight.shape], depth
    )

    slot = (z - jnp.arange(depth)) % depth
    quarter_sums = jnp.take(jnp.concatenate([up_sum0, up_sums]), slot, axis=0)
    named = [
        small_in[0], small_in[1], grad_b_qkv[0], small_mid[3], freqs8[:2].reshape(-1),
        small_mid[0], small_mid[1], small_mid[2], quarter_sums.reshape(-1),
    ]
    large = jnp.full((128,), ff_square + proj_square)
    if extra > 1:
        large = large / extra
    small = jnp.concatenate(named + [large])
    small = sum_all(small.reshape(-1, 128), depth, extra).reshape(-1)
    out, at = [], 0
    for vector in named:
        out.append(small[at : at + vector.size])
        at += vector.size
    t_gain1, t_shift1, t_b_qkv, t_b_out, t_freqs, t_gain2, t_shift2, t_b_down, t_up = out
    t_freqs = t_freqs.reshape(rope_freqs.shape)
    rot_sq = jnp.sum(t_freqs * t_freqs)
    skip = sum(v.size for v in named[:4])
    lane = jnp.arange(small.size)
    others = (lane < skip) | (lane >= skip + freqs8.shape[1] * 2) & (lane < at)
    other_sq = small[at] + jnp.sum(jnp.where(others, small * small, 0.0))
    t_b_up = lax.dynamic_slice_in_dim(t_up, z * b_up.shape[0], b_up.shape[0], 0)
    return (
        activations[None],
        input_grad[None],
        t_gain1,
        t_shift1,
        total_w_qkv,
        t_b_qkv,
        total_w_out,
        t_b_out,
        t_freqs,
        t_gain2,
        t_shift2,
        total_w_up,
        t_b_up,
        total_w_down,
        t_b_down,
        rot_sq,
        other_sq,
    )


def solution(mesh):
    wide, depth = mesh.shape["wide"], mesh.shape["narrow"]
    extra = wide // 8
    fine = Mesh(mesh.devices.reshape(extra, 2, 2, 2, depth), ("e", "a", "b", "c", "n"))
    w, n = ("e", "a", "b", "c"), "n"
    return jax.shard_map(
        functools.partial(on_device, extra=extra, depth=depth),
        mesh=fine,
        in_specs=(
            P(w, n, None), P(w, None), P(w, None), P(None, w, None),
            P(), P(), P(), P(), P(), P(), P(), P(), P(),
            P(None, n), P(n), P(n, None), P(), P(w, n, None),
        ),
        out_specs=(
            P(w, n, None), P(w, n, None),
            P(), P(), P(), P(), P(), P(), P(), P(), P(),
            P(None, n), P(n), P(n, None), P(), P(), P(),
        ),
        check_vma=False,
    )
```

time: 1860 us -> 411 us (0.22); the launches traced: 1840 us -> 407 us
  matrix products: 746 us -> 0 us
  other arithmetic: 401 us -> 32.1 us
  waiting for transfers between devices: 373 us -> 90.9 us
  local copies, waits for them, and re-layouts: 243 us -> 16.5 us
  Pallas kernels: 0 us -> 165 us
  starting transfers between devices: 0.61 us -> 96.8 us
  blocking collectives: 35.2 us -> 0 us
    dot_general x40 -> x0, matrix products: 746 us -> none  [the longest x8 178 us: masked_scores(): jnp.einsum('sqhd,skhd->shqk', q_block, rot_k_low, preferred_element_type=...]
    psum x2 -> x0, waiting for transfers between devices: 311 us -> none  [the longest x1 201 us: on_device(): d_norm2 = lax.psum(d_norm2_part, 'narrow')]
    pallas_call x0 -> x12, Pallas kernels: none -> 165 us  [the longest x2 40.2 us: backward_own_call(): pl.pallas_call(functools.partial(backward_own_kernel, first=first // BLK)...]
    convert_element_type x6 -> x12, other arithmetic: 170 us -> 10.1 us  [the longest x1 3.06 us: split_scatter(): rest = [x.astype(BF) for x in rest]]
    reduce_sum x23 -> x6, other arithmetic: 158 us -> 2.62 us  [the longest x1 1.21 us: on_device(): rot_sq = jnp.sum(t_freqs * t_freqs)]
    dynamic_update_slice x8 -> x0, local copies, waits for them, and re-layouts: 135 us -> none  [on_device(): lax.scan(forward_block, None, jnp.arange(block_count))]
    ppermute x0 -> x66, starting transfers between devices: none -> 96.8 us  [send(): return lax.ppermute(x, axis, pairs)]
    ppermute x0 -> x66, waiting for transfers between devices: none -> 90.9 us  [send(): return lax.ppermute(x, axis, pairs)]
  transfers between devices with their start and end apart: 5 -> 66, of which waited for: 3 -> 21; matrix products, arithmetic and copies ran while one was open for 72% -> 11% of each run, Pallas kernels for 0% -> 29%
where the time goes in v1:
time: 411 us; the launch traced here: 407 us
  Pallas kernels  165 us (40%)
  starting transfers between devices  96.8 us (24%)
  waiting for transfers between devices  90.9 us (22%)
  other arithmetic  32.1 us (8%)
  local copies, waits for them, and re-layouts  16.5 us (4%)
  between operations  5.93 us (1%)
    ppermute x66, starting transfers between devices, send(): return lax.ppermute(x, axis, pairs)  96.8 us
    ppermute x66, waiting for transfers between devices, send(): return lax.ppermute(x, axis, pairs)  90.9 us
    pallas_call x2, Pallas kernels, backward_own_call(): pl.pallas_call(functools.partial(backward_own_kernel, first=first // BLK)...  40.2 us
    pallas_call x1, Pallas kernels, forward_call(): pl.pallas_call(forward_kernel, grid=(groups,), in_specs=[SMEM, own_rows(o...  26.1 us
    pallas_call x1, Pallas kernels, middle_call(): pl.pallas_call(functools.partial(middle_kernel, slices=slices), in_specs=...  25.6 us
    pallas_call x2, Pallas kernels, assemble_call(): pl.pallas_call(functools.partial(assemble_kernel, split=split, outs=shape...  12.8 us
    pallas_call x1, Pallas kernels, middle_own_call(): pl.pallas_call(functools.partial(middle_own_kernel, slices=slices), in_sp...  12.5 us
    pallas_call x1, Pallas kernels, qkv_halo_call(): pl.pallas_call(qkv_halo_kernel, grid=(4,), in_specs=[ANY] * 4 + [at(oneho...  11.4 us
  transfers between devices with their start and end apart: 66, of which 21 were waited for; matrix products, arithmetic and copies ran while one was open for 11% of the time, Pallas kernels for 29%

profile of v1, /device:TPU:1, one launch (start us, length us, event | category | flops | bytes accessed | tf_op | source)
XLA Modules:
  0.0 406.8 jit_solution(815234100340254764)
XLA Ops:
  2.2 4.7 %collective-permute-start.4 = (bf16[512,768]{1,0:T(8,128)(2,1)}, bf16[512,768]{1,0:T(8,128)(2,1)S(1)}, u32[]{:S(2)}, u32[]{:S(2)}) collective-permute-start(bf16[512,768]{1,0:T(8,128)(2,1)} %bitcast.163), channel_id=1, source_target_pairs={{0,1},{1,2},{2,3},{4,5},{5,6},{6,7},{8,9},{9,10},{10,11},{12,13},{... | collective-permute-start | bytes 2359304 | tf_op jit(solution)/shard_map/ppermute | solution.py:890
  9.2 4.9 %collective-permute-start.3 = (bf16[64,768]{1,0:T(8,128)(2,1)S(1)}, bf16[64,768]{1,0:T(8,128)(2,1)S(1)}, u32[]{:S(2)}, u32[]{:S(2)}) collective-permute-start(bf16[64,768]{1,0:T(8,128)(2,1)S(1)} %get-tuple-element.307), channel_id=1, source_target_pairs={{0,2},{1,3},{4,6},{5,7},{8,10},{9,11},{12,14},{13,15},{16,18},{17,... | collective-permute-start | bytes 294920 | tf_op jit(solution)/shard_map/ppermute | solution.py:890
  17.2 2.3 compare_reduce_fusion
  24.7 2.2 compare_select_fusion.bias_ref
  26.9 1.7 fusion.6.hot_ref
  30.0 8.3 %qkv_own.1 = (bf16[1792,768]{1,0:T(8,128)(2,1)}, bf16[1792,768]{1,0:T(8,128)(2,1)}, bf16[1792,768]{1,0:T(8,128)(2,1)}, f32[512,768]{1,0:T(8,128)}, f32[512,768]{1,0:T(8,128)}, /*index=5*/bf16[768,2304]{1,0:T(8,128)(2,1)}) custom-call(bf16[512,768]{1,0:T(8,128)(2,1)} %bitcast.164, bf16[1792,128]{1,0:T(8,128)(2,1)} %fusion.6.hot_ref, ...), custom_call_target="tpu_custom_call" | custom-call | flops 9200000000 | bytes 24000000 | tf_op jit(solution)/shard_map/qkv_own/pallas_call | solution.py:139
  39.7 2.1 compare_select_fusion.1.bias_ref
  42.4 2.1 collective-permute-start.1
  45.9 11.4 %qkv_halo.1 = (bf16[1792,768]{1,0:T(8,128)(2,1)}, bf16[1792,768]{1,0:T(8,128)(2,1)}, bf16[1792,768]{1,0:T(8,128)(2,1)}) custom-call(bf16[64,768]{1,0:T(8,128)(2,1)} %copy-done.50, bf16[512,768]{1,0:T(8,128)(2,1)} %copy-done.32, bf16[512,768]{1,0:T(8,128)(2,1)} %copy-done.31, ...), custom_call_target="tpu_custom_call", output_to_operand_aliasing={{0}: (9, {}), {1}: (10, {}), {2}: (11, {})} | custom-call | flops 13224999936 | bytes 34500000 | tf_op jit(solution)/shard_map/qkv_halo/pallas_call | solution.py:199
  57.3 8.4 %collective-permute-done.1 = bf16[208,768]{1,0:T(8,128)(2,1)S(1)} collective-permute-done((bf16[208,768]{1,0:T(8,128)(2,1)S(1)}, bf16[208,768]{1,0:T(8,128)(2,1)S(1)}, u32[]{:S(2)}, u32[]{:S(2)}) %collective-permute-start.1) | collective-permute-done | bytes 319520 | tf_op jit(solution)/shard_map/ppermute | solution.py:890
  68.2 26.1 %attention_forward.1 = (f32[512,768]{1,0:T(8,128)}, bf16[512,768]{1,0:T(8,128)(2,1)}, f32[3,4,512]{2,1,0:T(4,128)}) custom-call(s32[4,2]{1,0:T(4,128)} %pad_add_fusion.bound_ref, bf16[1792,768]{1,0:T(8,128)(2,1)} %get-tuple-element.125.q_ref, bf16[1792,768]{1,0:T(8,128)(2,1)} %get-tuple-element.126.k_ref, bf16[1792,768]{1,0:T(8,128)(2,1)} %get-tuple-element.127.v_ref, ...), custom_call_target="tpu_custom_call" | custom-call | flops 20124999680 | bytes 52500000 | tf_op jit(solution)/shard_map/attention_forward/pallas_call | solution.py:297
  94.3 12.5 %middle_own.1 = (f32[512,768]{1,0:T(8,128)}, bf16[512,768]{1,0:T(8,128)(2,1)}, f32[512,768]{1,0:T(8,128)}, f32[512,768]{1,0:T(8,128)}, f32[1,768]{1,0:T(1,128)},...) custom-call(s32[2]{0:T(128)} %pad_add_fusion.2.place_ref, bf16[512,768]{1,0:T(8,128)(2,1)} %bitcast.165, ...), custom_call_target="tpu_custom_call" | custom-call | flops 13799999488 | bytes 36000000 | tf_op jit(solution)/shard_map/middle_own/pallas_call | solution.py:573
  107.0 2.3 collective-permute-start.10
  110.0 9.8 %collective-permute-done.10.refs_4_ = bf16[3,96,768]{2,1,0:T(8,128)(2,1)S(1)} collective-permute-done((bf16[3,96,768]{2,1,0:T(8,128)(2,1)S(1)}, bf16[3,96,768]{2,1,0:T(8,128)(2,1)S(1)}, u32[]{:S(2)}, u32[]{:S(2)}) %collective-permute-start.10) | collective-permute-done | bytes 442400 | tf_op jit(solution)/shard_map/ppermute | solution.py:890
  125.5 25.6 %middle.1 = (bf16[512,768]{1,0:T(8,128)(2,1)}, f32[512,768]{1,0:T(8,128)}, bf16[560,768]{1,0:T(8,128)(2,1)}, bf16[80,768]{1,0:T(8,128)(2,1)}, bf16[80,768]{1,0:T...) custom-call(s32[2]{0:T(128)} %pad_add_fusion.2.place_ref, ...), custom_call_target="tpu_custom_call" | custom-call | flops 29899999232 | bytes 78000000 | tf_op jit(solution)/shard_map/middle/pallas_call | solution.py:707
  155.2 4.9 %collective-permute-start.21 = (bf16[560,768]{1,0:T(8,128)(2,1)}, bf16[560,768]{1,0:T(8,128)(2,1)}, u32[]{:S(2)}, u32[]{:S(2)}) collective-permute-start(bf16[560,768]{1,0:T(8,128)(2,1)} %get-tuple-element.148.do_ref), channel_id=1, source_target_pairs={{0,1},{1,2},{2,3},{4,5},{5,6},{6,7},{8,9},{9,10},{10,11},{12,13},{... | collective-permute-start | bytes 2580488 | tf_op jit(solution)/shard_map/ppermute | solution.py:890
  161.5 3.8 collective-permute-start.20
  167.5 15.0 %attention_backward_own.2 = (f32[512,256]{1,0:T(8,128)}, f32[512,256]{1,0:T(8,128)}, f32[512,256]{1,0:T(8,128)}) custom-call(s32[4,2]{1,0:T(4,128)} %pad_add_fusion.bound_ref, bf16[1792,768]{1,0:T(8,128)(2,1)} %get-tuple-element.125.q_ref, bf16[560,768]{1,0:T(8,128)(2,1)} %get-tuple-element.148.do_ref, bf16[1792,768]{1,0:T(8,128)(2,1)} %get-tuple-element.126.k_ref, ...), custom_call_target="tpu_custom_call" | custom-call | flops 10924999680 | bytes 28500000 | tf_op jit(solution)/shard_map/attention_backward_own/pallas_call | solution.py:371
  182.5 3.1 fusion.10
  185.9 1.9 collective-permute-start.19
  187.8 25.2 %attention_backward_own.3 = (f32[512,512]{1,0:T(8,128)}, f32[512,512]{1,0:T(8,128)}, f32[512,512]{1,0:T(8,128)}) custom-call(s32[4,2]{1,0:T(4,128)} %pad_add_fusion.bound_ref, bf16[1792,768]{1,0:T(8,128)(2,1)} %get-tuple-element.125.q_ref, bf16[560,768]{1,0:T(8,128)(2,1)} %get-tuple-element.148.do_ref, bf16[1792,768]{1,0:T(8,128)(2,1)} %get-tuple-element.126.k_ref, ...), custom_call_target="tpu_custom_call" | custom-call | flops 21849999360 | bytes 57000000 | tf_op jit(solution)/shard_map/attention_backward_own/pallas_call | solution.py:371
  213.9 1.9 collective-permute-start.27
  215.8 9.6 %attention_backward_halo.1 = (f32[512,768]{1,0:T(8,128)}, f32[512,768]{1,0:T(8,128)}) custom-call(s32[14,2]{1,0:T(8,128)} %broadcast_multiply_fusion.bound_ref, bf16[1792,768]{1,0:T(8,128)(2,1)} %get-tuple-element.125.q_ref, bf16[80,768]{1,0:T(8,128)(2,1)} %copy-done.47, bf16[560,768]{1,0:T(8,128)(2,1)} %collective-permute-done.21.near_l, ...), custom_call_target="tpu_custom_call" | custom-call | flops 10350000128 | bytes 27000000 | tf_op jit(solution)/shard_map/attention_backward_halo/pallas_call | solution.py:462
  228.0 10.9 %turn_back.1 = (bf16[512,2304]{1,0:T(8,128)(2,1)}, f32[1,2304]{1,0:T(1,128)}, f32[8,384]{1,0:T(8,128)}, bf16[4,96,2304]{2,1,0:T(8,128)(2,1)}, bf16[4,96,2304]{2,1,0:T(8,128)(2,1)}) custom-call(s32[2]{0:T(128)} %pad_add_fusion.2.place_ref, bf16[512,768]{1,0:T(8,128)(2,1)} %bitcast.166, f32[6,768]{1,0:T(8,128)} %stack.139.vec_ref, ...), custom_call_target="tpu_custom_call" | custom-call | flops 12650000384 | bytes 33000000 | tf_op jit(solution)/shard_map/turn_back/pallas_call | solution.py:780
  240.3 1.9 collective-permute-start.26
  245.1 15.6 %collective-permute-start.32 = (bf16[192,768]{1,0:T(8,128)(2,1)S(1)}, bf16[192,768]{1,0:T(8,128)(2,1)S(1)}, u32[]{:S(2)}, u32[]{:S(2)}) collective-permute-start(bf16[192,768]{1,0:T(8,128)(2,1)S(1)} %get-tuple-element.311), channel_id=1, source_target_pairs={{0,1},{1,2},{2,3},{3,0},{4,5},{5,6},{6,7},{7,4},{8,9},{9,10},{10,1... | collective-permute-start | bytes 884744 | tf_op jit(solution)/shard_map/ppermute | solution.py:890
  262.4 2.3 collective-permute-start.30
  264.6 7.1 %input_grad.1 = (f32[512,768]{1,0:T(8,128)}, f32[2,768]{1,0:T(2,128)}) custom-call(bf16[512,768]{1,0:T(8,128)(2,1)} %bitcast.167, f32[6,768]{1,0:T(8,128)} %stack.139.vec_ref, bf16[512,2304]{1,0:T(8,128)(2,1)} %get-tuple-element.180.d_ref, bf16[768,2304]{1,0:T(8,128)(2,1)} %w_ref.3, f32[512,768]{1,0:T(8,128)} %get-tuple-element.181.dh_ref), custom_call_target="tpu_custom_call" | custom-call | flops 8049999872 | bytes 21000000 | tf_op jit(solution)/shard_map/input_grad/pallas_call | solution.py:813
  271.8 4.5 %collective-permute-done.31 = bf16[192,768]{1,0:T(8,128)(2,1)S(1)} collective-permute-done((bf16[192,768]{1,0:T(8,128)(2,1)S(1)}, bf16[192,768]{1,0:T(8,128)(2,1)S(1)}, u32[]{:S(2)}, u32[]{:S(2)}) %collective-permute-start.31) | collective-permute-done | bytes 294944 | tf_op jit(solution)/shard_map/ppermute | solution.py:890
  276.3 3.6 collective-permute-done.30
  281.3 1.8 collective-permute-start.58
  284.4 14.7 %collective-permute-done.35 = bf16[2,48,2304]{2,1,0:T(8,128)(2,1)S(1)} collective-permute-done((bf16[2,48,2304]{2,1,0:T(8,128)(2,1)S(1)}, bf16[2,48,2304]{2,1,0:T(8,128)(2,1)S(1)}, u32[]{:S(2)}, u32[]{:S(2)}) %collective-permute-start.35) | collective-permute-done | bytes 442400 | tf_op jit(solution)/shard_map/ppermute | solution.py:890
  300.5 4.4 %collective-permute-done.34 = bf16[48,2304]{1,0:T(8,128)(2,1)S(1)} collective-permute-done((bf16[48,2304]{1,0:T(8,128)(2,1)S(1)}, bf16[48,2304]{1,0:T(8,128)(2,1)S(1)}, u32[]{:S(2)}, u32[]{:S(2)}) %collective-permute-start.34) | collective-permute-done | bytes 221216 | tf_op jit(solution)/shard_map/ppermute | solution.py:890
  306.0 6.6 %collective-permute-start.37 = (bf16[24,3072]{1,0:T(8,128)(2,1)S(1)}, bf16[24,3072]{1,0:T(8,128)(2,1)S(1)}, u32[]{:S(2)}, u32[]{:S(2)}) collective-permute-start(bf16[24,3072]{1,0:T(8,128)(2,1)S(1)} %get-tuple-element.308), channel_id=1, source_target_pairs={{0,1},{1,2},{2,3},{3,0},{4,5},{5,6},{6,7},{7,4},{8,9},{9,10},{10,1... | collective-permute-start | bytes 442376 | tf_op jit(solution)/shard_map/ppermute | solution.py:890
  312.6 2.9 collective-permute-start.39
  315.7 2.4 collective-permute-done.37
  318.8 8.4 %collective-permute-done.38 = bf16[24,3072]{1,0:T(8,128)(2,1)S(1)} collective-permute-done((bf16[24,3072]{1,0:T(8,128)(2,1)S(1)}, bf16[24,3072]{1,0:T(8,128)(2,1)S(1)}, u32[]{:S(2)}, u32[]{:S(2)}) %collective-permute-start.38) | collective-permute-done | bytes 147488 | tf_op jit(solution)/shard_map/ppermute | solution.py:890
  329.2 2.5 collective-permute-start.40
  334.2 7.1 %collective-permute-done.41 = f32[85,128]{1,0:T(8,128)S(1)} collective-permute-done((f32[85,128]{1,0:T(8,128)S(1)}, f32[85,128]{1,0:T(8,128)S(1)}, u32[]{:S(2)}, u32[]{:S(2)}) %collective-permute-start.41) | collective-permute-done | bytes 43552 | tf_op jit(solution)/shard_map/ppermute | solution.py:890
  344.6 2.6 collective-permute-start.61
  347.2 2.3 collective-permute-start.63
  350.3 6.3 %collective-permute-done.46 = bf16[24,3072]{1,0:T(8,128)(2,1)S(1)} collective-permute-done((bf16[24,3072]{1,0:T(8,128)(2,1)S(1)}, bf16[24,3072]{1,0:T(8,128)(2,1)S(1)}, u32[]{:S(2)}, u32[]{:S(2)}) %collective-permute-start.46) | collective-permute-done | bytes 147488 | tf_op jit(solution)/shard_map/ppermute | solution.py:890
  361.6 5.9 %assemble.3 = (f32[768,768]{1,0:T(8,128)}, f32[768,768]{1,0:T(8,128)}) custom-call(s32[2]{0:T(128)} %pad_add_fusion.2.place_ref, bf16[2,96,768]{2,1,0:T(8,128)(2,1)} %bitcast.153, bf16[2,96,768]{2,1,0:T(8,128)(2,1)} %copy-done.12, bf16[2,96,768]{2,1,0:T(8,128)(2,1)} %copy-done.11, bf16[96,768]{1,0:T(8,128)(2,1)} %copy-done.44, bf16[96,768]{1,0:T(8,128)(2,1)} %copy-done.43, ...), custom_call_target="tpu_custom_call" | custom-call | flops 6899999744 | bytes 18000000 | tf_op jit(solution)/shard_map/assemble/pallas_call | solution.py:873
  369.5 3.8 collective-permute-done.49.refs_2_
  373.6 9.4 %collective-permute-done.48.refs_1_ = bf16[2,2,24,3072]{3,2,1,0:T(8,128)(2,1)S(1)} collective-permute-done((bf16[2,2,24,3072]{3,2,1,0:T(8,128)(2,1)S(1)}, bf16[2,2,24,3072]{3,2,1,0:T(8,128)(2,1)S(1)}, u32[]{:S(2)}, u32[]{:S(2)}) %collective-permute-start.48) | collective-permute-done | bytes 589856 | tf_op jit(solution)/shard_map/ppermute | solution.py:890
  386.0 3.5 collective-permute-done.51.refs_4_
  390.4 2.2 collective-permute-start.55
  398.6 6.8 %assemble.2 = (f32[768,2304]{1,0:T(8,128)}, f32[768,768]{1,0:T(8,128)}) custom-call(s32[2]{0:T(128)} %pad_add_fusion.2.place_ref, bf16[2,2,24,3072]{3,2,1,0:T(8,128)(2,1)} %bitcast.149, bf16[2,2,24,3072]{3,2,1,0:T(8,128)(2,1)} %copy-done.10, bf16[2,2,24,3072]{3,2,1,0:T(8,128)(2,1)} %copy-done.9, bf16[2,24,3072]{2,1,0:T(8,128)(2,1)} %collective-permute-done.50.refs_3_, ...), custom_call_target="tpu_custom_call" | custom-call | flops 6899999744 | bytes 18000000 | tf_op jit(solution)/shard_map/assemble/pallas_call | solution.py:873
  (342 shorter events, 71.6 us)
Async XLA Ops:
  0.8 43.9 %collective-permute-start.5 = (bf16[512,768]{1,0:T(8,128)(2,1)}, bf16[512,768]{1,0:T(8,128)(2,1)S(1)}, u32[]{:S(2)}, u32[]{:S(2)}) collective-permute-start(bf16[512,768]{1,0:T(8,128)(2,1)} %bitcast.162), channel_id=1, source_target_pairs={{1,0},{2,1},{3,2},{5,4},{6,5},{7,6},{9,8},{10,9},{11,10},{13,12},{... | collective-permute-start | bytes 2359304 | tf_op jit(solution)/shard_map/ppermute | solution.py:890
  2.2 42.5 %collective-permute-start.4 = (bf16[512,768]{1,0:T(8,128)(2,1)}, bf16[512,768]{1,0:T(8,128)(2,1)S(1)}, u32[]{:S(2)}, u32[]{:S(2)}) collective-permute-start(bf16[512,768]{1,0:T(8,128)(2,1)} %bitcast.163), channel_id=1, source_target_pairs={{0,1},{1,2},{2,3},{4,5},{5,6},{6,7},{8,9},{9,10},{10,11},{12,13},{... | collective-permute-start | bytes 2359304 | tf_op jit(solution)/shard_map/ppermute | solution.py:890
  7.9 34.5 %collective-permute-start.6 = (bf16[64,768]{1,0:T(8,128)(2,1)S(1)}, bf16[64,768]{1,0:T(8,128)(2,1)S(1)}, u32[]{:S(2)}, u32[]{:S(2)}) collective-permute-start(bf16[64,768]{1,0:T(8,128)(2,1)S(1)} %get-tuple-element.306), channel_id=1, source_target_pairs={{2,0},{3,1},{6,4},{7,5},{10,8},{11,9},{14,12},{15,13},{18,16},{19,... | collective-permute-start | bytes 294920 | tf_op jit(solution)/shard_map/ppermute | solution.py:890
  9.2 35.3 %collective-permute-start.3 = (bf16[64,768]{1,0:T(8,128)(2,1)S(1)}, bf16[64,768]{1,0:T(8,128)(2,1)S(1)}, u32[]{:S(2)}, u32[]{:S(2)}) collective-permute-start(bf16[64,768]{1,0:T(8,128)(2,1)S(1)} %get-tuple-element.307), channel_id=1, source_target_pairs={{0,2},{1,3},{4,6},{5,7},{8,10},{9,11},{12,14},{13,15},{16,18},{17,... | collective-permute-start | bytes 294920 | tf_op jit(solution)/shard_map/ppermute | solution.py:890
  16.2 41.1 %collective-permute-start.2 = (bf16[208,768]{1,0:T(8,128)(2,1)S(1)}, bf16[208,768]{1,0:T(8,128)(2,1)S(1)}, u32[]{:S(2)}, u32[]{:S(2)}) collective-permute-start(bf16[208,768]{1,0:T(8,128)(2,1)S(1)} %pad_maximum_fusion.6), channel_id=1, source_target_pairs={{0,3},{1,0},{2,1},{3,2},{4,7},{5,4},{6,5},{7,6},{8,11},{9,8},{10,9... | collective-permute-start | bytes 958472 | tf_op jit(solution)/shard_map/ppermute | solution.py:890
  42.4 23.3 %collective-permute-start.1 = (bf16[208,768]{1,0:T(8,128)(2,1)S(1)}, bf16[208,768]{1,0:T(8,128)(2,1)S(1)}, u32[]{:S(2)}, u32[]{:S(2)}) collective-permute-start(bf16[208,768]{1,0:T(8,128)(2,1)S(1)} %pad_maximum_fusion.6), channel_id=1, source_target_pairs={{0,2},{1,3},{2,0},{3,1},{4,6},{5,7},{6,4},{7,5},{8,10},{9,11},{10,... | collective-permute-start | bytes 958472 | tf_op jit(solution)/shard_map/ppermute | solution.py:890
  44.5 21.2 %collective-permute-start = (bf16[208,768]{1,0:T(8,128)(2,1)S(1)}, bf16[208,768]{1,0:T(8,128)(2,1)S(1)}, u32[]{:S(2)}, u32[]{:S(2)}) collective-permute-start(bf16[208,768]{1,0:T(8,128)(2,1)S(1)} %pad_maximum_fusion.6), channel_id=1, source_target_pairs={{0,1},{1,2},{2,3},{3,0},{4,5},{5,6},{6,7},{7,4},{8,9},{9,10},{10,1... | collective-permute-start | bytes 958472 | tf_op jit(solution)/shard_map/ppermute | solution.py:890
  65.9 28.4 %collective-permute-start.8 = (bf16[2,3,96,768]{3,2,1,0:T(8,128)(2,1)S(1)}, bf16[2,3,96,768]{3,2,1,0:T(8,128)(2,1)S(1)}, u32[]{:S(2)}, u32[]{:S(2)}) collective-permute-start(bf16[2,3,96,768]{3,2,1,0:T(8,128)(2,1)S(1)} %bitcast.170), channel_id=1, source_target_pairs={{0,16},{16,0},{1,17},{17,1},{2,18},{18,2},{3,19},{19,3},{4,20},{20... | collective-permute-start | bytes 2654216 | tf_op jit(solution)/shard_map/ppermute | solution.py:890
  67.0 27.3 %collective-permute-start.7 = (bf16[2,3,96,768]{3,2,1,0:T(8,128)(2,1)S(1)}, bf16[2,3,96,768]{3,2,1,0:T(8,128)(2,1)S(1)}, u32[]{:S(2)}, u32[]{:S(2)}) collective-permute-start(bf16[2,3,96,768]{3,2,1,0:T(8,128)(2,1)S(1)} %bitcast.171), channel_id=1, source_target_pairs={{0,8},{8,0},{1,9},{9,1},{2,10},{10,2},{3,11},{11,3},{4,12},{12,4},... | collective-permute-start | bytes 2654216 | tf_op jit(solution)/shard_map/ppermute | solution.py:890
  106.9 15.1 %collective-permute-start.11 = (bf16[4,192,768]{2,1,0:T(8,128)(2,1)}, bf16[4,192,768]{2,1,0:T(8,128)(2,1)S(1)}, u32[]{:S(2)}, u32[]{:S(2)}) collective-permute-start(bf16[4,192,768]{2,1,0:T(8,128)(2,1)} %get-tuple-element.137), channel_id=1, source_target_pairs={{0,4},{4,0},{1,5},{5,1},{2,6},{6,2},{3,7},{7,3},{8,12},{12,8},{9,1... | collective-permute-start | bytes 3538952 | tf_op jit(solution)/shard_map/ppermute | solution.py:890
  107.0 12.8 %collective-permute-start.10 = (bf16[3,96,768]{2,1,0:T(8,128)(2,1)S(1)}, bf16[3,96,768]{2,1,0:T(8,128)(2,1)S(1)}, u32[]{:S(2)}, u32[]{:S(2)}) collective-permute-start(bf16[3,96,768]{2,1,0:T(8,128)(2,1)S(1)} %slice_bitcast_fusion), channel_id=1, source_target_pairs={{0,8},{8,0},{1,9},{9,1},{2,10},{10,2},{3,11},{11,3},{4,12},{12,4},... | collective-permute-start | bytes 1327112 | tf_op jit(solution)/shard_map/ppermute | solution.py:890
  109.3 11.5 %collective-permute-start.9 = (bf16[3,96,768]{2,1,0:T(8,128)(2,1)S(1)}, bf16[3,96,768]{2,1,0:T(8,128)(2,1)S(1)}, u32[]{:S(2)}, u32[]{:S(2)}) collective-permute-start(bf16[3,96,768]{2,1,0:T(8,128)(2,1)S(1)} %slice_bitcast_fusion.1), channel_id=1, source_target_pairs={{0,16},{16,0},{1,17},{17,1},{2,18},{18,2},{3,19},{19,3},{4,20},{20... | collective-permute-start | bytes 1327112 | tf_op jit(solution)/shard_map/ppermute | solution.py:890
  109.4 14.4 %collective-permute-start.12 = (bf16[2,3,96,768]{3,2,1,0:T(8,128)(2,1)S(1)}, bf16[2,3,96,768]{3,2,1,0:T(8,128)(2,1)S(1)}, u32[]{:S(2)}, u32[]{:S(2)}) collective-permute-start(bf16[2,3,96,768]{3,2,1,0:T(8,128)(2,1)S(1)} %bitcast.172), channel_id=1, source_target_pairs={{0,4},{4,0},{1,5},{5,1},{2,6},{6,2},{3,7},{7,3},{8,12},{12,8},{9,1... | collective-permute-start | bytes 2654216 | tf_op jit(solution)/shard_map/ppermute | solution.py:890
  109.7 14.0 %collective-permute-start.13 = (bf16[2,3,96,768]{3,2,1,0:T(8,128)(2,1)S(1)}, bf16[2,3,96,768]{3,2,1,0:T(8,128)(2,1)S(1)}, u32[]{:S(2)}, u32[]{:S(2)}) collective-permute-start(bf16[2,3,96,768]{3,2,1,0:T(8,128)(2,1)S(1)} %collective-permute-done.7.refs_1_), channel_id=1, source_target_pairs={{0,4},{4,0},{1,5},{5,1},{2,6},{6,2},{3,7},{7,3},{8,12},{12,8},{9,1... | collective-permute-start | bytes 2654216 | tf_op jit(solution)/shard_map/ppermute | solution.py:890
  151.2 31.3 %collective-permute-start.17 = (bf16[4,672,768]{2,1,0:T(8,128)(2,1)}, bf16[4,672,768]{2,1,0:T(8,128)(2,1)}, u32[]{:S(2)}, u32[]{:S(2)}) collective-permute-start(bf16[4,672,768]{2,1,0:T(8,128)(2,1)} %get-tuple-element.147), channel_id=1, source_target_pairs={{0,4},{4,0},{1,5},{5,1},{2,6},{6,2},{3,7},{7,3},{8,12},{12,8},{9,1... | collective-permute-start | bytes 12386312 | tf_op jit(solution)/shard_map/ppermute | solution.py:890
  153.9 60.0 %collective-permute-start.22 = (bf16[560,768]{1,0:T(8,128)(2,1)}, bf16[560,768]{1,0:T(8,128)(2,1)}, u32[]{:S(2)}, u32[]{:S(2)}) collective-permute-start(bf16[560,768]{1,0:T(8,128)(2,1)} %get-tuple-element.148.do_ref), channel_id=1, source_target_pairs={{1,0},{2,1},{3,2},{5,4},{6,5},{7,6},{9,8},{10,9},{11,10},{13,12},{... | collective-permute-start | bytes 2580488 | tf_op jit(solution)/shard_map/ppermute | solution.py:890
  155.2 58.7 %collective-permute-start.21 = (bf16[560,768]{1,0:T(8,128)(2,1)}, bf16[560,768]{1,0:T(8,128)(2,1)}, u32[]{:S(2)}, u32[]{:S(2)}) collective-permute-start(bf16[560,768]{1,0:T(8,128)(2,1)} %get-tuple-element.148.do_ref), channel_id=1, source_target_pairs={{0,1},{1,2},{2,3},{4,5},{5,6},{6,7},{8,9},{9,10},{10,11},{12,13},{... | collective-permute-start | bytes 2580488 | tf_op jit(solution)/shard_map/ppermute | solution.py:890
  161.5 24.3 %collective-permute-start.20 = (bf16[80,768]{1,0:T(8,128)(2,1)}, bf16[80,768]{1,0:T(8,128)(2,1)S(1)}, u32[]{:S(2)}, u32[]{:S(2)}) collective-permute-start(bf16[80,768]{1,0:T(8,128)(2,1)} %get-tuple-element.153), channel_id=1, source_target_pairs={{0,2},{1,3},{4,6},{5,7},{8,10},{9,11},{12,14},{13,15},{16,18},{17,... | collective-permute-start | bytes 368648 | tf_op jit(solution)/shard_map/ppermute | solution.py:890
  165.3 47.7 %collective-permute-start.23 = (bf16[80,768]{1,0:T(8,128)(2,1)}, bf16[80,768]{1,0:T(8,128)(2,1)S(1)}, u32[]{:S(2)}, u32[]{:S(2)}) collective-permute-start(bf16[80,768]{1,0:T(8,128)(2,1)} %get-tuple-element.154), channel_id=1, source_target_pairs={{2,0},{3,1},{6,4},{7,5},{10,8},{11,9},{14,12},{15,13},{18,16},{19,... | collective-permute-start | bytes 368648 | tf_op jit(solution)/shard_map/ppermute | solution.py:890
  185.7 39.7 %collective-permute-start.18 = (bf16[2,336,768]{2,1,0:T(8,128)(2,1)S(1)}, bf16[2,336,768]{2,1,0:T(8,128)(2,1)S(1)}, u32[]{:S(2)}, u32[]{:S(2)}) collective-permute-start(bf16[2,336,768]{2,1,0:T(8,128)(2,1)S(1)} %pad_maximum_fusion), channel_id=1, source_target_pairs={{0,8},{8,0},{1,9},{9,1},{2,10},{10,2},{3,11},{11,3},{4,12},{12,4},... | collective-permute-start | bytes 3096584 | tf_op jit(solution)/shard_map/ppermute | solution.py:890
  185.9 39.5 %collective-permute-start.19 = (bf16[2,336,768]{2,1,0:T(8,128)(2,1)S(1)}, bf16[2,336,768]{2,1,0:T(8,128)(2,1)S(1)}, u32[]{:S(2)}, u32[]{:S(2)}) collective-permute-start(bf16[2,336,768]{2,1,0:T(8,128)(2,1)S(1)} %pad_maximum_fusion.1), channel_id=1, source_target_pairs={{0,16},{16,0},{1,17},{17,1},{2,18},{18,2},{3,19},{19,3},{4,20},{20... | collective-permute-start | bytes 3096584 | tf_op jit(solution)/shard_map/ppermute | solution.py:890
  213.1 47.7 %collective-permute-start.29 = (bf16[192,768]{1,0:T(8,128)(2,1)}, bf16[192,768]{1,0:T(8,128)(2,1)}, u32[]{:S(2)}, u32[]{:S(2)}) collective-permute-start(bf16[192,768]{1,0:T(8,128)(2,1)} %get-tuple-element.300), channel_id=1, source_target_pairs={{0,24},{8,16},{16,8},{24,0},{1,25},{9,17},{17,9},{25,1},{2,26},{10... | collective-permute-start | bytes 884744 | tf_op jit(solution)/shard_map/ppermute | solution.py:890
  213.9 48.4 %collective-permute-start.28 = (bf16[192,768]{1,0:T(8,128)(2,1)}, bf16[192,768]{1,0:T(8,128)(2,1)}, u32[]{:S(2)}, u32[]{:S(2)}) collective-permute-start(bf16[192,768]{1,0:T(8,128)(2,1)} %get-tuple-element.301), channel_id=1, source_target_pairs={{0,16},{16,0},{1,17},{17,1},{2,18},{18,2},{3,19},{19,3},{4,20},{20... | collective-permute-start | bytes 884744 | tf_op jit(solution)/shard_map/ppermute | solution.py:890
  213.9 57.9 %collective-permute-start.27 = (bf16[192,768]{1,0:T(8,128)(2,1)}, bf16[192,768]{1,0:T(8,128)(2,1)}, u32[]{:S(2)}, u32[]{:S(2)}) collective-permute-start(bf16[192,768]{1,0:T(8,128)(2,1)} %get-tuple-element.302), channel_id=1, source_target_pairs={{0,8},{8,0},{1,9},{9,1},{2,10},{10,2},{3,11},{11,3},{4,12},{12,4},... | collective-permute-start | bytes 884744 | tf_op jit(solution)/shard_map/ppermute | solution.py:890
  226.6 13.8 %collective-permute-start.24 = (bf16[336,768]{1,0:T(8,128)(2,1)}, bf16[336,768]{1,0:T(8,128)(2,1)}, u32[]{:S(2)}, u32[]{:S(2)}) collective-permute-start(bf16[336,768]{1,0:T(8,128)(2,1)} %fusion.5), channel_id=1, source_target_pairs={{0,16},{16,0},{1,17},{17,1},{2,18},{18,2},{3,19},{19,3},{4,20},{20... | collective-permute-start | bytes 1548296 | tf_op jit(solution)/shard_map/ppermute | solution.py:890
  228.0 14.2 %collective-permute-start.25 = (bf16[336,768]{1,0:T(8,128)(2,1)S(1)}, bf16[336,768]{1,0:T(8,128)(2,1)}, u32[]{:S(2)}, u32[]{:S(2)}) collective-permute-start(bf16[336,768]{1,0:T(8,128)(2,1)S(1)} %fusion.4), channel_id=1, source_target_pairs={{0,8},{8,0},{1,9},{9,1},{2,10},{10,2},{3,11},{11,3},{4,12},{12,4},... | collective-permute-start | bytes 1548296 | tf_op jit(solution)/shard_map/ppermute | solution.py:890
  240.3 43.5 %collective-permute-start.26 = (bf16[4,96,2304]{2,1,0:T(8,128)(2,1)}, bf16[4,96,2304]{2,1,0:T(8,128)(2,1)S(1)}, u32[]{:S(2)}, u32[]{:S(2)}) collective-permute-start(bf16[4,96,2304]{2,1,0:T(8,128)(2,1)} %get-tuple-element.183), channel_id=1, source_target_pairs={{0,4},{4,0},{1,5},{5,1},{2,6},{6,2},{3,7},{7,3},{8,12},{12,8},{9,1... | collective-permute-start | bytes 5308424 | tf_op jit(solution)/shard_map/ppermute | solution.py:890
  245.1 26.7 %collective-permute-start.32 = (bf16[192,768]{1,0:T(8,128)(2,1)S(1)}, bf16[192,768]{1,0:T(8,128)(2,1)S(1)}, u32[]{:S(2)}, u32[]{:S(2)}) collective-permute-start(bf16[192,768]{1,0:T(8,128)(2,1)S(1)} %get-tuple-element.311), channel_id=1, source_target_pairs={{0,1},{1,2},{2,3},{3,0},{4,5},{5,6},{6,7},{7,4},{8,9},{9,10},{10,1... | collective-permute-start | bytes 884744 | tf_op jit(solution)/shard_map/ppermute | solution.py:890
  260.7 15.5 %collective-permute-start.31 = (bf16[192,768]{1,0:T(8,128)(2,1)S(1)}, bf16[192,768]{1,0:T(8,128)(2,1)S(1)}, u32[]{:S(2)}, u32[]{:S(2)}) collective-permute-start(bf16[192,768]{1,0:T(8,128)(2,1)S(1)} %get-tuple-element.312), channel_id=1, source_target_pairs={{0,2},{1,3},{2,0},{3,1},{4,6},{5,7},{6,4},{7,5},{8,10},{9,11},{10,... | collective-permute-start | bytes 884744 | tf_op jit(solution)/shard_map/ppermute | solution.py:890
  262.4 17.5 %collective-permute-start.30 = (bf16[192,768]{1,0:T(8,128)(2,1)S(1)}, bf16[192,768]{1,0:T(8,128)(2,1)S(1)}, u32[]{:S(2)}, u32[]{:S(2)}) collective-permute-start(bf16[192,768]{1,0:T(8,128)(2,1)S(1)} %get-tuple-element.313), channel_id=1, source_target_pairs={{0,3},{1,0},{2,1},{3,2},{4,7},{5,4},{6,5},{7,6},{8,11},{9,8},{10,9... | collective-permute-start | bytes 884744 | tf_op jit(solution)/shard_map/ppermute | solution.py:890
  281.3 52.0 %collective-permute-start.58 = (bf16[2,96,768]{2,1,0:T(8,128)(2,1)S(1)}, bf16[2,96,768]{2,1,0:T(8,128)(2,1)S(1)}, u32[]{:S(2)}, u32[]{:S(2)}) collective-permute-start(bf16[2,96,768]{2,1,0:T(8,128)(2,1)S(1)} %bitcast.150), channel_id=1, source_target_pairs={{0,16},{16,0},{1,17},{17,1},{2,18},{18,2},{3,19},{19,3},{4,20},{20... | collective-permute-start | bytes 884744 | tf_op jit(solution)/shard_map/ppermute | solution.py:890
  284.2 15.0 %collective-permute-start.35 = (bf16[2,48,2304]{2,1,0:T(8,128)(2,1)S(1)}, bf16[2,48,2304]{2,1,0:T(8,128)(2,1)S(1)}, u32[]{:S(2)}, u32[]{:S(2)}) collective-permute-start(bf16[2,48,2304]{2,1,0:T(8,128)(2,1)S(1)} %pad_maximum_fusion.5), channel_id=1, source_target_pairs={{0,16},{16,0},{1,17},{17,1},{2,18},{18,2},{3,19},{19,3},{4,20},{20... | collective-permute-start | bytes 1327112 | tf_op jit(solution)/shard_map/ppermute | solution.py:890
  284.3 14.9 %collective-permute-start.33 = (bf16[2,48,2304]{2,1,0:T(8,128)(2,1)S(1)}, bf16[2,48,2304]{2,1,0:T(8,128)(2,1)S(1)}, u32[]{:S(2)}, u32[]{:S(2)}) collective-permute-start(bf16[2,48,2304]{2,1,0:T(8,128)(2,1)S(1)} %pad_maximum_fusion.4), channel_id=1, source_target_pairs={{0,8},{8,0},{1,9},{9,1},{2,10},{10,2},{3,11},{11,3},{4,12},{12,4},... | collective-permute-start | bytes 1327112 | tf_op jit(solution)/shard_map/ppermute | solution.py:890
  306.0 12.1 %collective-permute-start.37 = (bf16[24,3072]{1,0:T(8,128)(2,1)S(1)}, bf16[24,3072]{1,0:T(8,128)(2,1)S(1)}, u32[]{:S(2)}, u32[]{:S(2)}) collective-permute-start(bf16[24,3072]{1,0:T(8,128)(2,1)S(1)} %get-tuple-element.308), channel_id=1, source_target_pairs={{0,1},{1,2},{2,3},{3,0},{4,5},{5,6},{6,7},{7,4},{8,9},{9,10},{10,1... | collective-permute-start | bytes 442376 | tf_op jit(solution)/shard_map/ppermute | solution.py:890
  315.4 11.8 %collective-permute-start.38 = (bf16[24,3072]{1,0:T(8,128)(2,1)S(1)}, bf16[24,3072]{1,0:T(8,128)(2,1)S(1)}, u32[]{:S(2)}, u32[]{:S(2)}) collective-permute-start(bf16[24,3072]{1,0:T(8,128)(2,1)S(1)} %get-tuple-element.310), channel_id=1, source_target_pairs={{0,2},{1,3},{2,0},{3,1},{4,6},{5,7},{6,4},{7,5},{8,10},{9,11},{10,... | collective-permute-start | bytes 442376 | tf_op jit(solution)/shard_map/ppermute | solution.py:890
  331.7 10.9 %collective-permute-start.57 = (bf16[2,96,768]{2,1,0:T(8,128)(2,1)S(1)}, bf16[2,96,768]{2,1,0:T(8,128)(2,1)S(1)}, u32[]{:S(2)}, u32[]{:S(2)}) collective-permute-start(bf16[2,96,768]{2,1,0:T(8,128)(2,1)S(1)} %bitcast.151), channel_id=1, source_target_pairs={{0,8},{8,0},{1,9},{9,1},{2,10},{10,2},{3,11},{11,3},{4,12},{12,4},... | collective-permute-start | bytes 884744 | tf_op jit(solution)/shard_map/ppermute | solution.py:890
  333.3 11.3 %collective-permute-start.60 = (bf16[96,768]{1,0:T(8,128)(2,1)S(1)}, bf16[96,768]{1,0:T(8,128)(2,1)S(1)}, u32[]{:S(2)}, u32[]{:S(2)}) collective-permute-start(bf16[96,768]{1,0:T(8,128)(2,1)S(1)} %slice_bitcast_fusion.4), channel_id=1, source_target_pairs={{0,8},{8,0},{1,9},{9,1},{2,10},{10,2},{3,11},{11,3},{4,12},{12,4},... | collective-permute-start | bytes 442376 | tf_op jit(solution)/shard_map/ppermute | solution.py:890
  343.5 13.1 %collective-permute-start.46 = (bf16[24,3072]{1,0:T(8,128)(2,1)S(1)}, bf16[24,3072]{1,0:T(8,128)(2,1)S(1)}, u32[]{:S(2)}, u32[]{:S(2)}) collective-permute-start(bf16[24,3072]{1,0:T(8,128)(2,1)S(1)} %get-tuple-element.304), channel_id=1, source_target_pairs={{0,2},{1,3},{2,0},{3,1},{4,6},{5,7},{6,4},{7,5},{8,10},{9,11},{10,... | collective-permute-start | bytes 442376 | tf_op jit(solution)/shard_map/ppermute | solution.py:890
  344.6 13.3 %collective-permute-start.45 = (bf16[24,3072]{1,0:T(8,128)(2,1)S(1)}, bf16[24,3072]{1,0:T(8,128)(2,1)S(1)}, u32[]{:S(2)}, u32[]{:S(2)}) collective-permute-start(bf16[24,3072]{1,0:T(8,128)(2,1)S(1)} %get-tuple-element.304), channel_id=1, source_target_pairs={{0,1},{1,2},{2,3},{3,0},{4,5},{5,6},{6,7},{7,4},{8,9},{9,10},{10,1... | collective-permute-start | bytes 442376 | tf_op jit(solution)/shard_map/ppermute | solution.py:890
  344.6 13.3 %collective-permute-start.61 = (bf16[2,96,768]{2,1,0:T(8,128)(2,1)S(1)}, bf16[2,96,768]{2,1,0:T(8,128)(2,1)S(1)}, u32[]{:S(2)}, u32[]{:S(2)}) collective-permute-start(bf16[2,96,768]{2,1,0:T(8,128)(2,1)S(1)} %bitcast.152), channel_id=1, source_target_pairs={{0,4},{4,0},{1,5},{5,1},{2,6},{6,2},{3,7},{7,3},{8,12},{12,8},{9,1... | collective-permute-start | bytes 884744 | tf_op jit(solution)/shard_map/ppermute | solution.py:890
  347.2 12.9 %collective-permute-start.63 = (bf16[2,96,768]{2,1,0:T(8,128)(2,1)S(1)}, bf16[2,96,768]{2,1,0:T(8,128)(2,1)S(1)}, u32[]{:S(2)}, u32[]{:S(2)}) collective-permute-start(bf16[2,96,768]{2,1,0:T(8,128)(2,1)S(1)} %collective-permute-done.58.refs_2_), channel_id=1, source_target_pairs={{0,4},{4,0},{1,5},{5,1},{2,6},{6,2},{3,7},{7,3},{8,12},{12,8},{9,1... | collective-permute-start | bytes 884744 | tf_op jit(solution)/shard_map/ppermute | solution.py:890
  358.8 14.5 %collective-permute-start.49 = (bf16[2,2,24,3072]{3,2,1,0:T(8,128)(2,1)S(1)}, bf16[2,2,24,3072]{3,2,1,0:T(8,128)(2,1)S(1)}, u32[]{:S(2)}, u32[]{:S(2)}) collective-permute-start(bf16[2,2,24,3072]{3,2,1,0:T(8,128)(2,1)S(1)} %bitcast.146), channel_id=1, source_target_pairs={{0,16},{16,0},{1,17},{17,1},{2,18},{18,2},{3,19},{19,3},{4,20},{20... | collective-permute-start | bytes 1769480 | tf_op jit(solution)/shard_map/ppermute | solution.py:890
  367.5 30.1 %collective-permute-start.52 = (bf16[2,2,24,3072]{3,2,1,0:T(8,128)(2,1)S(1)}, bf16[2,2,24,3072]{3,2,1,0:T(8,128)(2,1)S(1)}, u32[]{:S(2)}, u32[]{:S(2)}) collective-permute-start(bf16[2,2,24,3072]{3,2,1,0:T(8,128)(2,1)S(1)} %bitcast.147), channel_id=1, source_target_pairs={{0,4},{4,0},{1,5},{5,1},{2,6},{6,2},{3,7},{7,3},{8,12},{12,8},{9,1... | collective-permute-start | bytes 1769480 | tf_op jit(solution)/shard_map/ppermute | solution.py:890
  368.1 14.9 %collective-permute-start.48 = (bf16[2,2,24,3072]{3,2,1,0:T(8,128)(2,1)S(1)}, bf16[2,2,24,3072]{3,2,1,0:T(8,128)(2,1)S(1)}, u32[]{:S(2)}, u32[]{:S(2)}) collective-permute-start(bf16[2,2,24,3072]{3,2,1,0:T(8,128)(2,1)S(1)} %bitcast.148), channel_id=1, source_target_pairs={{0,8},{8,0},{1,9},{9,1},{2,10},{10,2},{3,11},{11,3},{4,12},{12,4},... | collective-permute-start | bytes 1769480 | tf_op jit(solution)/shard_map/ppermute | solution.py:890
  368.6 15.2 %collective-permute-start.44 = (f32[85,128]{1,0:T(8,128)S(1)}, f32[85,128]{1,0:T(8,128)S(1)}, u32[]{:S(2)}, u32[]{:S(2)}) collective-permute-start(f32[85,128]{1,0:T(8,128)S(1)} %add.364), channel_id=1, source_target_pairs={{0,2},{1,3},{2,0},{3,1},{4,6},{5,7},{6,4},{7,5},{8,10},{9,11},{10,... | collective-permute-start | bytes 130568 | tf_op jit(solution)/shard_map/ppermute | solution.py:890
  373.4 16.0 %collective-permute-start.51 = (bf16[2,24,3072]{2,1,0:T(8,128)(2,1)S(1)}, bf16[2,24,3072]{2,1,0:T(8,128)(2,1)S(1)}, u32[]{:S(2)}, u32[]{:S(2)}) collective-permute-start(bf16[2,24,3072]{2,1,0:T(8,128)(2,1)S(1)} %slice_bitcast_fusion.2), channel_id=1, source_target_pairs={{0,8},{8,0},{1,9},{9,1},{2,10},{10,2},{3,11},{11,3},{4,12},{12,4},... | collective-permute-start | bytes 884744 | tf_op jit(solution)/shard_map/ppermute | solution.py:890
  384.4 13.3 %collective-permute-start.54 = (bf16[2,2,24,3072]{3,2,1,0:T(8,128)(2,1)S(1)}, bf16[2,2,24,3072]{3,2,1,0:T(8,128)(2,1)S(1)}, u32[]{:S(2)}, u32[]{:S(2)}) collective-permute-start(bf16[2,2,24,3072]{3,2,1,0:T(8,128)(2,1)S(1)} %collective-permute-done.49.refs_2_), channel_id=1, source_target_pairs={{0,4},{4,0},{1,5},{5,1},{2,6},{6,2},{3,7},{7,3},{8,12},{12,8},{9,1... | collective-permute-start | bytes 1769480 | tf_op jit(solution)/shard_map/ppermute | solution.py:890
  386.0 11.7 %collective-permute-start.53 = (bf16[2,2,24,3072]{3,2,1,0:T(8,128)(2,1)S(1)}, bf16[2,2,24,3072]{3,2,1,0:T(8,128)(2,1)}, u32[]{:S(2)}, u32[]{:S(2)}) collective-permute-start(bf16[2,2,24,3072]{3,2,1,0:T(8,128)(2,1)S(1)} %collective-permute-done.48.refs_1_), channel_id=1, source_target_pairs={{0,4},{4,0},{1,5},{5,1},{2,6},{6,2},{3,7},{7,3},{8,12},{12,8},{9,1... | collective-permute-start | bytes 1769480 | tf_op jit(solution)/shard_map/ppermute | solution.py:890
  (71 other events, 829.3 us)

commit v2 on v1

v2 whole, which is shorter than its diff:
```python
import functools

import jax
import jax.numpy as jnp
import numpy as np
from jax import lax
from jax.experimental import pallas as pl
from jax.experimental.pallas import tpu as pltpu
from jax.sharding import Mesh, PartitionSpec as P

EPS = 1e-06
MASKED = -1e30
BLK = 128
SPAN = 6
SPAN_SIDE = 3
SPAN_BACK = 2
GROUP = 4
REACH = 64
STAT_ROWS = 6
STAT_PAD = 16
SIDE = 32
LN1_GAIN, LN1_SHIFT, B_OUT, LN2_GAIN, LN2_SHIFT, B_DOWN = (slice(n, n + 1) for n in range(6))
LOG2E = np.float32(1.4426950408889634)
BF = jnp.bfloat16
F32 = jnp.float32
PLANE = ("a", "b", "c")
SWAP = [(0, 1), (1, 0)]
FIRST = [(i, i ^ (4 if i % 2 else 2)) for i in range(8)]
SECOND = [(i, i ^ (2 if i % 2 else 4)) for i in range(8)]
VMEM_LIMIT = 56 * 1024 * 1024


def dot(left, right):
    return lax.dot_general(left, right, (((1,), (0,)), ((), ())), preferred_element_type=F32)


def dot_nt(left, right):
    return lax.dot_general(left, right, (((1,), (1,)), ((), ())), preferred_element_type=F32)


def dot_tn(left, right):
    return lax.dot_general(left, right, (((0,), (0,)), ((), ())), preferred_element_type=F32)


def params(**kw):
    return pltpu.CompilerParams(vmem_limit_bytes=VMEM_LIMIT, **kw)


def cost(us):
    return pl.CostEstimate(
        flops=int(us * 1.15e9), bytes_accessed=int(us * 3.0e6), transcendentals=0
    )


def whole(shape):
    return pl.BlockSpec(shape, lambda *_: (0,) * len(shape))


ANY = pl.BlockSpec(memory_space=pl.ANY)
SMEM = pl.BlockSpec(memory_space=pltpu.SMEM)


def rounded(x):
    return lax.reduce_precision(x, exponent_bits=8, mantissa_bits=7)


def turn_table(rope_freqs):
    lanes = rope_freqs.shape[1] * rope_freqs.shape[2]
    freq = rope_freqs.reshape(2, 1, lanes)
    angle = jnp.arange(SIDE, dtype=F32)[None, :, None] * freq
    cosine, sine = jnp.cos(angle), jnp.sin(angle)

    def halves(x):
        return jnp.concatenate([x.astype(BF), (x - rounded(x)).astype(BF)], 0)

    def grouped(x):
        return x.reshape(2 * SIDE, lanes // 128, 1, 128)

    zero = jnp.zeros((2 * SIDE, lanes // 128, 2, 128), BF)
    rows = jnp.concatenate([grouped(halves(cosine[0])), grouped(halves(sine[0])), zero], 2)
    cols = jnp.concatenate([zero, grouped(halves(cosine[1])), grouped(halves(sine[1]))], 2)
    return jnp.concatenate([rows, cols], 0).reshape(4 * SIDE, 4 * lanes)


def cos_sin(onehot, table):
    parts = dot(onehot, table)
    cr, sr, cc, sc = (parts[:, lanes_of(n, 128)] for n in range(4))
    return cr * cc - sr * sc, sr * cc + cr * sc


def layer_norm_low(x, gain, shift):
    centred = x - jnp.mean(x, -1, keepdims=True)
    var = jnp.mean(centred * centred, -1, keepdims=True)
    return (centred * lax.rsqrt(var + EPS) * gain + shift).astype(BF)


def project(norm, hot_ref, table_ref, weights, b_ref, q_out, k_out, v_ref, exact):
    width = norm.shape[1]
    for g in range(width // 256):
        c, s = cos_sin(hot_ref[...], table_ref[:, lanes_of(g, 512)])
        for n, out in enumerate((q_out, k_out)):
            lo = n * width + 256 * g
            proj = dot(norm, weights[:, lo : lo + 256]) + b_ref[:, lo : lo + 256]
            for half, turned in enumerate(
                (proj[:, :128] * c - proj[:, 128:] * s, proj[:, :128] * s + proj[:, 128:] * c)
            ):
                at = slice(256 * g + 128 * half, 256 * g + 128 * half + 128)
                out[:, at] = turned.astype(BF)
                if exact:
                    exact[n][:, at] = turned
    for g in range(width // 256):
        lo = 2 * width + 256 * g
        v_ref[:, 256 * g : 256 * g + 256] = (
            dot(norm, weights[:, lo : lo + 256]) + b_ref[:, lo : lo + 256]
        ).astype(BF)


def qkv_own_kernel(
    x_ref, hot_ref, vec_ref, w_ref, b_ref, order_ref, table_ref,
    q_ref, k_ref, v_ref, pq_ref, pk_ref, w_turned,
):
    width = x_ref.shape[1]

    @pl.when(pl.program_id(0) == 0)
    def _():
        for g in range(2 * width // 256):
            at = slice(256 * g, 256 * g + 256)
            w_turned[:, at] = dot(w_ref[:, at], order_ref[...]).astype(BF)
        w_turned[:, 2 * width :] = w_ref[:, 2 * width :]

    norm = layer_norm_low(x_ref[...].astype(F32), vec_ref[LN1_GAIN], vec_ref[LN1_SHIFT])
    project(norm, hot_ref, table_ref, w_turned, b_ref, q_ref, k_ref, v_ref, (pq_ref, pk_ref))


def qkv_own_call(x, onehot, vectors, weight, bias, order, table, first):
    own, width = x.shape
    rows = onehot.shape[0]
    tile = 256
    shape = jax.ShapeDtypeStruct((rows, width), BF)
    exact = jax.ShapeDtypeStruct((own, width), F32)
    row = lambda w: pl.BlockSpec((tile, w), lambda i: (i, 0))
    inside = lambda w: pl.BlockSpec(
        (pl.Element(tile), pl.Element(w)), lambda i: (pl.multiple_of(first + tile * i, BLK), 0)
    )
    return pl.pallas_call(
        qkv_own_kernel,
        grid=(own // tile,),
        in_specs=[
            row(width),
            inside(onehot.shape[1]),
            whole(vectors.shape),
            whole(weight.shape),
            whole((1, 3 * width)),
            whole(order.shape),
            whole(table.shape),
        ],
        out_specs=[inside(width)] * 3 + [row(width)] * 2 + [whole(weight.shape)],
        out_shape=[shape] * 3 + [exact] * 2 + [jax.ShapeDtypeStruct(weight.shape, BF)],
        compiler_params=params(),
        cost_estimate=cost(8),
        name="qkv_own",
    )(x, onehot, vectors, weight, bias[None], order, table)


def qkv_halo_kernel(
    far_l, near_l, near_r, far_r, hot_ref, vec_ref, w_ref, b_ref, table_ref,
    q_in, k_in, v_in, q_ref, k_ref, v_ref, x_all, sem,
):
    width = x_all.shape[1]
    step = pl.program_id(0)
    tile = q_ref.shape[0]

    @pl.when(step == 0)
    def _():
        own, reach = near_l.shape[0], far_l.shape[0]
        total = x_all.shape[0]
        blank = total // 2 - own - reach
        copies = []
        at = blank
        for n, ref in enumerate((far_l, near_l, near_r, far_r)):
            copies.append(
                pltpu.make_async_copy(ref, x_all.at[at : at + ref.shape[0], :], sem.at[n])
            )
            copies[-1].start()
            at += ref.shape[0]
        x_all[:blank, :] = jnp.zeros((blank, width), BF)
        x_all[total - blank :, :] = jnp.zeros((blank, width), BF)
        for copy in copies:
            copy.wait()

    x = x_all[pl.ds(pl.multiple_of(step * tile, tile), tile), :].astype(F32)
    norm = layer_norm_low(x, vec_ref[LN1_GAIN], vec_ref[LN1_SHIFT])
    project(norm, hot_ref, table_ref, w_ref, b_ref, q_ref, k_ref, v_ref, ())


def qkv_halo_call(pieces, onehot, vectors, weight, bias, table, q, k, v, first):
    rows, width = q.shape
    own = pieces[1].shape[0]
    tile = first // 2
    shape = jax.ShapeDtypeStruct((rows, width), BF)
    at = lambda w: pl.BlockSpec(
        (pl.Element(tile), pl.Element(w)), lambda i: (pl.multiple_of(tile * i + jnp.where(i >= 2, own, 0), 64), 0)
    )
    return pl.pallas_call(
        qkv_halo_kernel,
        grid=(4,),
        in_specs=[ANY] * 4
        + [
            at(onehot.shape[1]),
            whole(vectors.shape),
            whole(weight.shape),
            whole((1, 3 * width)),
            whole(table.shape),
        ]
        + [ANY] * 3,
        out_specs=[at(width)] * 3,
        out_shape=[shape] * 3,
        input_output_aliases={9: 0, 10: 1, 11: 2},
        scratch_shapes=[pltpu.VMEM((2 * first, width), BF), pltpu.SemaphoreType.DMA((4,))],
        compiler_params=params(),
        cost_estimate=cost(11.5),
        name="qkv_halo",
    )(*pieces, onehot, vectors, weight, bias[None], table, q, k, v)


def head_stack(block, turned, scale=None):
    lane = lax.broadcasted_iota(jnp.int32, block.shape, 1)
    head = (lane % 128) // 32 if turned else lane // 64
    if scale is not None:
        block = block * scale
    zero = jnp.zeros_like(block)
    return jnp.concatenate([jnp.where(head == h, block, zero) for h in range(GROUP)], 0)


def fold8(x, op):
    return op(x.reshape(x.shape[0] // 8, 8, x.shape[1]), axis=0)


def key_span(ident_ref, ident_q, start, c, span, end):
    block = jnp.minimum(start + c * span, end - span)
    lower = (start + c * span - block) * BLK
    at = pl.ds(pl.multiple_of(block * BLK, BLK), span * BLK)
    row = lax.broadcasted_iota(jnp.int32, (span * BLK, BLK), 0)
    return at, (ident_ref[at, :] == ident_q) & (row >= lower)


def lanes_of(g, size=256):
    return slice(size * g, size * g + size)


def forward_kernel(
    bound_ref, q_ref, k_ref, v_ref, idk_ref, idq_ref, *refs, first, base
):
    o_ref, low_ref, lse_ref, s_ref, acc_ref, q4_ref = refs[-6:]
    i = pl.program_id(0) + base
    groups = k_ref.shape[1] // 256
    lanes = GROUP * BLK
    window = k_ref.shape[0] // BLK
    start, count = bound_ref[i, 0], bound_ref[i, 1]
    for g in range(groups):
        q4_ref[g] = head_stack(q_ref[:, lanes_of(g)], True, jnp.asarray(0.125, BF))
    ident_q = idq_ref[pl.ds(first // BLK + i, 1), :]

    def scores(c, top):
        at, seen = key_span(idk_ref, ident_q, start, c, SPAN, window)
        here = pl.ds(pl.multiple_of(c * SPAN * BLK, BLK), SPAN * BLK)
        tops = []
        for g in range(groups):
            s = dot_nt(k_ref[at, lanes_of(g)], q4_ref[g]) * LOG2E
            for h in range(GROUP):
                masked = jnp.where(seen, s[:, lanes_of(h, BLK)], MASKED)
                s_ref[g, here, lanes_of(h, BLK)] = masked
                tops.append(fold8(masked, jnp.max))
        return jnp.maximum(top, jnp.concatenate(tops, 1))

    top = lax.fori_loop(0, count, scores, jnp.full((8, groups * lanes), -3e38, F32))
    top = jnp.max(top, 0, keepdims=True)
    acc_ref[...] = jnp.zeros_like(acc_ref)

    def mix(c, total):
        at, _ = key_span(idk_ref, ident_q, start, c, SPAN, window)
        here = pl.ds(pl.multiple_of(c * SPAN * BLK, BLK), SPAN * BLK)
        sums = []
        for g in range(groups):
            e = jnp.exp2(s_ref[g, here, :] - top[:, lanes_of(g, lanes)])
            sums.append(fold8(e, jnp.sum))
            acc_ref[g] += dot_tn(v_ref[at, lanes_of(g)], e.astype(BF))
        return total + jnp.concatenate(sums, 1)

    total = lax.fori_loop(0, count, mix, jnp.zeros((8, groups * lanes), F32))
    total = jnp.sum(total, 0, keepdims=True)
    lse = top + jnp.log(total) * LOG2E
    inverse = 1.0 / total
    for g in range(groups):
        lse_ref[g] = lse[:, lanes_of(g, lanes)]
        acc = acc_ref[g] * inverse[:, lanes_of(g, lanes)]
        out = jnp.concatenate(
            [acc[64 * h : 64 * h + 64, lanes_of(h, BLK)] for h in range(GROUP)], 0
        ).T
        o_ref[:, lanes_of(g)] = out
        low_ref[:, lanes_of(g)] = out.astype(BF)


def stat_spec(groups, base=0):
    return pl.BlockSpec((groups, None, 1, GROUP * BLK), lambda i: (0, i + base, 0, 0))


def query_rows(first, width):
    return pl.BlockSpec(
        (pl.Element(BLK), pl.Element(width)), lambda i: (pl.multiple_of(first + BLK * i, BLK), 0)
    )


def forward_call(bounds, q_win, k_win, v_win, idk, idq, first, own, base, count, earlier=()):
    win, width = k_win.shape
    groups, blocks = width // 256, own // BLK
    row = pl.BlockSpec((BLK, width), lambda i: (i + base, 0))
    steps = -(-win // (SPAN * BLK))
    return pl.pallas_call(
        functools.partial(forward_kernel, first=first, base=base),
        grid=(count,),
        in_specs=[SMEM, query_rows(first + base * BLK, width)]
        + [whole((win, width))] * 2
        + [whole(idk.shape), whole(idq.shape)]
        + [ANY] * len(earlier),
        out_specs=[row, row, stat_spec(groups, base)],
        input_output_aliases={6 + n: n for n in range(len(earlier))},
        out_shape=[
            jax.ShapeDtypeStruct((own, width), F32),
            jax.ShapeDtypeStruct((own, width), BF),
            jax.ShapeDtypeStruct((groups, blocks, 1, GROUP * BLK), F32),
        ],
        scratch_shapes=[
            pltpu.VMEM((groups, steps * SPAN * BLK, GROUP * BLK), F32),
            pltpu.VMEM((groups, 256, GROUP * BLK), F32),
            pltpu.VMEM((groups, GROUP * BLK, 256), BF),
        ],
        compiler_params=params(),
        cost_estimate=cost(4 * count),
        name="attention_forward",
    )(bounds, q_win, k_win, v_win, idk, idq, *earlier)


def score_gradients(s, dp, lse, delta, seen):
    low_p, low_ds = [], []
    for h in range(GROUP):
        at = lanes_of(h, BLK)
        p = jnp.exp2(jnp.where(seen, s[:, at] * LOG2E - lse[:, at], MASKED))
        low_p.append(p.astype(BF))
        low_ds.append((p * (dp[:, at] - delta[:, at])).astype(BF))
    return jnp.concatenate(low_p, 1), jnp.concatenate(low_ds, 1)


def backward_own_kernel(
    bound_ref, q_ref, do_ref, k_ref, v_ref, idk_ref, idq_ref, lse_ref, delta_ref,
    dq_ref, dk_ref, dv_ref, acc_ref, q4_ref, do4_ref, *, first,
):
    i = pl.program_id(0)
    groups = k_ref.shape[1] // 256
    own = dk_ref.shape[0]

    @pl.when(i == 0)
    def _():
        dk_ref[...] = jnp.zeros_like(dk_ref)
        dv_ref[...] = jnp.zeros_like(dv_ref)

    for g in range(groups):
        q4_ref[g] = head_stack(q_ref[:, lanes_of(g)], True, jnp.asarray(0.125, BF))
        do4_ref[g] = head_stack(do_ref[:, lanes_of(g)], False)
    ident_q = idq_ref[pl.ds(first // BLK + i, 1), :]

    def attend(at, seen, inside):
        for g in range(groups):
            keys = k_ref[at, lanes_of(g)]
            s = dot_nt(keys, q4_ref[g])
            dp = dot_nt(v_ref[at, lanes_of(g)], do4_ref[g])
            low_p, low_ds = score_gradients(s, dp, lse_ref[g], delta_ref[g], seen)
            if inside:
                acc_ref[g] = dot_tn(keys, low_ds)
                dk_ref[:, lanes_of(g)] += dot(low_ds, q4_ref[g])
                dv_ref[:, lanes_of(g)] += dot(low_p, do4_ref[g])
            else:
                acc_ref[g] += dot_tn(keys, low_ds)

    attend(slice(first, first + own), idk_ref[first : first + own, :] == ident_q, True)
    for start, count, end in (
        (bound_ref[i, 2], bound_ref[i, 3], first // BLK),
        ((first + own) // BLK, bound_ref[i, 4], k_ref.shape[0] // BLK),
    ):

        def step(c, _):
            attend(*key_span(idk_ref, ident_q, start, c, SPAN_SIDE, end), False)
            return 0

        lax.fori_loop(0, count, step, 0)
    for g in range(groups):
        acc = acc_ref[g]
        parts = [acc[32 * h : 32 * h + 32, lanes_of(h, BLK)] for h in range(GROUP)]
        parts += [acc[128 + 32 * h : 160 + 32 * h, lanes_of(h, BLK)] for h in range(GROUP)]
        dq_ref[:, lanes_of(g)] = (jnp.concatenate(parts, 0) * 0.125).T


def backward_own_call(bounds, q_win, do_own, k_win, v_win, idk, idq, lse, delta, first, own):
    win, width = k_win.shape
    groups = width // 256
    row = pl.BlockSpec((BLK, width), lambda i: (i, 0))
    return pl.pallas_call(
        functools.partial(backward_own_kernel, first=first),
        grid=(own // BLK,),
        in_specs=[SMEM, query_rows(first, width), row]
        + [whole((win, width))] * 2
        + [whole(idk.shape), whole(idq.shape), stat_spec(groups), stat_spec(groups)],
        out_specs=[row] + [whole((own, width))] * 2,
        out_shape=[jax.ShapeDtypeStruct((own, width), F32)] * 3,
        scratch_shapes=[pltpu.VMEM((groups, 256, GROUP * BLK), F32)]
        + [pltpu.VMEM((groups, GROUP * BLK, 256), BF)] * 2,
        compiler_params=params(),
        cost_estimate=cost(20),
        name="attention_backward_own",
    )(bounds, q_win, do_own, k_win, v_win, idk, idq, lse, delta)


def backward_halo_kernel(
    bound_ref, q_ref, far_l, near_l, near_r, far_r, k_ref, v_ref, idk_ref, idq_ref, dk_in, dv_in,
    dk_ref, dv_ref, q4_ref, do_all, do4_ref, stat_ref, *, first,
):
    groups = k_ref.shape[1] // 256
    own, reach = k_ref.shape[0], far_l.shape[0] - STAT_PAD
    blocks = own // BLK
    side = first // BLK
    step_id = pl.program_id(0)
    j = jnp.where(step_id < side, step_id, step_id + blocks)
    lanes = GROUP * BLK

    def stats(ref, row, slot):
        parts = ref[row : row + 2 * STAT_ROWS, :].astype(F32)
        sums = parts[0:4] + parts[4:8] + parts[8:12]
        for g in range(groups):
            for n in range(2):
                stat_ref[n, g, slot : slot + 1, :] = jnp.concatenate(
                    [sums[2 * n : 2 * n + 1, lanes_of(g)], sums[2 * n + 1 : 2 * n + 2, lanes_of(g)]],
                    1,
                )

    @pl.when(step_id == 0)
    def _():
        dk_ref[...] = dk_in[...]
        dv_ref[...] = dv_in[...]
        blank = jnp.zeros((BLK - reach, do_all.shape[1]), BF)
        do_all[0 : BLK - reach, :] = blank
        do_all[BLK - reach : BLK, :] = far_l[:reach, :]
        do_all[BLK : BLK + own, :] = near_l[:own, :]
        do_all[BLK + own : BLK + 2 * own, :] = near_r[:own, :]
        do_all[BLK + 2 * own : BLK + 2 * own + reach, :] = far_r[:reach, :]
        do_all[BLK + 2 * own + reach :, :] = blank
        stats(far_l, reach, 0)
        for i in range(blocks):
            stats(near_l, own + 2 * STAT_ROWS * i, 1 + i)
            stats(near_r, own + 2 * STAT_ROWS * i, 1 + blocks + i)
        stats(far_r, reach, 1 + 2 * blocks)

    start, count = bound_ref[j, 0], bound_ref[j, 1]

    @pl.when(count > 0)
    def _():
        here = pl.ds(pl.multiple_of(step_id * BLK, BLK), BLK)
        for g in range(groups):
            q4_ref[g] = head_stack(q_ref[:, lanes_of(g)], True, jnp.asarray(0.125, BF))
            do4_ref[g] = head_stack(do_all[here, lanes_of(g)], False)
        ident_q = idq_ref[pl.ds(j, 1), :]

        def step(c, _):
            at, seen = key_span(idk_ref, ident_q, start, c, SPAN_BACK, blocks)
            for g in range(groups):
                s = dot_nt(k_ref[at, lanes_of(g)], q4_ref[g])
                dp = dot_nt(v_ref[at, lanes_of(g)], do4_ref[g])
                lse = stat_ref[0, g, pl.ds(step_id, 1), :]
                delta = stat_ref[1, g, pl.ds(step_id, 1), :]
                low_p, low_ds = score_gradients(s, dp, lse, delta, seen)
                dk_ref[at, lanes_of(g)] += dot(low_ds, q4_ref[g])
                dv_ref[at, lanes_of(g)] += dot(low_p, do4_ref[g])
            return 0

        lax.fori_loop(0, count, step, 0)


def backward_halo_call(bounds, q_win, pieces, k_win, v_win, idk, idq, dk, dv, first):
    own, width = dk.shape
    groups = width // 256
    side, blocks = first // BLK, own // BLK
    inside = lambda w: pl.BlockSpec(
        (pl.Element(own), pl.Element(w)), lambda i: (pl.multiple_of(first + 0 * i, BLK), 0)
    )
    outside = pl.BlockSpec((BLK, width), lambda i: (jnp.where(i < side, i, i + blocks), 0))
    return pl.pallas_call(
        functools.partial(backward_halo_kernel, first=first),
        grid=(2 * side,),
        in_specs=[SMEM, outside]
        + [whole(p.shape) for p in pieces]
        + [inside(width)] * 2
        + [inside(idk.shape[1]), whole(idq.shape)]
        + [whole((own, width))] * 2,
        out_specs=[whole((own, width))] * 2,
        out_shape=[jax.ShapeDtypeStruct((own, width), F32)] * 2,
        scratch_shapes=[
            pltpu.VMEM((groups, GROUP * BLK, 256), BF),
            pltpu.VMEM((2 * first, width), BF),
            pltpu.VMEM((groups, GROUP * BLK, 256), BF),
            pltpu.VMEM((2, groups, 16, GROUP * BLK), F32),
        ],
        compiler_params=params(),
        cost_estimate=cost(11),
        name="attention_backward_halo",
    )(bounds, q_win, *pieces, k_win, v_win, idk, idq, dk, dv)


def norm_parts(x):
    centred = x - jnp.mean(x, -1, keepdims=True)
    inverse = lax.rsqrt(jnp.mean(centred * centred, -1, keepdims=True) + EPS)
    return centred * inverse, inverse


def norm_back(grad, xhat, inverse, gain):
    scaled = grad * gain
    return inverse * (
        scaled
        - jnp.mean(scaled, -1, keepdims=True)
        - xhat * jnp.mean(scaled * xhat, -1, keepdims=True)
    )


def columns_sum(x):
    return jnp.sum(x, 0, keepdims=True)


def chip_order(ab, core):
    return jnp.where(core == 0, ab, ab % 2 * 2 + ab // 2)


def slices_out(place, source, keep, away, lead, sem, slices, rows):
    for n in range(slices):
        rel = place ^ n
        for target, odd in ((keep, 0), (away, 1)):
            core = place % 2 ^ odd

            @pl.when(rel % 2 == odd)
            def _():
                pltpu.make_async_copy(
                    source.at[n * rows : (n + 1) * rows, :],
                    target.at[chip_order(rel // 2, core), pl.ds(lead, rows), :],
                    sem.at[n],
                ).start()


def gathered(place, refs):
    for far in range(2):
        for n in range(4):
            rel = 2 * chip_order(jnp.int32(n), place % 2 ^ far) + far
            yield refs[4 * far + n], place ^ rel


def slices_wait(source, keep, sem, slices, rows):
    for n in range(slices):
        pltpu.make_async_copy(
            source.at[n * rows : (n + 1) * rows, :], keep.at[0, 0:rows, :], sem.at[n]
        ).wait()


def one_quarter(q, w_all, norm_ref, dy_ref, bu_ref, dbu_ref, out_acc, dn_acc, g_all, fresh):
    own, width = norm_ref.shape
    tile = 256
    for t in range((w_all.shape[1] - width) // tile):
        cols = slice(tile * t, tile * t + tile)
        down = slice(width + tile * t, width + tile * t + tile)
        norm, dy = norm_ref[...], dy_ref[...]
        up_w = w_all[q, :width, cols]
        down_w = w_all[q, down, :]
        pre = dot(norm, up_w) + bu_ref[pl.ds(q, 1), cols]
        cdf = 0.5 * (1.0 + lax.erf(pre * np.float32(0.7071067811865476)))
        density = jnp.exp(-0.5 * pre * pre) * np.float32(0.3989422804014327)
        act = (pre * cdf).astype(BF)
        d_pre = (dot_nt(dy, down_w) * (cdf + pre * density)).astype(BF)
        dbu_ref[pl.ds(q, 1), cols] = columns_sum(d_pre.astype(F32))
        if fresh and t == 0:
            out_acc[...] = dot(act, down_w)
            dn_acc[...] = dot_nt(d_pre, up_w)
        else:
            out_acc[...] += dot(act, down_w)
            dn_acc[...] += dot_nt(d_pre, up_w)
        g_all[q, :width, cols] = dot_tn(norm, d_pre).astype(BF)
        g_all[q, down, :] = dot_tn(act, dy).astype(BF)


def middle_own_kernel(
    place_ref, x_ref, low_ref, wo_ref, vec_ref, dy_ref, bu_ref, up_ref, down_ref,
    hid_ref, norm_ref, out_ref, dn_ref, dbu_ref, keep_ref, send_ref, w_all, g_all, w_sem, g_sem,
    *, slices,
):
    width = x_ref.shape[1]
    rows = w_all.shape[1] // slices
    copies = [
        pltpu.make_async_copy(up_ref, w_all.at[0, :width, :], w_sem.at[0]),
        pltpu.make_async_copy(down_ref, w_all.at[0, width:, :], w_sem.at[1]),
    ]
    for copy in copies:
        copy.start()
    hidden_in = x_ref[...].astype(F32) + dot(low_ref[...], wo_ref[...]) + vec_ref[B_OUT]
    hid_ref[...] = hidden_in
    norm_ref[...] = layer_norm_low(hidden_in, vec_ref[LN2_GAIN], vec_ref[LN2_SHIFT])
    for copy in copies:
        copy.wait()
    one_quarter(0, w_all, norm_ref, dy_ref, bu_ref, dbu_ref, out_ref, dn_ref, g_all, True)
    slices_out(place_ref[0], g_all.at[0], keep_ref, send_ref, 0, g_sem, slices, rows)
    slices_wait(g_all.at[0], keep_ref, g_sem, slices, rows)


def middle_own_call(place, x, low, w_out, vectors, dy, b_up, w_up, w_down, slices):
    own, width = x.shape
    hidden = b_up.shape[1]
    rows = width + hidden
    vmem = pl.BlockSpec(memory_space=pltpu.VMEM)
    sds = jax.ShapeDtypeStruct
    return pl.pallas_call(
        functools.partial(middle_own_kernel, slices=slices),
        in_specs=[SMEM] + [vmem] * 6 + [ANY] * 2,
        out_specs=[vmem] * 5 + [ANY] * 2,
        out_shape=[
            sds((own, width), F32),
            sds((own, width), BF),
            sds((own, width), F32),
            sds((own, width), F32),
            sds((1, hidden), F32),
        ]
        + [sds((slices // 2, rows // slices, width), BF)] * 2,
        scratch_shapes=[
            pltpu.VMEM((1, rows, width), BF),
            pltpu.VMEM((1, rows, width), BF),
            pltpu.SemaphoreType.DMA((2,)),
            pltpu.SemaphoreType.DMA((slices,)),
        ],
        compiler_params=params(),
        cost_estimate=cost(12),
        name="middle_own",
    )(place, x, low, w_out, vectors, dy, b_up, w_up, w_down)


def other_quarters(
    place, piece_refs, base, w_all, w_sem, norm_ref, dy_ref, bu_ref, dbu_ref, out_acc, dn_acc,
    g_all, g_sem, keep_ref, send_ref, slices,
):
    rows = w_all.shape[1] // slices

    def fetches(q):
        return [
            pltpu.make_async_copy(
                ref.at[base + q],
                w_all.at[q, pl.ds(pl.multiple_of(source * rows, rows), rows), :],
                w_sem.at[q, n],
            )
            for n, (ref, source) in enumerate(gathered(place, piece_refs))
        ]

    for q in range(w_all.shape[0]):
        for copy in fetches(q):
            copy.start()

    def quarter(q, _):
        for copy in fetches(q):
            copy.wait()
        one_quarter(q, w_all, norm_ref, dy_ref, bu_ref, dbu_ref, out_acc, dn_acc, g_all, False)
        slices_out(
            place, g_all.at[q], keep_ref, send_ref, pl.multiple_of(q * rows, rows), g_sem.at[q],
            slices, rows,
        )
        return 0

    lax.fori_loop(0, w_all.shape[0], quarter, 0)


def middle_next_kernel(place_ref, norm_ref, out_in, dn_in, dy_ref, bu_ref, *refs, slices, base):
    piece_refs = refs[:slices]
    out_ref, dn_ref, dbu_ref, keep_ref, send_ref, w_all, g_all, w_sem, g_sem = refs[slices:]
    out_ref[...] = out_in[...]
    dn_ref[...] = dn_in[...]
    other_quarters(
        place_ref[0], piece_refs, base, w_all, w_sem, norm_ref, dy_ref, bu_ref, dbu_ref, out_ref,
        dn_ref, g_all, g_sem, keep_ref, send_ref, slices,
    )
    rows = w_all.shape[1] // slices
    for q in range(w_all.shape[0]):
        slices_wait(g_all.at[q], keep_ref, g_sem.at[q], slices, rows)


def middle_next_call(place, norm, out, dn, dy, b_up, pieces, slices, base):
    own, width = norm.shape
    quarters, hidden = b_up.shape
    rows = width + hidden
    vmem = pl.BlockSpec(memory_space=pltpu.VMEM)
    sds = jax.ShapeDtypeStruct
    return pl.pallas_call(
        functools.partial(middle_next_kernel, slices=slices, base=base),
        in_specs=[SMEM] + [vmem] * 5 + [ANY] * len(pieces),
        out_specs=[vmem] * 3 + [ANY] * 2,
        out_shape=[sds((own, width), F32), sds((own, width), F32), sds((quarters, hidden), F32)]
        + [sds((slices // 2, quarters * rows // slices, width), BF)] * 2,
        scratch_shapes=[
            pltpu.VMEM((quarters, rows, width), BF),
            pltpu.VMEM((quarters, rows, width), BF),
            pltpu.SemaphoreType.DMA((quarters, slices)),
            pltpu.SemaphoreType.DMA((quarters, slices)),
        ],
        compiler_params=params(),
        cost_estimate=cost(8 * quarters),
        name="middle_next",
    )(place, norm, out, dn, dy, b_up, *pieces)


def middle_last_kernel(
    place_ref, hid_ref, norm_ref, out_in, dn_in, low_ref, mixed_ref, wo_ref, vec_ref, dy_ref,
    bu_ref, lse_ref, *refs, slices, base,
):
    piece_refs = refs[:slices]
    (
        act_ref, dh_ref, dheads_ref, head_ref, tail_ref, delta_ref, small_ref, dbu_ref,
        keep_ref, send_ref, w_all, g_all, go_all, out_acc, dn_acc, w_sem, g_sem,
    ) = refs[slices:]
    place = place_ref[0]
    own, width = norm_ref.shape
    quarters = w_all.shape[0]
    rows = w_all.shape[1] // slices
    out_acc[...] = out_in[...]
    dn_acc[...] = dn_in[...]
    other_quarters(
        place, piece_refs, base, w_all, w_sem, norm_ref, dy_ref, bu_ref, dbu_ref, out_acc, dn_acc,
        g_all, g_sem, keep_ref, send_ref, slices,
    )

    hidden_in = hid_ref[...]
    act_ref[...] = (hidden_in + out_acc[...] + vec_ref[B_DOWN]).astype(BF)
    xhat, inverse = norm_parts(hidden_in)
    dn = dn_acc[...]
    dy = dy_ref[...].astype(F32)
    d_hidden = dy + norm_back(dn, xhat, inverse, vec_ref[LN2_GAIN])
    dh_ref[...] = d_hidden
    d_att = d_hidden.astype(BF)
    small_ref[0:1, :] = columns_sum(dn * xhat)
    small_ref[1:2, :] = columns_sum(dn)
    small_ref[2:3, :] = columns_sum(dy)
    small_ref[3:4, :] = columns_sum(d_att.astype(F32))
    d_heads = dot_nt(d_att, wo_ref[...]).astype(BF)
    dheads_ref[:own, :] = d_heads
    spread = d_heads.astype(F32) * mixed_ref[...]
    pick = lax.broadcasted_iota(jnp.int32, (8, 256), 0)
    pick = (pick == lax.broadcasted_iota(jnp.int32, (8, 256), 1) // 64).astype(F32)
    for g in range(width // 256):
        for i in range(own // BLK):
            block = spread[BLK * i : BLK * i + BLK, 256 * g : 256 * g + 256]
            sums = lax.dot_general(
                pick, block, (((1,), (1,)), ((), ())),
                preferred_element_type=F32, precision=lax.Precision.HIGHEST,
            )
            delta = jnp.concatenate([sums[h : h + 1, :] for h in range(GROUP)], 1)
            delta_ref[g, i] = delta
            lse = lse_ref[g, i]
            left = jnp.concatenate(
                [lse[:, :256], lse[:, 256:], delta[:, :256], delta[:, 256:]], 0
            )
            parts = []
            for _ in range(3):
                parts.append(left.astype(BF))
                left = left - parts[-1].astype(F32)
            parts = jnp.concatenate(parts, 0)
            at = slice(256 * g, 256 * g + 256)
            lo = own + 2 * STAT_ROWS * i
            dheads_ref[lo : lo + 2 * STAT_ROWS, at] = parts
            for target, row in ((head_ref, 0), (tail_ref, own // BLK - 1)):
                if i == row:
                    target[REACH : REACH + 2 * STAT_ROWS, at] = parts
    blank = jnp.zeros((STAT_PAD - 2 * STAT_ROWS, width), BF)
    head_ref[REACH + 2 * STAT_ROWS :, :] = blank
    tail_ref[REACH + 2 * STAT_ROWS :, :] = blank
    head_ref[:REACH, :] = d_heads[:REACH, :]
    tail_ref[:REACH, :] = d_heads[own - REACH :, :]
    go_all[...] = dot_tn(low_ref[...], d_att).astype(BF)
    few = width // slices
    slices_out(place, go_all, keep_ref, send_ref, quarters * rows, g_sem.at[quarters], slices, few)
    for q in range(quarters):
        slices_wait(g_all.at[q], keep_ref, g_sem.at[q], slices, rows)
    slices_wait(go_all, keep_ref, g_sem.at[quarters], slices, few)


def middle_last_call(
    place, hidden_in, norm, out, dn, low, mixed, w_out, vectors, dy, b_up, lse, pieces, slices,
    base,
):
    own, width = norm.shape
    quarters, hidden = b_up.shape
    rows = width + hidden
    vmem = pl.BlockSpec(memory_space=pltpu.VMEM)
    sds = jax.ShapeDtypeStruct
    grads = sds((slices // 2, (quarters * rows + width) // slices, width), BF)
    return pl.pallas_call(
        functools.partial(middle_last_kernel, slices=slices, base=base),
        in_specs=[SMEM] + [vmem] * 11 + [ANY] * len(pieces),
        out_specs=[vmem] * 8 + [ANY] * 2,
        out_shape=[
            sds((own, width), BF),
            sds((own, width), F32),
            sds((own + own // BLK * 2 * STAT_ROWS, width), BF),
            sds((REACH + STAT_PAD, width), BF),
            sds((REACH + STAT_PAD, width), BF),
            sds((width // 256, own // BLK, 1, GROUP * BLK), F32),
            sds((4, width), F32),
            sds((quarters, hidden), F32),
            grads,
            grads,
        ],
        scratch_shapes=[
            pltpu.VMEM((quarters, rows, width), BF),
            pltpu.VMEM((quarters, rows, width), BF),
            pltpu.VMEM((width, width), BF),
            pltpu.VMEM((own, width), F32),
            pltpu.VMEM((own, width), F32),
            pltpu.SemaphoreType.DMA((quarters, slices)),
            pltpu.SemaphoreType.DMA((quarters + 1, slices)),
        ],
        compiler_params=params(),
        cost_estimate=cost(12),
        name="middle_last",
    )(place, hidden_in, norm, out, dn, low, mixed, w_out, vectors, dy, b_up, lse, *pieces)


def turn_back_kernel(
    place_ref, x_ref, vec_ref, dq_ref, dk_ref, dv_ref, q_ref, k_ref, hot_ref, table_ref, grid_ref,
    back_ref, d_ref, db_ref, freq_ref, keep_ref, send_ref, norm_ref, g_all, sem, *, slices,
):
    width = x_ref.shape[1]
    group = pl.program_id(0)

    @pl.when(group == 0)
    def _():
        norm_ref[...] = layer_norm_low(
            x_ref[...].astype(F32), vec_ref[LN1_GAIN], vec_ref[LN1_SHIFT]
        )

    c, s = cos_sin(hot_ref[...], table_ref[...])
    norm = norm_ref[...]

    def gradient(n, low):
        d_ref[n] = low
        db_ref[n : n + 1, :] = columns_sum(low.astype(F32))
        at = pl.ds(pl.multiple_of(n * width + group * 256, 256), 256)
        g_all[:, at] = dot_tn(norm, low).astype(BF)

    d_angle = 0.0
    for n, (grad, turned_ref) in enumerate(((dq_ref, q_ref), (dk_ref, k_ref))):
        g1, g2 = grad[:, :128], grad[:, 128:]
        d_angle = d_angle + (g2 * turned_ref[:, :128] - g1 * turned_ref[:, 128:])
        back = jnp.concatenate([g1 * c + g2 * s, g2 * c - g1 * s], 1).astype(BF)
        gradient(n, dot(back, back_ref[...]).astype(BF))
    freq_ref[...] = lax.dot_general(
        grid_ref[...], d_angle, (((1,), (0,)), ((), ())),
        preferred_element_type=F32, precision=lax.Precision.HIGHEST,
    )
    gradient(2, dv_ref[...].astype(BF))

    @pl.when(group == width // 256 - 1)
    def _():
        slices_out(place_ref[0], g_all, keep_ref, send_ref, 0, sem, slices, width // slices)
        slices_wait(g_all, keep_ref, sem, slices, width // slices)


def turn_back_call(
    place, x, vectors, dq, dk, dv, q_exact, k_exact, onehot, table, grid8, back, first, slices
):
    rows, width = dk.shape
    sds = jax.ShapeDtypeStruct
    part = pl.BlockSpec((rows, 256), lambda g: (0, g))
    hot = pl.BlockSpec(
        (pl.Element(rows), pl.Element(onehot.shape[1])),
        lambda g: (pl.multiple_of(first + 0 * g, BLK), 0),
    )
    return pl.pallas_call(
        functools.partial(turn_back_kernel, slices=slices),
        grid=(width // 256,),
        in_specs=[SMEM, whole(x.shape), whole(vectors.shape)]
        + [part] * 5
        + [
            hot,
            pl.BlockSpec((table.shape[0], 512), lambda g: (0, g)),
            whole(grid8.shape),
            whole(back.shape),
        ],
        out_specs=[
            pl.BlockSpec((3, rows, 256), lambda g: (0, 0, g)),
            pl.BlockSpec((3, 256), lambda g: (0, g)),
            pl.BlockSpec((8, 128), lambda g: (0, g)),
        ]
        + [ANY] * 2,
        out_shape=[
            sds((3, rows, width), BF),
            sds((3, width), F32),
            sds((8, width // 2), F32),
        ]
        + [sds((slices // 2, width // slices, 3 * width), BF)] * 2,
        scratch_shapes=[
            pltpu.VMEM((rows, width), BF),
            pltpu.VMEM((width, 3 * width), BF),
            pltpu.SemaphoreType.DMA((slices,)),
        ],
        compiler_params=params(),
        cost_estimate=cost(9),
        name="turn_back",
    )(place, x, vectors, dq, dk, dv, q_exact, k_exact, onehot, table, grid8, back)


def input_grad_kernel(x_ref, vec_ref, d_ref, w_ref, dh_ref, out_ref, small_ref):
    width = x_ref.shape[1]
    d_norm = sum(dot_nt(d_ref[n], w_ref[:, lanes_of(n, width)]) for n in range(3))
    xhat, inverse = norm_parts(x_ref[...].astype(F32))
    small_ref[0:1, :] = columns_sum(d_norm * xhat)
    small_ref[1:2, :] = columns_sum(d_norm)
    out_ref[...] = dh_ref[...] + norm_back(d_norm, xhat, inverse, vec_ref[LN1_GAIN])


def input_grad_call(x, vectors, d_qkv, weight, d_hidden):
    rows, width = x.shape
    return pl.pallas_call(
        input_grad_kernel,
        out_shape=[
            jax.ShapeDtypeStruct((rows, width), F32),
            jax.ShapeDtypeStruct((2, width), F32),
        ],
        compiler_params=params(),
        cost_estimate=cost(7),
        name="input_grad",
    )(x, vectors, d_qkv, weight, d_hidden)


def assemble_kernel(place_ref, *refs, split, outs):
    out_refs, (held, sem) = refs[4 : 4 + outs], refs[4 + outs :]
    pairs = refs[:4]
    piece_refs = [pairs[n // 2].at[n % 2] for n in range(8)]
    place, depth = place_ref[0], place_ref[1]
    slot = pl.program_id(0)

    def copy(ref, target):
        return pltpu.make_async_copy(ref, held.at[target], sem.at[target])

    @pl.when(slot == 0)
    def _():
        for ref, source in gathered(place, piece_refs):
            copy(ref, source).start()

    copy(piece_refs[0], slot).wait()
    rows = held.shape[-2]
    out_refs, squares = out_refs[:-1], out_refs[-1]

    @pl.when(slot == 0)
    def _():
        squares[...] = jnp.zeros_like(squares)

    def add_squares(block):
        total = fold8(block * block, jnp.sum)
        squares[...] += sum(total[:, lanes_of(n, 128)] for n in range(block.shape[1] // 128))

    if split:
        for n in range(split):
            block = held[slot, (depth - n + split) % split].astype(F32)
            add_squares(block)
            lo = 0
            for ref in out_refs:
                ref[n * rows : n * rows + rows, :] = block[:, lo : lo + ref.shape[1]]
                lo += ref.shape[1]
    else:
        block = held[slot].astype(F32)
        add_squares(block)
        each = held.shape[0] // len(out_refs)
        for n, ref in enumerate(out_refs):

            @pl.when(slot // each == n)
            def _():
                ref[...] = block


def assemble_call(place, arrays, shapes, split):
    pieces = 8
    rows = arrays[0].shape[-2] * max(split, 1)
    each = pieces if split else pieces // len(shapes)

    def spec(n, shape):
        lead = 0 if split else n * each
        return pl.BlockSpec((rows, shape[1]), lambda i: (jnp.clip(i - lead, 0, each - 1), 0))

    specs = [spec(n, shape) for n, shape in enumerate(shapes)] + [whole((8, 128))]
    shapes = shapes + [(8, 128)]
    return pl.pallas_call(
        functools.partial(assemble_kernel, split=split, outs=len(shapes)),
        grid=(pieces,),
        in_specs=[SMEM] + [ANY] * len(arrays),
        out_specs=specs,
        out_shape=[jax.ShapeDtypeStruct(s, F32) for s in shapes],
        scratch_shapes=[
            pltpu.VMEM((pieces,) + arrays[0].shape[1:], BF),
            pltpu.SemaphoreType.DMA((pieces,)),
        ],
        compiler_params=params(),
        cost_estimate=cost(6),
        name="assemble",
    )(place, *arrays)


def send(x, axis, pairs):
    return lax.ppermute(x, axis, pairs)


def plane_gather(piece):
    pair = jnp.stack([piece, send(piece, PLANE, FIRST)])
    return pair, send(pair, PLANE, SECOND)


def core_gather(pair, last):
    return [pair, last, send(pair, "c", SWAP), send(last, "c", SWAP)]


def wide_sum(x, extra):
    return lax.psum(x, "e") if extra > 1 else x


def sum_low(*terms):
    return functools.reduce(lambda x, y: x + y, [t.astype(F32) for t in terms])


def chip_sums(kept, far):
    total = [
        jnp.concatenate([sum_low(x[n], y[n]) for x, y in zip(kept, far)], 0).astype(BF)
        for n in range(4)
    ]
    return jnp.stack([total[1], total[3]]), (total[0], total[2])


def after(x, *others):
    return lax.optimization_barrier((x, others))[0]


def ring(size, step):
    return [(i, (i + step) % size) for i in range(size)]


def add_from(vector, axis, reach=0, size=2):
    return vector + send(vector, axis, [(i, i ^ (reach or 1)) for i in range(size)])


def on_device(
    tokens,
    segment,
    padding,
    coords,
    ln1_gain,
    ln1_shift,
    query_key_value_weight,
    b_qkv,
    output_weight,
    b_out,
    rope_freqs,
    ln2_gain,
    ln2_shift,
    w_up,
    b_up,
    w_down,
    b_down,
    cotangent,
    *,
    extra,
    depth,
):
    tokens, cotangent = tokens[0], cotangent[0]
    own, width = tokens.shape
    length = own * depth
    heads = rope_freqs.shape[1]
    half = width // heads // 2
    groups = heads // GROUP
    slices = 8
    outer = BLK
    side = own + outer
    win = own + 2 * side
    blocks = own // BLK
    z = lax.axis_index("n")
    plane = lax.axis_index("a") * 4 + lax.axis_index("b") * 2 + lax.axis_index("c")
    place = jnp.stack([plane, z]).astype(jnp.int32)
    up = [(i, i + 1) for i in range(depth - 1)]
    down = [(i + 1, i) for i in range(depth - 1)]
    up2 = [(i, i + 2) for i in range(depth - 2)]
    down2 = [(i + 2, i) for i in range(depth - 2)]

    def around(x, head, tail):
        before2 = send(tail, "n", up2)
        before = send(x, "n", up)
        after_ = send(x, "n", down)
        after2 = send(head, "n", down2)
        return [before2, before, after_, after2]

    position = jnp.arange(length, dtype=jnp.int32)
    ident = jnp.where(padding[0] == 0, segment[0], 1000 + position)
    ident = jnp.concatenate(
        [jnp.full((side,), -1, jnp.int32), ident, jnp.full((side,), 1 << 20, jnp.int32)]
    )
    ident_win = lax.dynamic_slice_in_dim(ident, z * own, win, 0)
    near = lax.broadcasted_iota(jnp.int32, (win,), 0)
    ident_win = jnp.where(near < outer - REACH, -1, ident_win)
    ident_win = jnp.where(near >= win - outer + REACH, 1 << 20, ident_win)
    idk = jnp.broadcast_to(ident_win[:, None], (win, BLK))
    idq = ident_win.reshape(win // BLK, BLK)

    lowest, highest = idq[:, 0], idq[:, BLK - 1]

    def bounds(queries, keys):
        before = highest[keys][None, :] < lowest[queries][:, None]
        reached = lowest[keys][None, :] <= highest[queries][:, None]
        return jnp.sum(before, 1), jnp.sum(reached, 1)

    def steps(blocks, span):
        return (jnp.maximum(blocks, 0) + span - 1) // span

    mid = slice(side // BLK, side // BLK + blocks)
    lo, hi = bounds(mid, slice(None))
    bounds_fwd = [
        lo, steps(hi - lo, SPAN), jnp.minimum(lo, mid.start), steps(mid.start - lo, SPAN_SIDE),
        steps(hi - mid.stop, SPAN_SIDE),
    ]
    bounds_fwd = jnp.stack(bounds_fwd, 1).astype(jnp.int32)
    lo, hi = bounds(slice(None), mid)
    bounds_bwd = jnp.stack([lo, steps(hi - lo, SPAN_BACK)], 1).astype(jnp.int32)

    grid = jnp.pad(coords[:, 0], ((0, 0), (side, side)))
    grid_win = lax.dynamic_slice_in_dim(grid, z * own, win, 1)
    grid_own = lax.dynamic_slice_in_dim(grid, z * own + side, own, 1)
    lane = jnp.arange(4 * SIDE)
    picked = jnp.where(lane[None, :] < 2 * SIDE, grid_win[0][:, None], grid_win[1][:, None])
    onehot = (picked == (lane % SIDE)[None, :]).astype(BF)
    table = turn_table(rope_freqs)

    local = np.arange(256)
    order = np.zeros((256, 256), np.float32)
    order[(local % 128) // 32 * 64 + local // 128 * 32 + local % 32, local] = 1.0
    order = jnp.asarray(order, BF)
    qk_bias = b_qkv[: 2 * width].reshape(2 * groups, GROUP, 2, half).swapaxes(1, 2)
    bias_turned = jnp.concatenate([qk_bias.reshape(-1), b_qkv[2 * width :]])

    x_parts = around(tokens, tokens[:REACH], tokens[own - REACH :])
    vectors = jnp.stack([ln1_gain, ln1_shift, b_out, ln2_gain, ln2_shift, b_down])
    rot_q, rot_k, values, q_exact, k_exact, weight_turned = qkv_own_call(
        tokens, onehot, vectors, query_key_value_weight, bias_turned, order, table, side
    )

    rows = (width + w_down.shape[0]) // slices
    eighth = jnp.where(
        plane < width // rows,
        lax.dynamic_slice_in_dim(w_up, jnp.minimum(plane * rows, width - rows), rows, 0),
        lax.dynamic_slice_in_dim(w_down, jnp.maximum(plane * rows - width, 0), rows, 0),
    )
    left, bias_rows = b_up, []
    for _ in range(3):
        bias_rows.append(left.astype(BF))
        left = left - rounded(left)
    bias_rows = jnp.pad(jnp.stack(bias_rows), ((0, 13), (0, 0)))
    eighth = jnp.concatenate([eighth, bias_rows], 0)
    others = [send(eighth, "n", ring(depth, k)) for k in range(1, depth)]
    x_parts, rot_q = lax.optimization_barrier((x_parts, rot_q))
    rot_q, rot_k, values = qkv_halo_call(
        x_parts, onehot, vectors, weight_turned, bias_turned, table, rot_q, rot_k, values, side
    )
    part = forward_call(bounds_fwd, rot_q, rot_k, values, idk, idq, side, own, 0, blocks // 2)
    others, part = lax.optimization_barrier((others, part))
    up_biases = jnp.concatenate(
        [jnp.sum(x[rows : rows + 3].astype(F32), 0, keepdims=True) for x in others]
    )
    own_w = jnp.stack([x[:rows] for x in others])
    over_1, over_2 = send(own_w, PLANE, FIRST), send(own_w, PLANE, SECOND)
    part, _ = lax.optimization_barrier((part, own_w))
    mixed, mixed_low, lse = forward_call(
        bounds_fwd, rot_q, rot_k, values, idk, idq, side, own, blocks // 2, blocks // 2, part
    )
    hidden_in, norm2, out0, dn0, up_sum0, kept_own, sent_own = middle_own_call(
        place, tokens, mixed_low, output_weight, vectors, cotangent, b_up[None],
        w_up, w_down, slices,
    )
    over_1, over_2, norm2 = lax.optimization_barrier((over_1, over_2, norm2))
    diagonal = send(over_1, PLANE, SECOND)
    far_own = send(after(sent_own, over_1, over_2), "c", SWAP)
    near = [own_w, over_1, over_2, diagonal]
    pieces = near + [send(x, "c", SWAP) for x in near]
    norm2 = after(norm2, far_own)
    split = depth - 2
    out1, dn1, up_sum1, kept_next, sent_next = middle_next_call(
        place, norm2, out0, dn0, cotangent, up_biases[:split], pieces, slices, 0
    )
    far_next = send(sent_next, "c", SWAP)
    (
        activations, d_hidden, d_heads, d_head, d_tail, delta, small_mid, up_sum2, kept_last,
        sent_last,
    ) = middle_last_call(
        place, hidden_in, norm2, out1, dn1, mixed_low, mixed, output_weight, vectors, cotangent,
        up_biases[split:], lse, pieces, slices, split,
    )
    up_sums = (up_sum0, up_sum1, up_sum2)
    far_next, d_heads = lax.optimization_barrier((far_next, d_heads))
    away_a, rest_a = chip_sums((kept_own, kept_next), (far_own, far_next))
    got_1a = send(away_a, PLANE, FIRST)
    far_last = send(sent_last, "c", SWAP)
    do_parts = around(d_heads, d_head, d_tail)

    dq, dk, dv = backward_own_call(
        bounds_fwd, rot_q, d_heads, rot_k, values, idk, idq, lse, delta, side, own
    )
    got_1a, far_last, dq = lax.optimization_barrier((got_1a, far_last, dq))
    away_a = sum_low(rest_a[1], got_1a[1]).astype(BF)
    got_2a = send(away_a, PLANE, SECOND)
    away_b, rest_b = chip_sums((kept_last,), (far_last,))
    got_1b = send(away_b, PLANE, FIRST)
    do_parts, dq, dk, _ = lax.optimization_barrier((do_parts, dq, dk, (away_a, away_b)))
    dk, dv = backward_halo_call(
        bounds_bwd, rot_q, do_parts, rot_k, values, idk, idq, dk, dv, side
    )
    got_1b, got_2a, dk = lax.optimization_barrier((got_1b, got_2a, dk))
    away_b = sum_low(rest_b[1], got_1b[1]).astype(BF)
    got_2b = send(away_b, PLANE, SECOND)

    def part_a(k):
        at = slice(k * rows, k * rows + rows)
        return wide_sum(sum_low(rest_a[0][at], got_1a[0, at], got_2a[at]), extra)

    ff_sent = [part_a(k).astype(BF) for k in range(1, depth - 1)]
    ff_got = [send(ff_sent[k - 1], "n", ring(depth, -k)) for k in range(1, depth - 1)]
    dk = after(dk, away_b, ff_sent)

    grid8 = jnp.pad(grid_own.astype(F32), ((0, 6), (0, 0)))
    d_qkv, grad_b_qkv, freqs8, kept_qkv, sent_qkv = turn_back_call(
        place, tokens, vectors, dq, dk, dv, q_exact, k_exact, onehot, table, grid8,
        order.T, side, slices,
    )
    far_qkv = send(sent_qkv, "c", SWAP)
    got_2b, far_qkv, d_qkv = lax.optimization_barrier((got_2b, far_qkv, d_qkv))
    away, rest_qkv = chip_sums((kept_qkv,), (far_qkv,))
    got_1_qkv = send(away, PLANE, FIRST)

    def part_b(lo, hi):
        at = slice(lo, hi)
        return wide_sum(sum_low(rest_b[0][at], got_1b[0, at], got_2b[at]), extra)

    got_2b = after(got_2b, away)
    ff_sent = part_b(0, rows).astype(BF)
    ff_got.append(send(ff_sent, "n", ring(depth, 1 - depth)))
    input_grad, small_in = input_grad_call(
        tokens, vectors, after(d_qkv, away, ff_sent), query_key_value_weight, d_hidden
    )
    got_1_qkv, small_in = lax.optimization_barrier((got_1_qkv, small_in))
    away = sum_low(rest_qkv[1], got_1_qkv[1]).astype(BF)
    got_2_qkv = send(away, PLANE, SECOND)
    ff_got, small_in, _ = lax.optimization_barrier((ff_got, small_in, away))
    ff_total = part_a(0) + sum_low(*ff_got)
    plane_qkv = wide_sum(sum_low(rest_qkv[0], got_1_qkv[0], got_2_qkv), extra)

    slot = (z - jnp.arange(depth)) % depth
    quarter_sums = jnp.take(jnp.concatenate(up_sums), slot, axis=0)
    named = [
        small_in[0], small_in[1], grad_b_qkv.reshape(-1), small_mid[3], freqs8[:2].reshape(-1),
        small_mid[0], small_mid[1], small_mid[2], quarter_sums.reshape(-1),
    ]
    small = add_from(jnp.concatenate(named).reshape(-1, 128), "c")

    part = jnp.concatenate([plane_qkv, part_b(rows, rows + width // slices)], 1).astype(BF)
    thin = part.shape[0] // depth
    cut = lambda k: lax.dynamic_slice_in_dim(part, ((z + k) % depth) * thin, thin, 0)
    got = [send(cut(k), "n", ring(depth, k)) for k in range(1, depth)]
    small = add_from(add_from(after(small, part), "b"), "a")
    if extra > 1:
        small = lax.psum(small, "e")
    got, small = lax.optimization_barrier((got, small))
    low = sum_low(cut(0), *got).astype(BF)
    strip = jnp.stack([low] + [send(low, "n", ring(depth, k)) for k in range(1, depth)])
    ff_pair, ff_last = plane_gather(after(ff_total, low).astype(BF))
    pair, last = plane_gather(strip)
    ff_pieces = [after(x, strip) for x in core_gather(ff_pair, ff_last)]
    total_w_up, total_w_down, ff_squares = assemble_call(
        place, ff_pieces, [w_up.shape, w_down.shape], 0
    )
    small = jnp.concatenate([small, ff_squares], 0)
    reach = 1
    while reach < depth:
        small = add_from(small, "n", reach, depth)
        reach *= 2
    last, small = lax.optimization_barrier((last, small))
    total_w_qkv, total_w_out, squares = assemble_call(
        place, core_gather(pair, last), [query_key_value_weight.shape, output_weight.shape], depth
    )
    small, large_sq = small[:-8].reshape(-1), jnp.sum(small[-8:] + squares)

    out, at = [], 0
    for vector in named:
        out.append(small[at : at + vector.size])
        at += vector.size
    t_gain1, t_shift1, t_b_qkv, t_b_out, t_freqs, t_gain2, t_shift2, t_b_down, t_up = out
    t_freqs = t_freqs.reshape(rope_freqs.shape)
    rot_sq = jnp.sum(t_freqs * t_freqs)
    skip = sum(v.size for v in named[:4])
    lane = jnp.arange(small.size)
    others = (lane < skip) | (lane >= skip + freqs8.shape[1] * 2)
    other_sq = large_sq + jnp.sum(jnp.where(others, small * small, 0.0))
    t_b_up = lax.dynamic_slice_in_dim(t_up, z * b_up.shape[0], b_up.shape[0], 0)
    return (
        activations[None],
        input_grad[None],
        t_gain1,
        t_shift1,
        total_w_qkv,
        t_b_qkv,
        total_w_out,
        t_b_out,
        t_freqs,
        t_gain2,
        t_shift2,
        total_w_up,
        t_b_up,
        total_w_down,
        t_b_down,
        rot_sq,
        other_sq,
    )


def solution(mesh):
    wide, depth = mesh.shape["wide"], mesh.shape["narrow"]
    extra = wide // 8
    fine = Mesh(mesh.devices.reshape(extra, 2, 2, 2, depth), ("e", "a", "b", "c", "n"))
    w, n = ("e", "a", "b", "c"), "n"
    return jax.shard_map(
        functools.partial(on_device, extra=extra, depth=depth),
        mesh=fine,
        in_specs=(
            P(w, n, None), P(w, None), P(w, None), P(None, w, None),
            P(), P(), P(), P(), P(), P(), P(), P(), P(),
            P(None, n), P(n), P(n, None), P(), P(w, n, None),
        ),
        out_specs=(
            P(w, n, None), P(w, n, None),
            P(), P(), P(), P(), P(), P(), P(), P(), P(),
            P(None, n), P(n), P(n, None), P(), P(), P(),
        ),
        check_vma=False,
    )
```

time: 411 us -> 343 us (0.83)
  waiting for transfers between devices: 90.9 us -> 58 us
  Pallas kernels: 165 us -> 141 us
  starting transfers between devices: 96.8 us -> 83.4 us
    ppermute x66 -> x50, waiting for transfers between devices: 90.9 us -> 58 us  [send(): return lax.ppermute(x, axis, pairs)]
    pallas_call x8 -> x9, Pallas kernels: 125 us -> 102 us  [the longest x1 18 us: backward_own_call(): pl.pallas_call(functools.partial(backward_own_kernel, first=first), grid=...]
    ppermute x66 -> x50, starting transfers between devices: 96.8 us -> 83.4 us  [send(): return lax.ppermute(x, axis, pairs)]
    add x4 -> x7, other arithmetic: 0.03 us -> 4.27 us  [the longest x1 2.05 us: sum_low(): return functools.reduce(lambda x, y: x + y, [t.astype(F32) for t in terms])]
  transfers between devices with their start and end apart: 66 -> 50, of which waited for: 21 -> 14; matrix products, arithmetic and copies ran while one was open for 11% -> 12% of each run, Pallas kernels for 29% -> 32%
where the time goes in v2:
time: 343 us; the launch traced here: 337 us
  Pallas kernels  141 us (41%)
  starting transfers between devices  83.4 us (24%)
  waiting for transfers between devices  58 us (17%)
  other arithmetic  30.8 us (9%)
  local copies, waits for them, and re-layouts  18.8 us (5%)
  between operations  4.63 us (1%)
    ppermute x50, starting transfers between devices, send(): return lax.ppermute(x, axis, pairs)  83.4 us
    ppermute x50, waiting for transfers between devices, send(): return lax.ppermute(x, axis, pairs)  58 us
    pallas_call x1, Pallas kernels, backward_own_call(): pl.pallas_call(functools.partial(backward_own_kernel, first=first), grid=...  18 us
    pallas_call x2, Pallas kernels, forward_call(): pl.pallas_call(functools.partial(forward_kernel, first=first, base=base),...  16.5 us
    pallas_call x1, Pallas kernels, middle_last_call(): pl.pallas_call(functools.partial(middle_last_kernel, slices=slices, base=...  16.2 us
    pallas_call x1, Pallas kernels, middle_next_call(): pl.pallas_call(functools.partial(middle_next_kernel, slices=slices, base=...  16.1 us
    pallas_call x2, Pallas kernels, assemble_call(): pl.pallas_call(functools.partial(assemble_kernel, split=split, outs=len(s...  13.7 us
    pallas_call x1, Pallas kernels, middle_own_call(): pl.pallas_call(functools.partial(middle_own_kernel, slices=slices), in_sp...  11.9 us
  transfers between devices with their start and end apart: 50, of which 14 were waited for; matrix products, arithmetic and copies ran while one was open for 12% of the time, Pallas kernels for 32%

profile of v2, /device:TPU:1, one launch (start us, length us, event | category | flops | bytes accessed | tf_op | source)
XLA Modules:
  0.0 337.0 jit_solution(8540142630832365286)
XLA Ops:
  0.7 4.2 %collective-permute-start.1 = (bf16[512,768]{1,0:T(8,128)(2,1)}, bf16[512,768]{1,0:T(8,128)(2,1)S(1)}, u32[]{:S(2)}, u32[]{:S(2)}) collective-permute-start(bf16[512,768]{1,0:T(8,128)(2,1)} %bitcast.107), channel_id=1, source_target_pairs={{0,1},{1,2},{2,3},{4,5},{5,6},{6,7},{8,9},{9,10},{10,11},{12,13},{... | collective-permute-start | bytes 2359304 | tf_op jit(solution)/shard_map/ppermute | solution.py:1014
  7.2 5.0 %collective-permute-start = (bf16[64,768]{1,0:T(8,128)(2,1)S(1)}, bf16[64,768]{1,0:T(8,128)(2,1)S(1)}, u32[]{:S(2)}, u32[]{:S(2)}) collective-permute-start(bf16[64,768]{1,0:T(8,128)(2,1)S(1)} %get-tuple-element.353), channel_id=1, source_target_pairs={{0,2},{1,3},{4,6},{5,7},{8,10},{9,11},{12,14},{13,15},{16,18},{17,... | collective-permute-start | bytes 294920 | tf_op jit(solution)/shard_map/ppermute | solution.py:1014
  22.5 1.7 fusion.1.hot_ref
  25.5 8.6 %qkv_own.1 = (bf16[1792,768]{1,0:T(8,128)(2,1)}, bf16[1792,768]{1,0:T(8,128)(2,1)}, bf16[1792,768]{1,0:T(8,128)(2,1)}, f32[512,768]{1,0:T(8,128)}, f32[512,768]{1,0:T(8,128)}, /*index=5*/bf16[768,2304]{1,0:T(8,128)(2,1)}) custom-call(bf16[512,768]{1,0:T(8,128)(2,1)} %bitcast.109, bf16[1792,128]{1,0:T(8,128)(2,1)} %fusion.1.hot_ref, ...), custom_call_target="tpu_custom_call" | custom-call | flops 9200000000 | bytes 24000000 | tf_op jit(solution)/shard_map/qkv_own/pallas_call | solution.py:145
  34.7 3.0 collective-permute-start.5
  40.2 11.9 %qkv_halo.1 = (bf16[1792,768]{1,0:T(8,128)(2,1)}, bf16[1792,768]{1,0:T(8,128)(2,1)}, bf16[1792,768]{1,0:T(8,128)(2,1)}) custom-call(bf16[64,768]{1,0:T(8,128)(2,1)} %copy-done.53, bf16[512,768]{1,0:T(8,128)(2,1)} %copy-done.45, bf16[512,768]{1,0:T(8,128)(2,1)} %copy-done.46, ...), custom_call_target="tpu_custom_call", output_to_operand_aliasing={{0}: (9, {}), {1}: (10, {}), {2}: (11, {})} | custom-call | flops 13224999936 | bytes 34500000 | tf_op jit(solution)/shard_map/qkv_halo/pallas_call | solution.py:204
  53.3 8.0 %attention_forward.2 = (f32[512,768]{1,0:T(8,128)}, bf16[512,768]{1,0:T(8,128)(2,1)}, f32[3,4,1,512]{3,2,1,0:T(1,128)}) custom-call(s32[4,5]{1,0:T(4,128)} %stack.123.bound_ref, bf16[1792,768]{1,0:T(8,128)(2,1)} %get-tuple-element.138.q_ref, bf16[1792,768]{1,0:T(8,128)(2,1)} %get-tuple-element.139.k_ref, bf16[1792,768]{1,0:T(8,128)(2,1)} %get-tuple-element.140.v_ref, ...), custom_call_target="tpu_custom_call" | custom-call | flops 9200000000 | bytes 24000000 | tf_op jit(solution)/shard_map/attention_forward/pallas_call | solution.py:319
  64.7 8.5 %attention_forward.3 = (f32[512,768]{1,0:T(8,128)}, bf16[512,768]{1,0:T(8,128)(2,1)}, f32[3,4,1,512]{3,2,1,0:T(1,128)}) custom-call(s32[4,5]{1,0:T(4,128)} %stack.123.bound_ref, bf16[1792,768]{1,0:T(8,128)(2,1)} %get-tuple-element.138.q_ref, bf16[1792,768]{1,0:T(8,128)(2,1)} %get-tuple-element.139.k_ref, ...), custom_call_target="tpu_custom_call", output_to_operand_aliasing={{0}: (6, {}), {1}: (7, {}), {2}: (8, {})} | custom-call | flops 9200000000 | bytes 24000000 | tf_op jit(solution)/shard_map/attention_forward/pallas_call | solution.py:319
  73.2 11.9 %middle_own.1 = (f32[512,768]{1,0:T(8,128)}, bf16[512,768]{1,0:T(8,128)(2,1)}, f32[512,768]{1,0:T(8,128)}, f32[512,768]{1,0:T(8,128)}, f32[1,768]{1,0:T(1,128)},...) custom-call(s32[2]{0:T(128)} %pad_add_fusion.1.place_ref, bf16[512,768]{1,0:T(8,128)(2,1)} %bitcast.110, ...), custom_call_target="tpu_custom_call" | custom-call | flops 13799999488 | bytes 36000000 | tf_op jit(solution)/shard_map/middle_own/pallas_call | solution.py:623
  85.6 3.4 %collective-permute-start.9 = (bf16[4,192,768]{2,1,0:T(8,128)(2,1)}, bf16[4,192,768]{2,1,0:T(8,128)(2,1)}, u32[]{:S(2)}, u32[]{:S(2)}) collective-permute-start(bf16[4,192,768]{2,1,0:T(8,128)(2,1)} %get-tuple-element.160), channel_id=1, source_target_pairs={{0,4},{4,0},{1,5},{5,1},{2,6},{6,2},{3,7},{7,3},{8,12},{12,8},{9,1... | collective-permute-start | bytes 3538952 | tf_op jit(solution)/shard_map/ppermute | solution.py:1014
  89.5 8.0 %collective-permute-done.10.refs_3_ = bf16[3,192,768]{2,1,0:T(8,128)(2,1)S(1)} collective-permute-done((bf16[3,192,768]{2,1,0:T(8,128)(2,1)S(1)}, bf16[3,192,768]{2,1,0:T(8,128)(2,1)S(1)}, u32[]{:S(2)}, u32[]{:S(2)}) %collective-permute-start.10) | collective-permute-done | bytes 884768 | tf_op jit(solution)/shard_map/ppermute | solution.py:1014
  97.5 4.0 %collective-permute-start.14 = (bf16[3,192,768]{2,1,0:T(8,128)(2,1)S(1)}, bf16[3,192,768]{2,1,0:T(8,128)(2,1)S(1)}, u32[]{:S(2)}, u32[]{:S(2)}) collective-permute-start(bf16[3,192,768]{2,1,0:T(8,128)(2,1)S(1)} %collective-permute-done.10.refs_3_), channel_id=1, source_target_pairs={{0,4},{4,0},{1,5},{5,1},{2,6},{6,2},{3,7},{7,3},{8,12},{12,8},{9,1... | collective-permute-start | bytes 2654216 | tf_op jit(solution)/shard_map/ppermute | solution.py:1014
  104.6 16.1 %middle_next.1 = (f32[512,768]{1,0:T(8,128)}, f32[512,768]{1,0:T(8,128)}, f32[2,768]{1,0:T(2,128)}, bf16[4,384,768]{2,1,0:T(8,128)(2,1)}, bf16[4,384,768]{2,1,0:T(8,128)(2,1)}) custom-call(s32[2]{0:T(128)} %pad_add_fusion.1.place_ref, bf16[512,768]{1,0:T(8,128)(2,1)} %get-tuple-element.161.norm_ref, f32[512,768]{1,0:T(8,128)} %get-tuple-element.162.out_in, ...), custom_call_target="tpu_custom_call" | custom-call | flops 18400000000 | bytes 48000000 | tf_op jit(solution)/shard_map/middle_next/pallas_call | solution.py:700
  125.0 2.1 fusion.10
  127.1 16.2 %middle_last.1 = (bf16[512,768]{1,0:T(8,128)(2,1)}, f32[512,768]{1,0:T(8,128)}, bf16[560,768]{1,0:T(8,128)(2,1)}, bf16[80,768]{1,0:T(8,128)(2,1)}, bf16[80,768]{...) custom-call(s32[2]{0:T(128)} %pad_add_fusion.1.place_ref, ...), custom_call_target="tpu_custom_call" | custom-call | flops 13799999488 | bytes 36000000 | tf_op jit(solution)/shard_map/middle_last/pallas_call | solution.py:802
  143.6 2.0 collective-permute-start.20
  145.6 4.5 %collective-permute-start.21 = (bf16[560,768]{1,0:T(8,128)(2,1)}, bf16[560,768]{1,0:T(8,128)(2,1)}, u32[]{:S(2)}, u32[]{:S(2)}) collective-permute-start(bf16[560,768]{1,0:T(8,128)(2,1)} %get-tuple-element.176.do_ref), channel_id=1, source_target_pairs={{0,1},{1,2},{2,3},{4,5},{5,6},{6,7},{8,9},{9,10},{10,11},{12,13},{... | collective-permute-start | bytes 2580488 | tf_op jit(solution)/shard_map/ppermute | solution.py:1014
  152.1 1.8 collective-permute-start.16
  153.9 18.0 %attention_backward_own.1 = (f32[512,768]{1,0:T(8,128)}, f32[512,768]{1,0:T(8,128)}, f32[512,768]{1,0:T(8,128)}) custom-call(s32[4,5]{1,0:T(4,128)} %stack.123.bound_ref, bf16[1792,768]{1,0:T(8,128)(2,1)} %get-tuple-element.138.q_ref, bf16[560,768]{1,0:T(8,128)(2,1)} %get-tuple-element.176.do_ref, bf16[1792,768]{1,0:T(8,128)(2,1)} %get-tuple-element.139.k_ref, ...), custom_call_target="tpu_custom_call" | custom-call | flops 23000000512 | bytes 60000000 | tf_op jit(solution)/shard_map/attention_backward_own/pallas_call | solution.py:407
  175.2 1.5 collective-permute-start.19
  176.7 1.6 add_convert_fusion.8
  179.3 4.0 %collective-permute-start.18 = (bf16[2,288,768]{2,1,0:T(8,128)(2,1)}, bf16[2,288,768]{2,1,0:T(8,128)(2,1)S(1)}, u32[]{:S(2)}, u32[]{:S(2)}) collective-permute-start(bf16[2,288,768]{2,1,0:T(8,128)(2,1)} %pad_maximum_fusion.3), channel_id=1, source_target_pairs={{0,8},{4,20},{8,0},{12,28},{16,24},{20,4},{24,16},{28,12},{1,9},{5... | collective-permute-start | bytes 2654216 | tf_op jit(solution)/shard_map/ppermute | solution.py:1014
  183.9 10.7 %attention_backward_halo.1 = (f32[512,768]{1,0:T(8,128)}, f32[512,768]{1,0:T(8,128)}) custom-call(s32[14,2]{1,0:T(8,128)} %copy.93.bound_ref, bf16[1792,768]{1,0:T(8,128)(2,1)} %get-tuple-element.138.q_ref, bf16[80,768]{1,0:T(8,128)(2,1)} %copy-done.51, bf16[560,768]{1,0:T(8,128)(2,1)} %collective-permute-done.21.near_l, ...), custom_call_target="tpu_custom_call" | custom-call | flops 12650000384 | bytes 33000000 | tf_op jit(solution)/shard_map/attention_backward_halo/pallas_call | solution.py:495
  194.6 7.5 %collective-permute-done.18 = bf16[2,288,768]{2,1,0:T(8,128)(2,1)S(1)} collective-permute-done((bf16[2,288,768]{2,1,0:T(8,128)(2,1)}, bf16[2,288,768]{2,1,0:T(8,128)(2,1)S(1)}, u32[]{:S(2)}, u32[]{:S(2)}) %collective-permute-start.18) | collective-permute-done | bytes 884768 | tf_op jit(solution)/shard_map/ppermute | solution.py:1014
  202.2 1.5 fusion.8
  204.7 10.7 %turn_back.1 = (bf16[3,512,768]{2,1,0:T(8,128)(2,1)}, f32[3,768]{1,0:T(4,128)}, f32[8,384]{1,0:T(8,128)}, bf16[4,96,2304]{2,1,0:T(8,128)(2,1)}, bf16[4,96,2304]{2,1,0:T(8,128)(2,1)}) custom-call(s32[2]{0:T(128)} %pad_add_fusion.1.place_ref, bf16[512,768]{1,0:T(8,128)(2,1)} %bitcast.111, f32[6,768]{1,0:T(8,128)} %stack.130.vec_ref, ...), custom_call_target="tpu_custom_call" | custom-call | flops 10350000128 | bytes 27000000 | tf_op jit(solution)/shard_map/turn_back/pallas_call | solution.py:883
  216.5 8.6 %collective-permute-start.31 = (bf16[192,768]{1,0:T(8,128)(2,1)}, bf16[192,768]{1,0:T(8,128)(2,1)S(1)}, u32[]{:S(2)}, u32[]{:S(2)}) collective-permute-start(bf16[192,768]{1,0:T(8,128)(2,1)} %get-tuple-element.348), channel_id=1, source_target_pairs={{0,3},{1,0},{2,1},{3,2},{4,7},{5,4},{6,5},{7,6},{8,11},{9,8},{10,9... | collective-permute-start | bytes 884744 | tf_op jit(solution)/shard_map/ppermute | solution.py:1014
  226.5 1.8 add_convert_fusion.10
  229.6 2.8 collective-permute-start.33
  232.3 7.2 %input_grad.1 = (f32[512,768]{1,0:T(8,128)}, f32[2,768]{1,0:T(2,128)}) custom-call(bf16[512,768]{1,0:T(8,128)(2,1)} %bitcast.112, f32[6,768]{1,0:T(8,128)} %stack.130.vec_ref, bf16[3,512,768]{2,1,0:T(8,128)(2,1)} %get-tuple-element.207.d_ref, bf16[768,2304]{1,0:T(8,128)(2,1)} %w_ref.3, f32[512,768]{1,0:T(8,128)} %get-tuple-element.208.dh_ref), custom_call_target="tpu_custom_call" | custom-call | flops 8049999872 | bytes 21000000 | tf_op jit(solution)/shard_map/input_grad/pallas_call | solution.py:928
  242.2 7.6 %collective-permute-done.32 = bf16[192,768]{1,0:T(8,128)(2,1)} collective-permute-done((bf16[192,768]{1,0:T(8,128)(2,1)}, bf16[192,768]{1,0:T(8,128)(2,1)}, u32[]{:S(2)}, u32[]{:S(2)}) %collective-permute-start.32) | collective-permute-done | bytes 294944 | tf_op jit(solution)/shard_map/ppermute | solution.py:1014
  254.1 5.0 %collective-permute-done.35 = f32[84,128]{1,0:T(8,128)S(1)} collective-permute-done((f32[84,128]{1,0:T(8,128)S(1)}, f32[84,128]{1,0:T(8,128)S(1)}, u32[]{:S(2)}, u32[]{:S(2)}) %collective-permute-start.35) | collective-permute-done | bytes 43040 | tf_op jit(solution)/shard_map/ppermute | solution.py:1014
  259.7 1.5 fusion.2
  261.9 2.0 collective-permute-start.29
  263.9 2.3 collective-permute-start.30
  266.2 1.5 fusion.4
  268.9 5.7 %collective-permute-done.29 = bf16[24,3072]{1,0:T(8,128)(2,1)S(1)} collective-permute-done((bf16[24,3072]{1,0:T(8,128)(2,1)S(1)}, bf16[24,3072]{1,0:T(8,128)(2,1)S(1)}, u32[]{:S(2)}, u32[]{:S(2)}) %collective-permute-start.29) | collective-permute-done | bytes 147488 | tf_op jit(solution)/shard_map/ppermute | solution.py:1014
  276.0 3.0 collective-permute-start.37
  279.0 1.6 collective-permute-start.38
  281.2 3.0 collective-permute-done.37
  284.3 6.7 %collective-permute-done.38 = bf16[24,3072]{1,0:T(8,128)(2,1)S(1)} collective-permute-done((bf16[24,3072]{1,0:T(8,128)(2,1)S(1)}, bf16[24,3072]{1,0:T(8,128)(2,1)S(1)}, u32[]{:S(2)}, u32[]{:S(2)}) %collective-permute-start.38) | collective-permute-done | bytes 147488 | tf_op jit(solution)/shard_map/ppermute | solution.py:1014
  292.7 7.4 %collective-permute-done.40 = bf16[4,24,3072]{2,1,0:T(8,128)(2,1)S(1)} collective-permute-done((bf16[4,24,3072]{2,1,0:T(8,128)(2,1)S(1)}, bf16[4,24,3072]{2,1,0:T(8,128)(2,1)S(1)}, u32[]{:S(2)}, u32[]{:S(2)}) %collective-permute-start.40) | collective-permute-done | bytes 589856 | tf_op jit(solution)/shard_map/ppermute | solution.py:1014
  302.1 6.1 %assemble.2 = (f32[768,768]{1,0:T(8,128)}, f32[768,768]{1,0:T(8,128)}, f32[8,128]{1,0:T(8,128)}) custom-call(s32[2]{0:T(128)} %pad_add_fusion.1.place_ref, bf16[2,192,768]{2,1,0:T(8,128)(2,1)} %copy-done.8, bf16[2,192,768]{2,1,0:T(8,128)(2,1)} %copy-done.47, bf16[2,192,768]{2,1,0:T(8,128)(2,1)} %copy-done.48, bf16[2,192,768]{2,1,0:T(8,128)(2,1)} %copy-done.49), custom_call_target="tpu_custom_call" | custom-call | flops 6899999744 | bytes 18000000 | tf_op jit(solution)/shard_map/assemble/pallas_call | solution.py:997
  308.9 3.4 %collective-permute-start.46 = (f32[92,128]{1,0:T(8,128)S(1)}, f32[92,128]{1,0:T(8,128)S(1)}, u32[]{:S(2)}, u32[]{:S(2)}) collective-permute-start(f32[92,128]{1,0:T(8,128)S(1)} %pad_maximum_fusion.8), channel_id=1, source_target_pairs={{0,1},{1,0},{2,3},{3,2},{4,5},{5,4},{6,7},{7,6},{8,9},{9,8},{10,11... | collective-permute-start | bytes 141320 | tf_op jit(solution)/shard_map/ppermute | solution.py:1014
  312.4 1.8 collective-permute-done.46
  315.3 2.8 collective-permute-start.48
  318.7 3.0 collective-permute-start.49
  325.5 7.6 %assemble.3 = (f32[768,2304]{1,0:T(8,128)}, f32[768,768]{1,0:T(8,128)}, f32[8,128]{1,0:T(8,128)}) custom-call(s32[2]{0:T(128)} %pad_add_fusion.1.place_ref, bf16[2,4,24,3072]{3,2,1,0:T(8,128)(2,1)} %copy-done.3, bf16[2,4,24,3072]{3,2,1,0:T(8,128)(2,1)} %copy-done.37, bf16[2,4,24,3072]{3,2,1,0:T(8,128)(2,1)} %collective-permute-done.48.refs_2_, ...), custom_call_target="tpu_custom_call" | custom-call | flops 6899999744 | bytes 18000000 | tf_op jit(solution)/shard_map/assemble/pallas_call | solution.py:997
  (307 shorter events, 63.8 us)
Async XLA Ops:
  0.7 38.3 %collective-permute-start.1 = (bf16[512,768]{1,0:T(8,128)(2,1)}, bf16[512,768]{1,0:T(8,128)(2,1)S(1)}, u32[]{:S(2)}, u32[]{:S(2)}) collective-permute-start(bf16[512,768]{1,0:T(8,128)(2,1)} %bitcast.107), channel_id=1, source_target_pairs={{0,1},{1,2},{2,3},{4,5},{5,6},{6,7},{8,9},{9,10},{10,11},{12,13},{... | collective-permute-start | bytes 2359304 | tf_op jit(solution)/shard_map/ppermute | solution.py:1014
  4.9 34.1 %collective-permute-start.2 = (bf16[512,768]{1,0:T(8,128)(2,1)}, bf16[512,768]{1,0:T(8,128)(2,1)S(1)}, u32[]{:S(2)}, u32[]{:S(2)}) collective-permute-start(bf16[512,768]{1,0:T(8,128)(2,1)} %bitcast.108), channel_id=1, source_target_pairs={{1,0},{2,1},{3,2},{5,4},{6,5},{7,6},{9,8},{10,9},{11,10},{13,12},{... | collective-permute-start | bytes 2359304 | tf_op jit(solution)/shard_map/ppermute | solution.py:1014
  7.2 27.5 %collective-permute-start = (bf16[64,768]{1,0:T(8,128)(2,1)S(1)}, bf16[64,768]{1,0:T(8,128)(2,1)S(1)}, u32[]{:S(2)}, u32[]{:S(2)}) collective-permute-start(bf16[64,768]{1,0:T(8,128)(2,1)S(1)} %get-tuple-element.353), channel_id=1, source_target_pairs={{0,2},{1,3},{4,6},{5,7},{8,10},{9,11},{12,14},{13,15},{16,18},{17,... | collective-permute-start | bytes 294920 | tf_op jit(solution)/shard_map/ppermute | solution.py:1014
  12.2 25.6 %collective-permute-start.3 = (bf16[64,768]{1,0:T(8,128)(2,1)S(1)}, bf16[64,768]{1,0:T(8,128)(2,1)S(1)}, u32[]{:S(2)}, u32[]{:S(2)}) collective-permute-start(bf16[64,768]{1,0:T(8,128)(2,1)S(1)} %get-tuple-element.352), channel_id=1, source_target_pairs={{2,0},{3,1},{6,4},{7,5},{10,8},{11,9},{14,12},{15,13},{18,16},{19,... | collective-permute-start | bytes 294920 | tf_op jit(solution)/shard_map/ppermute | solution.py:1014
  15.6 45.7 %collective-permute-start.4 = (bf16[208,768]{1,0:T(8,128)(2,1)S(1)}, bf16[208,768]{1,0:T(8,128)(2,1)S(1)}, u32[]{:S(2)}, u32[]{:S(2)}) collective-permute-start(bf16[208,768]{1,0:T(8,128)(2,1)S(1)} %pad_maximum_fusion.7), channel_id=1, source_target_pairs={{0,1},{1,2},{2,3},{3,0},{4,5},{5,6},{6,7},{7,4},{8,9},{9,10},{10,1... | collective-permute-start | bytes 958472 | tf_op jit(solution)/shard_map/ppermute | solution.py:1014
  34.7 26.6 %collective-permute-start.5 = (bf16[208,768]{1,0:T(8,128)(2,1)S(1)}, bf16[208,768]{1,0:T(8,128)(2,1)S(1)}, u32[]{:S(2)}, u32[]{:S(2)}) collective-permute-start(bf16[208,768]{1,0:T(8,128)(2,1)S(1)} %pad_maximum_fusion.7), channel_id=1, source_target_pairs={{0,2},{1,3},{2,0},{3,1},{4,6},{5,7},{6,4},{7,5},{8,10},{9,11},{10,... | collective-permute-start | bytes 958472 | tf_op jit(solution)/shard_map/ppermute | solution.py:1014
  37.7 23.6 %collective-permute-start.6 = (bf16[208,768]{1,0:T(8,128)(2,1)S(1)}, bf16[208,768]{1,0:T(8,128)(2,1)S(1)}, u32[]{:S(2)}, u32[]{:S(2)}) collective-permute-start(bf16[208,768]{1,0:T(8,128)(2,1)S(1)} %pad_maximum_fusion.7), channel_id=1, source_target_pairs={{0,3},{1,0},{2,1},{3,2},{4,7},{5,4},{6,5},{7,6},{8,11},{9,8},{10,9... | collective-permute-start | bytes 958472 | tf_op jit(solution)/shard_map/ppermute | solution.py:1014
  62.2 23.0 %collective-permute-start.7 = (bf16[3,192,768]{2,1,0:T(8,128)(2,1)S(1)}, bf16[3,192,768]{2,1,0:T(8,128)(2,1)S(1)}, u32[]{:S(2)}, u32[]{:S(2)}) collective-permute-start(bf16[3,192,768]{2,1,0:T(8,128)(2,1)S(1)} %pad_maximum_fusion.2.refs_0_), channel_id=1, source_target_pairs={{0,8},{4,20},{8,0},{12,28},{16,24},{20,4},{24,16},{28,12},{1,9},{5... | collective-permute-start | bytes 2654216 | tf_op jit(solution)/shard_map/ppermute | solution.py:1014
  63.5 21.7 %collective-permute-start.8 = (bf16[3,192,768]{2,1,0:T(8,128)(2,1)S(1)}, bf16[3,192,768]{2,1,0:T(8,128)(2,1)S(1)}, u32[]{:S(2)}, u32[]{:S(2)}) collective-permute-start(bf16[3,192,768]{2,1,0:T(8,128)(2,1)S(1)} %pad_maximum_fusion.2.refs_0_), channel_id=1, source_target_pairs={{0,16},{4,12},{8,24},{12,4},{16,0},{20,28},{24,8},{28,20},{1,17},{... | collective-permute-start | bytes 2654216 | tf_op jit(solution)/shard_map/ppermute | solution.py:1014
  85.2 12.3 %collective-permute-start.10 = (bf16[3,192,768]{2,1,0:T(8,128)(2,1)S(1)}, bf16[3,192,768]{2,1,0:T(8,128)(2,1)S(1)}, u32[]{:S(2)}, u32[]{:S(2)}) collective-permute-start(bf16[3,192,768]{2,1,0:T(8,128)(2,1)S(1)} %collective-permute-done.7.refs_1_), channel_id=1, source_target_pairs={{0,16},{4,12},{8,24},{12,4},{16,0},{20,28},{24,8},{28,20},{1,17},{... | collective-permute-start | bytes 2654216 | tf_op jit(solution)/shard_map/ppermute | solution.py:1014
  85.6 16.6 %collective-permute-start.9 = (bf16[4,192,768]{2,1,0:T(8,128)(2,1)}, bf16[4,192,768]{2,1,0:T(8,128)(2,1)}, u32[]{:S(2)}, u32[]{:S(2)}) collective-permute-start(bf16[4,192,768]{2,1,0:T(8,128)(2,1)} %get-tuple-element.160), channel_id=1, source_target_pairs={{0,4},{4,0},{1,5},{5,1},{2,6},{6,2},{3,7},{7,3},{8,12},{12,8},{9,1... | collective-permute-start | bytes 3538952 | tf_op jit(solution)/shard_map/ppermute | solution.py:1014
  89.0 13.2 %collective-permute-start.11 = (bf16[3,192,768]{2,1,0:T(8,128)(2,1)S(1)}, bf16[3,192,768]{2,1,0:T(8,128)(2,1)S(1)}, u32[]{:S(2)}, u32[]{:S(2)}) collective-permute-start(bf16[3,192,768]{2,1,0:T(8,128)(2,1)S(1)} %pad_maximum_fusion.2.refs_0_), channel_id=1, source_target_pairs={{0,4},{4,0},{1,5},{5,1},{2,6},{6,2},{3,7},{7,3},{8,12},{12,8},{9,1... | collective-permute-start | bytes 2654216 | tf_op jit(solution)/shard_map/ppermute | solution.py:1014
  89.0 13.2 %collective-permute-start.12 = (bf16[3,192,768]{2,1,0:T(8,128)(2,1)S(1)}, bf16[3,192,768]{2,1,0:T(8,128)(2,1)S(1)}, u32[]{:S(2)}, u32[]{:S(2)}) collective-permute-start(bf16[3,192,768]{2,1,0:T(8,128)(2,1)S(1)} %collective-permute-done.7.refs_1_), channel_id=1, source_target_pairs={{0,4},{4,0},{1,5},{5,1},{2,6},{6,2},{3,7},{7,3},{8,12},{12,8},{9,1... | collective-permute-start | bytes 2654216 | tf_op jit(solution)/shard_map/ppermute | solution.py:1014
  89.5 12.7 %collective-permute-start.13 = (bf16[3,192,768]{2,1,0:T(8,128)(2,1)S(1)}, bf16[3,192,768]{2,1,0:T(8,128)(2,1)S(1)}, u32[]{:S(2)}, u32[]{:S(2)}) collective-permute-start(bf16[3,192,768]{2,1,0:T(8,128)(2,1)S(1)} %collective-permute-done.8.refs_2_), channel_id=1, source_target_pairs={{0,4},{4,0},{1,5},{5,1},{2,6},{6,2},{3,7},{7,3},{8,12},{12,8},{9,1... | collective-permute-start | bytes 2654216 | tf_op jit(solution)/shard_map/ppermute | solution.py:1014
  97.5 6.1 %collective-permute-start.14 = (bf16[3,192,768]{2,1,0:T(8,128)(2,1)S(1)}, bf16[3,192,768]{2,1,0:T(8,128)(2,1)S(1)}, u32[]{:S(2)}, u32[]{:S(2)}) collective-permute-start(bf16[3,192,768]{2,1,0:T(8,128)(2,1)S(1)} %collective-permute-done.10.refs_3_), channel_id=1, source_target_pairs={{0,4},{4,0},{1,5},{5,1},{2,6},{6,2},{3,7},{7,3},{8,12},{12,8},{9,1... | collective-permute-start | bytes 2654216 | tf_op jit(solution)/shard_map/ppermute | solution.py:1014
  120.7 24.9 %collective-permute-start.15 = (bf16[4,384,768]{2,1,0:T(8,128)(2,1)}, bf16[4,384,768]{2,1,0:T(8,128)(2,1)S(1)}, u32[]{:S(2)}, u32[]{:S(2)}) collective-permute-start(bf16[4,384,768]{2,1,0:T(8,128)(2,1)} %get-tuple-element.172), channel_id=1, source_target_pairs={{0,4},{4,0},{1,5},{5,1},{2,6},{6,2},{3,7},{7,3},{8,12},{12,8},{9,1... | collective-permute-start | bytes 7077896 | tf_op jit(solution)/shard_map/ppermute | solution.py:1014
  143.3 28.5 %collective-permute-start.17 = (bf16[4,288,768]{2,1,0:T(8,128)(2,1)}, bf16[4,288,768]{2,1,0:T(8,128)(2,1)}, u32[]{:S(2)}, u32[]{:S(2)}) collective-permute-start(bf16[4,288,768]{2,1,0:T(8,128)(2,1)} %get-tuple-element.175), channel_id=1, source_target_pairs={{0,4},{4,0},{1,5},{5,1},{2,6},{6,2},{3,7},{7,3},{8,12},{12,8},{9,1... | collective-permute-start | bytes 5308424 | tf_op jit(solution)/shard_map/ppermute | solution.py:1014
  143.6 35.7 %collective-permute-start.20 = (bf16[80,768]{1,0:T(8,128)(2,1)}, bf16[80,768]{1,0:T(8,128)(2,1)S(1)}, u32[]{:S(2)}, u32[]{:S(2)}) collective-permute-start(bf16[80,768]{1,0:T(8,128)(2,1)} %get-tuple-element.181), channel_id=1, source_target_pairs={{0,2},{1,3},{4,6},{5,7},{8,10},{9,11},{12,14},{13,15},{16,18},{17,... | collective-permute-start | bytes 368648 | tf_op jit(solution)/shard_map/ppermute | solution.py:1014
  145.6 37.7 %collective-permute-start.21 = (bf16[560,768]{1,0:T(8,128)(2,1)}, bf16[560,768]{1,0:T(8,128)(2,1)}, u32[]{:S(2)}, u32[]{:S(2)}) collective-permute-start(bf16[560,768]{1,0:T(8,128)(2,1)} %get-tuple-element.176.do_ref), channel_id=1, source_target_pairs={{0,1},{1,2},{2,3},{4,5},{5,6},{6,7},{8,9},{9,10},{10,11},{12,13},{... | collective-permute-start | bytes 2580488 | tf_op jit(solution)/shard_map/ppermute | solution.py:1014
  150.1 33.2 %collective-permute-start.22 = (bf16[560,768]{1,0:T(8,128)(2,1)}, bf16[560,768]{1,0:T(8,128)(2,1)}, u32[]{:S(2)}, u32[]{:S(2)}) collective-permute-start(bf16[560,768]{1,0:T(8,128)(2,1)} %get-tuple-element.176.do_ref), channel_id=1, source_target_pairs={{1,0},{2,1},{3,2},{5,4},{6,5},{7,6},{9,8},{10,9},{11,10},{13,12},{... | collective-permute-start | bytes 2580488 | tf_op jit(solution)/shard_map/ppermute | solution.py:1014
  152.1 22.0 %collective-permute-start.16 = (bf16[2,576,768]{2,1,0:T(8,128)(2,1)S(1)}, bf16[2,576,768]{2,1,0:T(8,128)(2,1)S(1)}, u32[]{:S(2)}, u32[]{:S(2)}) collective-permute-start(bf16[2,576,768]{2,1,0:T(8,128)(2,1)S(1)} %maximum_maximum_fusion), channel_id=1, source_target_pairs={{0,8},{4,20},{8,0},{12,28},{16,24},{20,4},{24,16},{28,12},{1,9},{5... | collective-permute-start | bytes 5308424 | tf_op jit(solution)/shard_map/ppermute | solution.py:1014
  171.9 11.4 %collective-permute-start.23 = (bf16[80,768]{1,0:T(8,128)(2,1)S(1)}, bf16[80,768]{1,0:T(8,128)(2,1)S(1)}, u32[]{:S(2)}, u32[]{:S(2)}) collective-permute-start(bf16[80,768]{1,0:T(8,128)(2,1)S(1)} %copy-done.50), channel_id=1, source_target_pairs={{2,0},{3,1},{6,4},{7,5},{10,8},{11,9},{14,12},{15,13},{18,16},{19,... | collective-permute-start | bytes 368648 | tf_op jit(solution)/shard_map/ppermute | solution.py:1014
  175.2 19.4 %collective-permute-start.19 = (bf16[576,768]{1,0:T(8,128)(2,1)}, bf16[576,768]{1,0:T(8,128)(2,1)S(1)}, u32[]{:S(2)}, u32[]{:S(2)}) collective-permute-start(bf16[576,768]{1,0:T(8,128)(2,1)} %fusion), channel_id=1, source_target_pairs={{0,16},{4,12},{8,24},{12,4},{16,0},{20,28},{24,8},{28,20},{1,17},{... | collective-permute-start | bytes 2654216 | tf_op jit(solution)/shard_map/ppermute | solution.py:1014
  179.3 22.9 %collective-permute-start.18 = (bf16[2,288,768]{2,1,0:T(8,128)(2,1)}, bf16[2,288,768]{2,1,0:T(8,128)(2,1)S(1)}, u32[]{:S(2)}, u32[]{:S(2)}) collective-permute-start(bf16[2,288,768]{2,1,0:T(8,128)(2,1)} %pad_maximum_fusion.3), channel_id=1, source_target_pairs={{0,8},{4,20},{8,0},{12,28},{16,24},{20,4},{24,16},{28,12},{1,9},{5... | collective-permute-start | bytes 2654216 | tf_op jit(solution)/shard_map/ppermute | solution.py:1014
  215.4 11.1 %collective-permute-start.25 = (bf16[4,96,2304]{2,1,0:T(8,128)(2,1)}, bf16[4,96,2304]{2,1,0:T(8,128)(2,1)}, u32[]{:S(2)}, u32[]{:S(2)}) collective-permute-start(bf16[4,96,2304]{2,1,0:T(8,128)(2,1)} %get-tuple-element.200), channel_id=1, source_target_pairs={{0,4},{4,0},{1,5},{5,1},{2,6},{6,2},{3,7},{7,3},{8,12},{12,8},{9,1... | collective-permute-start | bytes 5308424 | tf_op jit(solution)/shard_map/ppermute | solution.py:1014
  215.6 10.9 %collective-permute-start.24 = (bf16[288,768]{1,0:T(8,128)(2,1)S(1)}, bf16[288,768]{1,0:T(8,128)(2,1)S(1)}, u32[]{:S(2)}, u32[]{:S(2)}) collective-permute-start(bf16[288,768]{1,0:T(8,128)(2,1)S(1)} %fusion.8), channel_id=1, source_target_pairs={{0,16},{4,12},{8,24},{12,4},{16,0},{20,28},{24,8},{28,20},{1,17},{... | collective-permute-start | bytes 1327112 | tf_op jit(solution)/shard_map/ppermute | solution.py:1014
  216.5 25.7 %collective-permute-start.31 = (bf16[192,768]{1,0:T(8,128)(2,1)}, bf16[192,768]{1,0:T(8,128)(2,1)S(1)}, u32[]{:S(2)}, u32[]{:S(2)}) collective-permute-start(bf16[192,768]{1,0:T(8,128)(2,1)} %get-tuple-element.348), channel_id=1, source_target_pairs={{0,3},{1,0},{2,1},{3,2},{4,7},{5,4},{6,5},{7,6},{8,11},{9,8},{10,9... | collective-permute-start | bytes 884744 | tf_op jit(solution)/shard_map/ppermute | solution.py:1014
  225.1 24.8 %collective-permute-start.32 = (bf16[192,768]{1,0:T(8,128)(2,1)}, bf16[192,768]{1,0:T(8,128)(2,1)}, u32[]{:S(2)}, u32[]{:S(2)}) collective-permute-start(bf16[192,768]{1,0:T(8,128)(2,1)} %get-tuple-element.347), channel_id=1, source_target_pairs={{0,2},{1,3},{2,0},{3,1},{4,6},{5,7},{6,4},{7,5},{8,10},{9,11},{10,... | collective-permute-start | bytes 884744 | tf_op jit(solution)/shard_map/ppermute | solution.py:1014
  228.4 12.4 %collective-permute-start.26 = (bf16[2,96,2304]{2,1,0:T(8,128)(2,1)S(1)}, bf16[2,96,2304]{2,1,0:T(8,128)(2,1)}, u32[]{:S(2)}, u32[]{:S(2)}) collective-permute-start(bf16[2,96,2304]{2,1,0:T(8,128)(2,1)S(1)} %pad_maximum_fusion.4), channel_id=1, source_target_pairs={{0,8},{4,20},{8,0},{12,28},{16,24},{20,4},{24,16},{28,12},{1,9},{5... | collective-permute-start | bytes 2654216 | tf_op jit(solution)/shard_map/ppermute | solution.py:1014
  229.6 20.3 %collective-permute-start.33 = (bf16[192,768]{1,0:T(8,128)(2,1)S(1)}, bf16[192,768]{1,0:T(8,128)(2,1)S(1)}, u32[]{:S(2)}, u32[]{:S(2)}) collective-permute-start(bf16[192,768]{1,0:T(8,128)(2,1)S(1)} %fusion.5), channel_id=1, source_target_pairs={{0,1},{1,2},{2,3},{3,0},{4,5},{5,6},{6,7},{7,4},{8,9},{9,10},{10,1... | collective-permute-start | bytes 884744 | tf_op jit(solution)/shard_map/ppermute | solution.py:1014
  251.0 8.7 %collective-permute-start.27 = (bf16[96,2304]{1,0:T(8,128)(2,1)S(1)}, bf16[96,2304]{1,0:T(8,128)(2,1)S(1)}, u32[]{:S(2)}, u32[]{:S(2)}) collective-permute-start(bf16[96,2304]{1,0:T(8,128)(2,1)S(1)} %fusion.9), channel_id=1, source_target_pairs={{0,16},{4,12},{8,24},{12,4},{16,0},{20,28},{24,8},{28,20},{1,17},{... | collective-permute-start | bytes 1327112 | tf_op jit(solution)/shard_map/ppermute | solution.py:1014
  252.2 6.9 %collective-permute-start.35 = (f32[84,128]{1,0:T(8,128)S(1)}, f32[84,128]{1,0:T(8,128)S(1)}, u32[]{:S(2)}, u32[]{:S(2)}) collective-permute-start(f32[84,128]{1,0:T(8,128)S(1)} %bitcast_add_fusion.6), channel_id=1, source_target_pairs={{0,8},{8,0},{1,9},{9,1},{2,10},{10,2},{3,11},{11,3},{4,12},{12,4},... | collective-permute-start | bytes 129032 | tf_op jit(solution)/shard_map/ppermute | solution.py:1014
  259.1 8.5 %collective-permute-start.36 = (f32[84,128]{1,0:T(8,128)S(1)}, f32[84,128]{1,0:T(8,128)S(1)}, u32[]{:S(2)}, u32[]{:S(2)}) collective-permute-start(f32[84,128]{1,0:T(8,128)S(1)} %add.413), channel_id=1, source_target_pairs={{0,16},{16,0},{1,17},{17,1},{2,18},{18,2},{3,19},{19,3},{4,20},{20... | collective-permute-start | bytes 129032 | tf_op jit(solution)/shard_map/ppermute | solution.py:1014
  261.3 7.6 %collective-permute-start.28 = (bf16[24,3072]{1,0:T(8,128)(2,1)S(1)}, bf16[24,3072]{1,0:T(8,128)(2,1)S(1)}, u32[]{:S(2)}, u32[]{:S(2)}) collective-permute-start(bf16[24,3072]{1,0:T(8,128)(2,1)S(1)} %get-tuple-element.357), channel_id=1, source_target_pairs={{0,1},{1,2},{2,3},{3,0},{4,5},{5,6},{6,7},{7,4},{8,9},{9,10},{10,1... | collective-permute-start | bytes 442376 | tf_op jit(solution)/shard_map/ppermute | solution.py:1014
  261.9 12.7 %collective-permute-start.29 = (bf16[24,3072]{1,0:T(8,128)(2,1)S(1)}, bf16[24,3072]{1,0:T(8,128)(2,1)S(1)}, u32[]{:S(2)}, u32[]{:S(2)}) collective-permute-start(bf16[24,3072]{1,0:T(8,128)(2,1)S(1)} %get-tuple-element.358), channel_id=1, source_target_pairs={{0,2},{1,3},{2,0},{3,1},{4,6},{5,7},{6,4},{7,5},{8,10},{9,11},{10,... | collective-permute-start | bytes 442376 | tf_op jit(solution)/shard_map/ppermute | solution.py:1014
  263.9 10.7 %collective-permute-start.30 = (bf16[24,3072]{1,0:T(8,128)(2,1)S(1)}, bf16[24,3072]{1,0:T(8,128)(2,1)S(1)}, u32[]{:S(2)}, u32[]{:S(2)}) collective-permute-start(bf16[24,3072]{1,0:T(8,128)(2,1)S(1)} %get-tuple-element.356), channel_id=1, source_target_pairs={{0,3},{1,0},{2,1},{3,2},{4,7},{5,4},{6,5},{7,6},{8,11},{9,8},{10,9... | collective-permute-start | bytes 442376 | tf_op jit(solution)/shard_map/ppermute | solution.py:1014
  274.7 6.4 %collective-permute-start.42 = (bf16[192,768]{1,0:T(8,128)(2,1)S(1)}, bf16[192,768]{1,0:T(8,128)(2,1)S(1)}, u32[]{:S(2)}, u32[]{:S(2)}) collective-permute-start(bf16[192,768]{1,0:T(8,128)(2,1)S(1)} %fusion.4), channel_id=1, source_target_pairs={{0,8},{4,20},{8,0},{12,28},{16,24},{20,4},{24,16},{28,12},{1,9},{5... | collective-permute-start | bytes 884744 | tf_op jit(solution)/shard_map/ppermute | solution.py:1014
  276.0 8.3 %collective-permute-start.37 = (bf16[24,3072]{1,0:T(8,128)(2,1)S(1)}, bf16[24,3072]{1,0:T(8,128)(2,1)S(1)}, u32[]{:S(2)}, u32[]{:S(2)}) collective-permute-start(bf16[24,3072]{1,0:T(8,128)(2,1)S(1)} %add_convert_fusion.18), channel_id=1, source_target_pairs={{0,1},{1,2},{2,3},{3,0},{4,5},{5,6},{6,7},{7,4},{8,9},{9,10},{10,1... | collective-permute-start | bytes 442376 | tf_op jit(solution)/shard_map/ppermute | solution.py:1014
  279.0 11.9 %collective-permute-start.38 = (bf16[24,3072]{1,0:T(8,128)(2,1)S(1)}, bf16[24,3072]{1,0:T(8,128)(2,1)S(1)}, u32[]{:S(2)}, u32[]{:S(2)}) collective-permute-start(bf16[24,3072]{1,0:T(8,128)(2,1)S(1)} %add_convert_fusion.18), channel_id=1, source_target_pairs={{0,2},{1,3},{2,0},{3,1},{4,6},{5,7},{6,4},{7,5},{8,10},{9,11},{10,... | collective-permute-start | bytes 442376 | tf_op jit(solution)/shard_map/ppermute | solution.py:1014
  280.6 10.3 %collective-permute-start.39 = (bf16[24,3072]{1,0:T(8,128)(2,1)S(1)}, bf16[24,3072]{1,0:T(8,128)(2,1)S(1)}, u32[]{:S(2)}, u32[]{:S(2)}) collective-permute-start(bf16[24,3072]{1,0:T(8,128)(2,1)S(1)} %add_convert_fusion.18), channel_id=1, source_target_pairs={{0,3},{1,0},{2,1},{3,2},{4,7},{5,4},{6,5},{7,6},{8,11},{9,8},{10,9... | collective-permute-start | bytes 442376 | tf_op jit(solution)/shard_map/ppermute | solution.py:1014
  281.2 10.6 %collective-permute-start.43 = (bf16[2,192,768]{2,1,0:T(8,128)(2,1)S(1)}, bf16[2,192,768]{2,1,0:T(8,128)(2,1)S(1)}, u32[]{:S(2)}, u32[]{:S(2)}) collective-permute-start(bf16[2,192,768]{2,1,0:T(8,128)(2,1)S(1)} %pad_maximum_fusion.6.refs_0_), channel_id=1, source_target_pairs={{0,16},{4,12},{8,24},{12,4},{16,0},{20,28},{24,8},{28,20},{1,17},{... | collective-permute-start | bytes 1769480 | tf_op jit(solution)/shard_map/ppermute | solution.py:1014
  291.1 9.1 %collective-permute-start.40 = (bf16[4,24,3072]{2,1,0:T(8,128)(2,1)S(1)}, bf16[4,24,3072]{2,1,0:T(8,128)(2,1)S(1)}, u32[]{:S(2)}, u32[]{:S(2)}) collective-permute-start(bf16[4,24,3072]{2,1,0:T(8,128)(2,1)S(1)} %get-tuple-element.355), channel_id=1, source_target_pairs={{0,8},{4,20},{8,0},{12,28},{16,24},{20,4},{24,16},{28,12},{1,9},{5... | collective-permute-start | bytes 1769480 | tf_op jit(solution)/shard_map/ppermute | solution.py:1014
  291.1 9.2 %collective-permute-start.44 = (bf16[2,192,768]{2,1,0:T(8,128)(2,1)S(1)}, bf16[2,192,768]{2,1,0:T(8,128)(2,1)S(1)}, u32[]{:S(2)}, u32[]{:S(2)}) collective-permute-start(bf16[2,192,768]{2,1,0:T(8,128)(2,1)S(1)} %pad_maximum_fusion.6.refs_0_), channel_id=1, source_target_pairs={{0,4},{4,0},{1,5},{5,1},{2,6},{6,2},{3,7},{7,3},{8,12},{12,8},{9,1... | collective-permute-start | bytes 1769480 | tf_op jit(solution)/shard_map/ppermute | solution.py:1014
  291.8 8.6 %collective-permute-start.45 = (bf16[2,192,768]{2,1,0:T(8,128)(2,1)S(1)}, bf16[2,192,768]{2,1,0:T(8,128)(2,1)S(1)}, u32[]{:S(2)}, u32[]{:S(2)}) collective-permute-start(bf16[2,192,768]{2,1,0:T(8,128)(2,1)S(1)} %collective-permute-done.43.refs_1_), channel_id=1, source_target_pairs={{0,4},{4,0},{1,5},{5,1},{2,6},{6,2},{3,7},{7,3},{8,12},{12,8},{9,1... | collective-permute-start | bytes 1769480 | tf_op jit(solution)/shard_map/ppermute | solution.py:1014
  300.3 18.4 %collective-permute-start.41 = (bf16[2,4,24,3072]{3,2,1,0:T(8,128)(2,1)S(1)}, bf16[2,4,24,3072]{3,2,1,0:T(8,128)(2,1)S(1)}, u32[]{:S(2)}, u32[]{:S(2)}) collective-permute-start(bf16[2,4,24,3072]{3,2,1,0:T(8,128)(2,1)S(1)} %pad_maximum_fusion.1.refs_0_), channel_id=1, source_target_pairs={{0,16},{4,12},{8,24},{12,4},{16,0},{20,28},{24,8},{28,20},{1,17},{... | collective-permute-start | bytes 3538952 | tf_op jit(solution)/shard_map/ppermute | solution.py:1014
  308.9 5.2 %collective-permute-start.46 = (f32[92,128]{1,0:T(8,128)S(1)}, f32[92,128]{1,0:T(8,128)S(1)}, u32[]{:S(2)}, u32[]{:S(2)}) collective-permute-start(f32[92,128]{1,0:T(8,128)S(1)} %pad_maximum_fusion.8), channel_id=1, source_target_pairs={{0,1},{1,0},{2,3},{3,2},{4,5},{5,4},{6,7},{7,6},{8,9},{9,8},{10,11... | collective-permute-start | bytes 141320 | tf_op jit(solution)/shard_map/ppermute | solution.py:1014
  315.3 10.2 %collective-permute-start.48 = (bf16[2,4,24,3072]{3,2,1,0:T(8,128)(2,1)S(1)}, bf16[2,4,24,3072]{3,2,1,0:T(8,128)(2,1)}, u32[]{:S(2)}, u32[]{:S(2)}) collective-permute-start(bf16[2,4,24,3072]{3,2,1,0:T(8,128)(2,1)S(1)} %pad_maximum_fusion.1.refs_0_), channel_id=1, source_target_pairs={{0,4},{4,0},{1,5},{5,1},{2,6},{6,2},{3,7},{7,3},{8,12},{12,8},{9,1... | collective-permute-start | bytes 3538952 | tf_op jit(solution)/shard_map/ppermute | solution.py:1014
  318.7 6.8 %collective-permute-start.49 = (bf16[2,4,24,3072]{3,2,1,0:T(8,128)(2,1)S(1)}, bf16[2,4,24,3072]{3,2,1,0:T(8,128)(2,1)}, u32[]{:S(2)}, u32[]{:S(2)}) collective-permute-start(bf16[2,4,24,3072]{3,2,1,0:T(8,128)(2,1)S(1)} %collective-permute-done.41.refs_1_), channel_id=1, source_target_pairs={{0,4},{4,0},{1,5},{5,1},{2,6},{6,2},{3,7},{7,3},{8,12},{12,8},{9,1... | collective-permute-start | bytes 3538952 | tf_op jit(solution)/shard_map/ppermute | solution.py:1014
  (58 other events, 533.2 us)

commit v3 on v2

--- a/solution.py
+++ b/solution.py
@@ -94,13 +94,16 @@
     return (centred * lax.rsqrt(var + EPS) * gain + shift).astype(BF)
 
 
-def project(norm, hot_ref, table_ref, weights, b_ref, q_out, k_out, v_ref, exact):
+def project(norm, hot_ref, table_ref, weights, b_ref, outs, exact=()):
     width = norm.shape[1]
     for g in range(width // 256):
         c, s = cos_sin(hot_ref[...], table_ref[:, lanes_of(g, 512)])
-        for n, out in enumerate((q_out, k_out)):
+        for n, out in outs:
             lo = n * width + 256 * g
             proj = dot(norm, weights[:, lo : lo + 256]) + b_ref[:, lo : lo + 256]
+            if n == 2:
+                out[:, lanes_of(g)] = proj.astype(BF)
+                continue
             for half, turned in enumerate(
                 (proj[:, :128] * c - proj[:, 128:] * s, proj[:, :128] * s + proj[:, 128:] * c)
             ):
@@ -108,11 +111,6 @@
                 out[:, at] = turned.astype(BF)
                 if exact:
                     exact[n][:, at] = turned
-    for g in range(width // 256):
-        lo = 2 * width + 256 * g
-        v_ref[:, 256 * g : 256 * g + 256] = (
-            dot(norm, weights[:, lo : lo + 256]) + b_ref[:, lo : lo + 256]
-        ).astype(BF)
 
 
 def qkv_own_kernel(
@@ -129,7 +127,8 @@
         w_turned[:, 2 * width :] = w_ref[:, 2 * width :]
 
     norm = layer_norm_low(x_ref[...].astype(F32), vec_ref[LN1_GAIN], vec_ref[LN1_SHIFT])
-    project(norm, hot_ref, table_ref, w_turned, b_ref, q_ref, k_ref, v_ref, (pq_ref, pk_ref))
+    outs = [(0, q_ref), (1, k_ref), (2, v_ref)]
+    project(norm, hot_ref, table_ref, w_turned, b_ref, outs, (pq_ref, pk_ref))
 
 
 def qkv_own_call(x, onehot, vectors, weight, bias, order, table, first):
@@ -162,13 +161,14 @@
     )(x, onehot, vectors, weight, bias[None], order, table)
 
 
-def qkv_halo_kernel(
-    far_l, near_l, near_r, far_r, hot_ref, vec_ref, w_ref, b_ref, table_ref,
-    q_in, k_in, v_in, q_ref, k_ref, v_ref, x_all, sem,
+def halo_kernel(
+    far_l, near_l, near_r, far_r, hot_ref, vec_ref, w_ref, b_ref, table_ref, *refs, which
 ):
+    refs = refs[len(which) :]
+    out_refs, (x_all, sem) = refs[: len(which)], refs[len(which) :]
     width = x_all.shape[1]
     step = pl.program_id(0)
-    tile = q_ref.shape[0]
+    tile = out_refs[0].shape[0]
 
     @pl.when(step == 0)
     def _():
@@ -190,19 +190,19 @@
 
     x = x_all[pl.ds(pl.multiple_of(step * tile, tile), tile), :].astype(F32)
     norm = layer_norm_low(x, vec_ref[LN1_GAIN], vec_ref[LN1_SHIFT])
-    project(norm, hot_ref, table_ref, w_ref, b_ref, q_ref, k_ref, v_ref, ())
-
-
-def qkv_halo_call(pieces, onehot, vectors, weight, bias, table, q, k, v, first):
-    rows, width = q.shape
+    project(norm, hot_ref, table_ref, w_ref, b_ref, list(zip(which, out_refs)))
+
+
+def halo_call(pieces, onehot, vectors, weight, bias, table, arrays, which, first):
+    rows, width = arrays[0].shape
     own = pieces[1].shape[0]
     tile = first // 2
-    shape = jax.ShapeDtypeStruct((rows, width), BF)
     at = lambda w: pl.BlockSpec(
-        (pl.Element(tile), pl.Element(w)), lambda i: (pl.multiple_of(tile * i + jnp.where(i >= 2, own, 0), 64), 0)
+        (pl.Element(tile), pl.Element(w)),
+        lambda i: (pl.multiple_of(tile * i + jnp.where(i >= 2, own, 0), 64), 0),
     )
     return pl.pallas_call(
-        qkv_halo_kernel,
+        functools.partial(halo_kernel, which=which),
         grid=(4,),
         in_specs=[ANY] * 4
         + [
@@ -212,15 +212,15 @@
             whole((1, 3 * width)),
             whole(table.shape),
         ]
-        + [ANY] * 3,
-        out_specs=[at(width)] * 3,
-        out_shape=[shape] * 3,
-        input_output_aliases={9: 0, 10: 1, 11: 2},
+        + [ANY] * len(which),
+        out_specs=[at(width)] * len(which),
+        out_shape=[jax.ShapeDtypeStruct((rows, width), BF)] * len(which),
+        input_output_aliases={9 + n: n for n in range(len(which))},
         scratch_shapes=[pltpu.VMEM((2 * first, width), BF), pltpu.SemaphoreType.DMA((4,))],
         compiler_params=params(),
-        cost_estimate=cost(11.5),
-        name="qkv_halo",
-    )(*pieces, onehot, vectors, weight, bias[None], table, q, k, v)
+        cost_estimate=cost(4 * len(which)),
+        name="halo",
+    )(*pieces, onehot, vectors, weight, bias[None], table, *arrays)
 
 
 def head_stack(block, turned, scale=None):
@@ -568,7 +568,7 @@
 
 def one_quarter(q, w_all, norm_ref, dy_ref, bu_ref, dbu_ref, out_acc, dn_acc, g_all, fresh):
     own, width = norm_ref.shape
-    tile = 256
+    tile = w_all.shape[1] - width
     for t in range((w_all.shape[1] - width) // tile):
         cols = slice(tile * t, tile * t + tile)
         down = slice(width + tile * t, width + tile * t + tile)
@@ -644,111 +644,102 @@
     )(place, x, low, w_out, vectors, dy, b_up, w_up, w_down)
 
 
-def other_quarters(
-    place, piece_refs, base, w_all, w_sem, norm_ref, dy_ref, bu_ref, dbu_ref, out_acc, dn_acc,
-    g_all, g_sem, keep_ref, send_ref, slices,
+def middle_kernel(
+    place_ref, vec_ref, bu_ref, lse_ref, norm_in, dy_in, out_in, dn_in, hid_in, low_in, mixed_in,
+    wo_in, keep_in, send_in, *refs, slices,
 ):
+    piece_refs = refs[:slices]
+    (
+        act_out, dh_out, dheads_ref, head_ref, tail_ref, delta_ref, small_ref, dbu_ref, keep_ref,
+        send_ref,
+        w_all, g_all, go_all, norm_ref, dy_ref, out_acc, dn_acc, hid_ref, low_ref, mixed_ref,
+        wo_ref, act_ref, dh_ref, own_grads, w_sem, g_sem, in_sem, out_sem,
+    ) = refs[slices:]
+    place = place_ref[0]
+    own, width = norm_ref.shape
+    quarters = w_all.shape[0]
     rows = w_all.shape[1] // slices
 
     def fetches(q):
         return [
             pltpu.make_async_copy(
-                ref.at[base + q],
+                ref.at[q],
                 w_all.at[q, pl.ds(pl.multiple_of(source * rows, rows), rows), :],
                 w_sem.at[q, n],
             )
             for n, (ref, source) in enumerate(gathered(place, piece_refs))
         ]
 
-    for q in range(w_all.shape[0]):
+    inputs = [
+        pltpu.make_async_copy(source, target, in_sem.at[n])
+        for n, (source, target) in enumerate(
+            (
+                (norm_in, norm_ref), (dy_in, dy_ref), (out_in, out_acc), (dn_in, dn_acc),
+                (hid_in, hid_ref), (low_in, low_ref), (mixed_in, mixed_ref), (wo_in, wo_ref),
+                (keep_in, own_grads.at[0]), (send_in, own_grads.at[1]),
+            )
+        )
+    ]
+    for copy in inputs[:2] + fetches(0) + inputs[2:4]:
+        copy.start()
+    for q in range(1, quarters):
         for copy in fetches(q):
             copy.start()
+    for copy in inputs[4:]:
+        copy.start()
+    for copy in inputs[:2]:
+        copy.wait()
 
     def quarter(q, _):
         for copy in fetches(q):
             copy.wait()
+
+        @pl.when(q == 0)
+        def _():
+            for copy in inputs[2:4]:
+                copy.wait()
+
         one_quarter(q, w_all, norm_ref, dy_ref, bu_ref, dbu_ref, out_acc, dn_acc, g_all, False)
         slices_out(
-            place, g_all.at[q], keep_ref, send_ref, pl.multiple_of(q * rows, rows), g_sem.at[q],
-            slices, rows,
+            place, g_all.at[q], keep_ref, send_ref, pl.multiple_of(q * rows + rows, rows),
+            g_sem.at[q], slices, rows,
         )
         return 0
 
-    lax.fori_loop(0, w_all.shape[0], quarter, 0)
-
-
-def middle_next_kernel(place_ref, norm_ref, out_in, dn_in, dy_ref, bu_ref, *refs, slices, base):
-    piece_refs = refs[:slices]
-    out_ref, dn_ref, dbu_ref, keep_ref, send_ref, w_all, g_all, w_sem, g_sem = refs[slices:]
-    out_ref[...] = out_in[...]
-    dn_ref[...] = dn_in[...]
-    other_quarters(
-        place_ref[0], piece_refs, base, w_all, w_sem, norm_ref, dy_ref, bu_ref, dbu_ref, out_ref,
-        dn_ref, g_all, g_sem, keep_ref, send_ref, slices,
-    )
-    rows = w_all.shape[1] // slices
-    for q in range(w_all.shape[0]):
-        slices_wait(g_all.at[q], keep_ref, g_sem.at[q], slices, rows)
-
-
-def middle_next_call(place, norm, out, dn, dy, b_up, pieces, slices, base):
-    own, width = norm.shape
-    quarters, hidden = b_up.shape
-    rows = width + hidden
-    vmem = pl.BlockSpec(memory_space=pltpu.VMEM)
-    sds = jax.ShapeDtypeStruct
-    return pl.pallas_call(
-        functools.partial(middle_next_kernel, slices=slices, base=base),
-        in_specs=[SMEM] + [vmem] * 5 + [ANY] * len(pieces),
-        out_specs=[vmem] * 3 + [ANY] * 2,
-        out_shape=[sds((own, width), F32), sds((own, width), F32), sds((quarters, hidden), F32)]
-        + [sds((slices // 2, quarters * rows // slices, width), BF)] * 2,
-        scratch_shapes=[
-            pltpu.VMEM((quarters, rows, width), BF),
-            pltpu.VMEM((quarters, rows, width), BF),
-            pltpu.SemaphoreType.DMA((quarters, slices)),
-            pltpu.SemaphoreType.DMA((quarters, slices)),
-        ],
-        compiler_params=params(),
-        cost_estimate=cost(8 * quarters),
-        name="middle_next",
-    )(place, norm, out, dn, dy, b_up, *pieces)
-
-
-def middle_last_kernel(
-    place_ref, hid_ref, norm_ref, out_in, dn_in, low_ref, mixed_ref, wo_ref, vec_ref, dy_ref,
-    bu_ref, lse_ref, *refs, slices, base,
-):
-    piece_refs = refs[:slices]
-    (
-        act_ref, dh_ref, dheads_ref, head_ref, tail_ref, delta_ref, small_ref, dbu_ref,
-        keep_ref, send_ref, w_all, g_all, go_all, out_acc, dn_acc, w_sem, g_sem,
-    ) = refs[slices:]
-    place = place_ref[0]
-    own, width = norm_ref.shape
-    quarters = w_all.shape[0]
-    rows = w_all.shape[1] // slices
-    out_acc[...] = out_in[...]
-    dn_acc[...] = dn_in[...]
-    other_quarters(
-        place, piece_refs, base, w_all, w_sem, norm_ref, dy_ref, bu_ref, dbu_ref, out_acc, dn_acc,
-        g_all, g_sem, keep_ref, send_ref, slices,
-    )
-
+    lax.fori_loop(0, quarters, quarter, 0)
+
+    for copy in inputs[4:]:
+        copy.wait()
     hidden_in = hid_ref[...]
-    act_ref[...] = (hidden_in + out_acc[...] + vec_ref[B_DOWN]).astype(BF)
     xhat, inverse = norm_parts(hidden_in)
     dn = dn_acc[...]
     dy = dy_ref[...].astype(F32)
     d_hidden = dy + norm_back(dn, xhat, inverse, vec_ref[LN2_GAIN])
     dh_ref[...] = d_hidden
     d_att = d_hidden.astype(BF)
+    d_heads = dot_nt(d_att, wo_ref[...]).astype(BF)
+    dheads_ref[:own, :] = d_heads
+    go_all[...] = dot_tn(low_ref[...], d_att).astype(BF)
+    few = width // slices
+    base = quarters * rows + rows
+    slices_out(place, go_all, keep_ref, send_ref, base, g_sem.at[quarters], slices, few)
+    act_ref[...] = (hidden_in + out_acc[...] + vec_ref[B_DOWN]).astype(BF)
+    outputs = [
+        pltpu.make_async_copy(source, target, out_sem.at[n])
+        for n, (source, target) in enumerate(
+            (
+                (act_ref, act_out), (dh_ref, dh_out),
+                (own_grads.at[0], keep_ref.at[:, 0:rows, :]),
+                (own_grads.at[1], send_ref.at[:, 0:rows, :]),
+            )
+        )
+    ]
+    for copy in outputs:
+        copy.start()
     small_ref[0:1, :] = columns_sum(dn * xhat)
     small_ref[1:2, :] = columns_sum(dn)
     small_ref[2:3, :] = columns_sum(dy)
     small_ref[3:4, :] = columns_sum(d_att.astype(F32))
-    d_heads = dot_nt(d_att, wo_ref[...]).astype(BF)
-    dheads_ref[:own, :] = d_heads
     spread = d_heads.astype(F32) * mixed_ref[...]
     pick = lax.broadcasted_iota(jnp.int32, (8, 256), 0)
     pick = (pick == lax.broadcasted_iota(jnp.int32, (8, 256), 1) // 64).astype(F32)
@@ -781,28 +772,27 @@
     tail_ref[REACH + 2 * STAT_ROWS :, :] = blank
     head_ref[:REACH, :] = d_heads[:REACH, :]
     tail_ref[:REACH, :] = d_heads[own - REACH :, :]
-    go_all[...] = dot_tn(low_ref[...], d_att).astype(BF)
-    few = width // slices
-    slices_out(place, go_all, keep_ref, send_ref, quarters * rows, g_sem.at[quarters], slices, few)
     for q in range(quarters):
         slices_wait(g_all.at[q], keep_ref, g_sem.at[q], slices, rows)
     slices_wait(go_all, keep_ref, g_sem.at[quarters], slices, few)
-
-
-def middle_last_call(
-    place, hidden_in, norm, out, dn, low, mixed, w_out, vectors, dy, b_up, lse, pieces, slices,
-    base,
+    for copy in outputs:
+        copy.wait()
+
+
+def middle_call(
+    place, hidden_in, norm, out, dn, low, mixed, w_out, vectors, dy, b_up, lse, kept, sent, pieces,
+    slices,
 ):
     own, width = norm.shape
     quarters, hidden = b_up.shape
     rows = width + hidden
     vmem = pl.BlockSpec(memory_space=pltpu.VMEM)
     sds = jax.ShapeDtypeStruct
-    grads = sds((slices // 2, (quarters * rows + width) // slices, width), BF)
+    grads = sds((slices // 2, ((quarters + 1) * rows + width) // slices, width), BF)
     return pl.pallas_call(
-        functools.partial(middle_last_kernel, slices=slices, base=base),
-        in_specs=[SMEM] + [vmem] * 11 + [ANY] * len(pieces),
-        out_specs=[vmem] * 8 + [ANY] * 2,
+        functools.partial(middle_kernel, slices=slices),
+        in_specs=[SMEM] + [vmem] * 3 + [ANY] * (10 + len(pieces)),
+        out_specs=[ANY] * 2 + [vmem] * 6 + [ANY] * 2,
         out_shape=[
             sds((own, width), BF),
             sds((own, width), F32),
@@ -819,15 +809,29 @@
             pltpu.VMEM((quarters, rows, width), BF),
             pltpu.VMEM((quarters, rows, width), BF),
             pltpu.VMEM((width, width), BF),
+            pltpu.VMEM((own, width), BF),
+            pltpu.VMEM((own, width), BF),
             pltpu.VMEM((own, width), F32),
             pltpu.VMEM((own, width), F32),
+            pltpu.VMEM((own, width), F32),
+            pltpu.VMEM((own, width), BF),
+            pltpu.VMEM((own, width), F32),
+            pltpu.VMEM((width, width), BF),
+            pltpu.VMEM((own, width), BF),
+            pltpu.VMEM((own, width), F32),
+            pltpu.VMEM((2,) + kept.shape, BF),
             pltpu.SemaphoreType.DMA((quarters, slices)),
             pltpu.SemaphoreType.DMA((quarters + 1, slices)),
+            pltpu.SemaphoreType.DMA((10,)),
+            pltpu.SemaphoreType.DMA((4,)),
         ],
         compiler_params=params(),
-        cost_estimate=cost(12),
-        name="middle_last",
-    )(place, hidden_in, norm, out, dn, low, mixed, w_out, vectors, dy, b_up, lse, *pieces)
+        cost_estimate=cost(20),
+        name="middle",
+    )(
+        place, vectors, b_up, lse, norm, dy, out, dn, hidden_in, low, mixed, w_out, kept, sent,
+        *pieces,
+    )
 
 
 def turn_back_kernel(
@@ -914,31 +918,49 @@
     )(place, x, vectors, dq, dk, dv, q_exact, k_exact, onehot, table, grid8, back)
 
 
-def input_grad_kernel(x_ref, vec_ref, d_ref, w_ref, dh_ref, out_ref, small_ref):
+def input_grad_kernel(
+    place_ref, x_ref, vec_ref, d_ref, w_ref, dh_ref, db_ref, mid_ref, freq_ref, up0_ref, up_ref,
+    out_ref, small_ref,
+):
     width = x_ref.shape[1]
     d_norm = sum(dot_nt(d_ref[n], w_ref[:, lanes_of(n, width)]) for n in range(3))
     xhat, inverse = norm_parts(x_ref[...].astype(F32))
-    small_ref[0:1, :] = columns_sum(d_norm * xhat)
-    small_ref[1:2, :] = columns_sum(d_norm)
     out_ref[...] = dh_ref[...] + norm_back(d_norm, xhat, inverse, vec_ref[LN1_GAIN])
-
-
-def input_grad_call(x, vectors, d_qkv, weight, d_hidden):
+    row = 0
+    for vector in (
+        columns_sum(d_norm * xhat), columns_sum(d_norm), *(db_ref[n : n + 1, :] for n in range(3)),
+        mid_ref[3:4, :], freq_ref[0:1, :], freq_ref[1:2, :], *(mid_ref[n : n + 1, :] for n in range(3)),
+    ):
+        for n in range(vector.shape[1] // 128):
+            small_ref[row : row + 1, :] = vector[:, lanes_of(n, 128)]
+            row += 1
+    depth = 1 + up_ref.shape[0]
+    hidden = up0_ref.shape[1] // 128
+    for k in range(depth):
+        quarter = (place_ref[1] - k + depth) % depth
+        vector = up_ref[k - 1 : k, :] if k else up0_ref[...]
+        for n in range(hidden):
+            small_ref[pl.ds(row + quarter * hidden + n, 1), :] = vector[:, lanes_of(n, 128)]
+
+
+def input_grad_call(place, x, vectors, d_qkv, weight, d_hidden, db_qkv, small_mid, freqs, up0, up):
     rows, width = x.shape
+    short = 9 * width + freqs.shape[1] * 2 + up0.size * (1 + up.shape[0])
     return pl.pallas_call(
         input_grad_kernel,
+        in_specs=[SMEM] + [pl.BlockSpec(memory_space=pltpu.VMEM)] * 10,
         out_shape=[
             jax.ShapeDtypeStruct((rows, width), F32),
-            jax.ShapeDtypeStruct((2, width), F32),
+            jax.ShapeDtypeStruct((short // 128, 128), F32),
         ],
         compiler_params=params(),
         cost_estimate=cost(7),
         name="input_grad",
-    )(x, vectors, d_qkv, weight, d_hidden)
-
-
-def assemble_kernel(place_ref, *refs, split, outs):
-    out_refs, (held, sem) = refs[4 : 4 + outs], refs[4 + outs :]
+    )(place, x, vectors, d_qkv, weight, d_hidden, db_qkv, small_mid, freqs, up0, up)
+
+
+def assemble_kernel(place_ref, *refs, split, outs, skip):
+    out_refs, (held, sem) = refs[-2 - outs : -2], refs[-2:]
     pairs = refs[:4]
     piece_refs = [pairs[n // 2].at[n % 2] for n in range(8)]
     place, depth = place_ref[0], place_ref[1]
@@ -954,6 +976,9 @@
 
     copy(piece_refs[0], slot).wait()
     rows = held.shape[-2]
+    total_ref = None
+    if skip is not None:
+        out_refs, total_ref = out_refs[:-1], out_refs[-1]
     out_refs, squares = out_refs[:-1], out_refs[-1]
 
     @pl.when(slot == 0)
@@ -981,9 +1006,22 @@
             @pl.when(slot // each == n)
             def _():
                 ref[...] = block
-
-
-def assemble_call(place, arrays, shapes, split):
+    if skip is not None:
+        small_ref = refs[4]
+
+        @pl.when(slot == held.shape[0] - 1)
+        def _():
+            short = small_ref[...]
+            row = lax.broadcasted_iota(jnp.int32, short.shape, 0)
+            mine = (row >= skip[0]) & (row < skip[1])
+            parts = row >= short.shape[0] - 8
+            others = jnp.where(mine, 0.0, jnp.where(parts, short, short * short))
+            turned = jnp.where(mine, short * short, 0.0)
+            total_ref[0:1, :] = jnp.full((1, 128), jnp.sum(turned))
+            total_ref[1:2, :] = jnp.full((1, 128), jnp.sum(others) + jnp.sum(squares[...]))
+
+
+def assemble_call(place, arrays, shapes, split, small=None, skip=None):
     pieces = 8
     rows = arrays[0].shape[-2] * max(split, 1)
     each = pieces if split else pieces // len(shapes)
@@ -994,10 +1032,13 @@
 
     specs = [spec(n, shape) for n, shape in enumerate(shapes)] + [whole((8, 128))]
     shapes = shapes + [(8, 128)]
+    given = []
+    if small is not None:
+        given, specs, shapes = [small], specs + [whole((2, 128))], shapes + [(2, 128)]
     return pl.pallas_call(
-        functools.partial(assemble_kernel, split=split, outs=len(shapes)),
+        functools.partial(assemble_kernel, split=split, outs=len(shapes), skip=skip),
         grid=(pieces,),
-        in_specs=[SMEM] + [ANY] * len(arrays),
+        in_specs=[SMEM] + [ANY] * len(arrays) + [whole(x.shape) for x in given],
         out_specs=specs,
         out_shape=[jax.ShapeDtypeStruct(s, F32) for s in shapes],
         scratch_shapes=[
@@ -1007,7 +1048,7 @@
         compiler_params=params(),
         cost_estimate=cost(6),
         name="assemble",
-    )(place, *arrays)
+    )(place, *arrays, *given)
 
 
 def send(x, axis, pairs):
@@ -1029,14 +1070,6 @@
 
 def sum_low(*terms):
     return functools.reduce(lambda x, y: x + y, [t.astype(F32) for t in terms])
-
-
-def chip_sums(kept, far):
-    total = [
-        jnp.concatenate([sum_low(x[n], y[n]) for x, y in zip(kept, far)], 0).astype(BF)
-        for n in range(4)
-    ]
-    return jnp.stack([total[1], total[3]]), (total[0], total[2])
 
 
 def after(x, *others):
@@ -1152,7 +1185,6 @@
     rot_q, rot_k, values, q_exact, k_exact, weight_turned = qkv_own_call(
         tokens, onehot, vectors, query_key_value_weight, bias_turned, order, table, side
     )
-
     rows = (width + w_down.shape[0]) // slices
     eighth = jnp.where(
         plane < width // rows,
@@ -1166,10 +1198,9 @@
     bias_rows = jnp.pad(jnp.stack(bias_rows), ((0, 13), (0, 0)))
     eighth = jnp.concatenate([eighth, bias_rows], 0)
     others = [send(eighth, "n", ring(depth, k)) for k in range(1, depth)]
-    x_parts, rot_q = lax.optimization_barrier((x_parts, rot_q))
-    rot_q, rot_k, values = qkv_halo_call(
-        x_parts, onehot, vectors, weight_turned, bias_turned, table, rot_q, rot_k, values, side
-    )
+    x_parts, rot_q, idk = lax.optimization_barrier((x_parts, rot_q, idk))
+    halo_args = (x_parts, onehot, vectors, weight_turned, bias_turned, table)
+    rot_q, rot_k, values = halo_call(*halo_args, (rot_q, rot_k, values), (0, 1, 2), side)
     part = forward_call(bounds_fwd, rot_q, rot_k, values, idk, idq, side, own, 0, blocks // 2)
     others, part = lax.optimization_barrier((others, part))
     up_biases = jnp.concatenate(
@@ -1187,89 +1218,79 @@
     )
     over_1, over_2, norm2 = lax.optimization_barrier((over_1, over_2, norm2))
     diagonal = send(over_1, PLANE, SECOND)
-    far_own = send(after(sent_own, over_1, over_2), "c", SWAP)
     near = [own_w, over_1, over_2, diagonal]
     pieces = near + [send(x, "c", SWAP) for x in near]
-    norm2 = after(norm2, far_own)
-    split = depth - 2
-    out1, dn1, up_sum1, kept_next, sent_next = middle_next_call(
-        place, norm2, out0, dn0, cotangent, up_biases[:split], pieces, slices, 0
-    )
-    far_next = send(sent_next, "c", SWAP)
+    grid8 = jnp.pad(grid_own.astype(F32), ((0, 6), (0, 0)))
+    norm2, up_biases, bounds_bwd = lax.optimization_barrier((norm2, up_biases, bounds_bwd))
     (
-        activations, d_hidden, d_heads, d_head, d_tail, delta, small_mid, up_sum2, kept_last,
-        sent_last,
-    ) = middle_last_call(
-        place, hidden_in, norm2, out1, dn1, mixed_low, mixed, output_weight, vectors, cotangent,
-        up_biases[split:], lse, pieces, slices, split,
-    )
-    up_sums = (up_sum0, up_sum1, up_sum2)
-    far_next, d_heads = lax.optimization_barrier((far_next, d_heads))
-    away_a, rest_a = chip_sums((kept_own, kept_next), (far_own, far_next))
-    got_1a = send(away_a, PLANE, FIRST)
-    far_last = send(sent_last, "c", SWAP)
+        activations, d_hidden, d_heads, d_head, d_tail, delta, small_mid, up_sums, kept_mid,
+        sent_mid,
+    ) = middle_call(
+        place, hidden_in, norm2, out0, dn0, mixed_low, mixed, output_weight, vectors, cotangent,
+        up_biases, lse, kept_own, sent_own, pieces, slices,
+    )
+    far_mid = send(sent_mid, "c", SWAP)
     do_parts = around(d_heads, d_head, d_tail)
 
+    early = (depth - 1) * rows
+    lots = (slice(0, early), slice(early, depth * rows + width // slices))
+
+    def chip_sum(lot, n):
+        return sum_low(kept_mid[n, lots[lot]], far_mid[n, lots[lot]])
+
+    def plane_part(lot, lo, hi):
+        at, there = slice(lots[lot].start + lo, lots[lot].start + hi), slice(lo, hi)
+        total = sum_low(kept_mid[0, at], far_mid[0, at], got_1[lot][0, there], got_2[lot][there])
+        return wide_sum(total, extra)
+
+    got_1, got_2 = [None, None], [None, None]
+    away = chip_sum(0, slice(1, None, 2)).astype(BF)
+    got_1[0] = send(away, PLANE, FIRST)
     dq, dk, dv = backward_own_call(
-        bounds_fwd, rot_q, d_heads, rot_k, values, idk, idq, lse, delta, side, own
-    )
-    got_1a, far_last, dq = lax.optimization_barrier((got_1a, far_last, dq))
-    away_a = sum_low(rest_a[1], got_1a[1]).astype(BF)
-    got_2a = send(away_a, PLANE, SECOND)
-    away_b, rest_b = chip_sums((kept_last,), (far_last,))
-    got_1b = send(away_b, PLANE, FIRST)
-    do_parts, dq, dk, _ = lax.optimization_barrier((do_parts, dq, dk, (away_a, away_b)))
+        bounds_fwd, rot_q, d_heads, rot_k, values, idk, idq, lse, after(delta, away), side, own
+    )
+    got_1[0], dq = lax.optimization_barrier((got_1[0], dq))
+    away = (chip_sum(0, 2) + got_1[0][1].astype(F32)).astype(BF)
+    got_2[0] = send(away, PLANE, SECOND)
+    away_b = chip_sum(1, slice(1, None, 2)).astype(BF)
+    got_1[1] = send(away_b, PLANE, FIRST)
+    do_parts, dq, dk, _ = lax.optimization_barrier((do_parts, dq, dk, (away, away_b)))
     dk, dv = backward_halo_call(
         bounds_bwd, rot_q, do_parts, rot_k, values, idk, idq, dk, dv, side
     )
-    got_1b, got_2a, dk = lax.optimization_barrier((got_1b, got_2a, dk))
-    away_b = sum_low(rest_b[1], got_1b[1]).astype(BF)
-    got_2b = send(away_b, PLANE, SECOND)
-
-    def part_a(k):
-        at = slice(k * rows, k * rows + rows)
-        return wide_sum(sum_low(rest_a[0][at], got_1a[0, at], got_2a[at]), extra)
-
-    ff_sent = [part_a(k).astype(BF) for k in range(1, depth - 1)]
+    got_1[1], got_2[0], dk = lax.optimization_barrier((got_1[1], got_2[0], dk))
+    away = (chip_sum(1, 2) + got_1[1][1].astype(F32)).astype(BF)
+    got_2[1] = send(away, PLANE, SECOND)
+    ff_sent = [plane_part(0, k * rows, k * rows + rows).astype(BF) for k in range(1, depth - 1)]
     ff_got = [send(ff_sent[k - 1], "n", ring(depth, -k)) for k in range(1, depth - 1)]
-    dk = after(dk, away_b, ff_sent)
-
-    grid8 = jnp.pad(grid_own.astype(F32), ((0, 6), (0, 0)))
+    dk = after(dk, away, ff_sent)
+
     d_qkv, grad_b_qkv, freqs8, kept_qkv, sent_qkv = turn_back_call(
         place, tokens, vectors, dq, dk, dv, q_exact, k_exact, onehot, table, grid8,
         order.T, side, slices,
     )
     far_qkv = send(sent_qkv, "c", SWAP)
-    got_2b, far_qkv, d_qkv = lax.optimization_barrier((got_2b, far_qkv, d_qkv))
-    away, rest_qkv = chip_sums((kept_qkv,), (far_qkv,))
+    away = sum_low(kept_qkv[1::2], far_qkv[1::2]).astype(BF)
     got_1_qkv = send(away, PLANE, FIRST)
-
-    def part_b(lo, hi):
-        at = slice(lo, hi)
-        return wide_sum(sum_low(rest_b[0][at], got_1b[0, at], got_2b[at]), extra)
-
-    got_2b = after(got_2b, away)
-    ff_sent = part_b(0, rows).astype(BF)
+    got_2[1] = after(got_2[1], away)
+    ff_sent = plane_part(1, 0, rows).astype(BF)
     ff_got.append(send(ff_sent, "n", ring(depth, 1 - depth)))
     input_grad, small_in = input_grad_call(
-        tokens, vectors, after(d_qkv, away, ff_sent), query_key_value_weight, d_hidden
+        place, tokens, vectors, after(d_qkv, ff_sent), query_key_value_weight, d_hidden,
+        grad_b_qkv, small_mid, freqs8, up_sum0, up_sums,
     )
     got_1_qkv, small_in = lax.optimization_barrier((got_1_qkv, small_in))
-    away = sum_low(rest_qkv[1], got_1_qkv[1]).astype(BF)
+    away = sum_low(kept_qkv[2], far_qkv[2], got_1_qkv[1]).astype(BF)
     got_2_qkv = send(away, PLANE, SECOND)
     ff_got, small_in, _ = lax.optimization_barrier((ff_got, small_in, away))
-    ff_total = part_a(0) + sum_low(*ff_got)
-    plane_qkv = wide_sum(sum_low(rest_qkv[0], got_1_qkv[0], got_2_qkv), extra)
-
-    slot = (z - jnp.arange(depth)) % depth
-    quarter_sums = jnp.take(jnp.concatenate(up_sums), slot, axis=0)
-    named = [
-        small_in[0], small_in[1], grad_b_qkv.reshape(-1), small_mid[3], freqs8[:2].reshape(-1),
-        small_mid[0], small_mid[1], small_mid[2], quarter_sums.reshape(-1),
-    ]
-    small = add_from(jnp.concatenate(named).reshape(-1, 128), "c")
-
-    part = jnp.concatenate([plane_qkv, part_b(rows, rows + width // slices)], 1).astype(BF)
+    plane_qkv = wide_sum(sum_low(kept_qkv[0], far_qkv[0], got_1_qkv[0], got_2_qkv), extra)
+    ff_total = plane_part(0, 0, rows) + sum_low(*ff_got)
+
+    sizes = [width, width, 3 * width, width, rope_freqs.size] + [width] * 3 + [b_up.size * depth]
+    small = add_from(small_in, "c")
+
+    part = plane_part(1, rows, rows + width // slices)
+    part = jnp.concatenate([plane_qkv, part], 1).astype(BF)
     thin = part.shape[0] // depth
     cut = lambda k: lax.dynamic_slice_in_dim(part, ((z + k) % depth) * thin, thin, 0)
     got = [send(cut(k), "n", ring(depth, k)) for k in range(1, depth)]
@@ -1291,22 +1312,19 @@
         small = add_from(small, "n", reach, depth)
         reach *= 2
     last, small = lax.optimization_barrier((last, small))
-    total_w_qkv, total_w_out, squares = assemble_call(
-        place, core_gather(pair, last), [query_key_value_weight.shape, output_weight.shape], depth
-    )
-    small, large_sq = small[:-8].reshape(-1), jnp.sum(small[-8:] + squares)
-
+    turned = sum(sizes[:4]) // 128
+    total_w_qkv, total_w_out, _, norms = assemble_call(
+        place, core_gather(pair, last), [query_key_value_weight.shape, output_weight.shape], depth,
+        small, (turned, turned + sizes[4] // 128),
+    )
+    small = small[:-8].reshape(-1)
     out, at = [], 0
-    for vector in named:
-        out.append(small[at : at + vector.size])
-        at += vector.size
+    for size in sizes:
+        out.append(small[at : at + size])
+        at += size
     t_gain1, t_shift1, t_b_qkv, t_b_out, t_freqs, t_gain2, t_shift2, t_b_down, t_up = out
     t_freqs = t_freqs.reshape(rope_freqs.shape)
-    rot_sq = jnp.sum(t_freqs * t_freqs)
-    skip = sum(v.size for v in named[:4])
-    lane = jnp.arange(small.size)
-    others = (lane < skip) | (lane >= skip + freqs8.shape[1] * 2)
-    other_sq = large_sq + jnp.sum(jnp.where(others, small * small, 0.0))
+    rot_sq, other_sq = norms[0, 0], norms[1, 0]
     t_b_up = lax.dynamic_slice_in_dim(t_up, z * b_up.shape[0], b_up.shape[0], 0)
     return (
         activations[None],

time: 343 us -> 325 us (0.948)
  waiting for transfers between devices: 58 us -> 52.4 us
    convert_element_type x7 -> x8, other arithmetic: 9.53 us -> 18.4 us  [the longest x1 3.79 us: on_device(): away = chip_sum(0, slice(1, None, 2)).astype(BF)]
    pallas_call x4 -> x3, Pallas kernels: 51.3 us -> 42.5 us  [the longest x1 23.3 us: middle_call(): pl.pallas_call(functools.partial(middle_kernel, slices=slices), in_specs=...]
    ppermute x50 -> x48, waiting for transfers between devices: 58 us -> 52.4 us  [send(): return lax.ppermute(x, axis, pairs)]
    pallas_call x1, Pallas kernels: 18 us -> 22.9 us  [backward_own_call(): pl.pallas_call(functools.partial(backward_own_kernel, first=first), grid=...]
    ppermute x50 -> x48, starting transfers between devices: 83.4 us -> 80 us  [send(): return lax.ppermute(x, axis, pairs)]
  transfers between devices with their start and end apart: 50 -> 48, of which waited for: 14 -> 14; matrix products, arithmetic and copies ran while one was open for 12% -> 12% of each run, Pallas kernels for 32% -> 30%
where the time goes in v3:
time: 325 us; the launch traced here: 320 us
  Pallas kernels  139 us (43%)
  starting transfers between devices  80 us (25%)
  waiting for transfers between devices  52.4 us (16%)
  other arithmetic  31.4 us (10%)
  local copies, waits for them, and re-layouts  15.6 us (5%)
    ppermute x48, starting transfers between devices, send(): return lax.ppermute(x, axis, pairs)  80 us
    ppermute x48, waiting for transfers between devices, send(): return lax.ppermute(x, axis, pairs)  52.4 us
    pallas_call x1, Pallas kernels, middle_call(): pl.pallas_call(functools.partial(middle_kernel, slices=slices), in_specs=...  23.3 us
    pallas_call x1, Pallas kernels, backward_own_call(): pl.pallas_call(functools.partial(backward_own_kernel, first=first), grid=...  22.9 us
    pallas_call x2, Pallas kernels, forward_call(): pl.pallas_call(functools.partial(forward_kernel, first=first, base=base),...  16 us
    pallas_call x2, Pallas kernels, assemble_call(): pl.pallas_call(functools.partial(assemble_kernel, split=split, outs=len(s...  14.2 us
    pallas_call x1, Pallas kernels, backward_halo_call(): pl.pallas_call(functools.partial(backward_halo_kernel, first=first), grid...  12 us
    pallas_call x1, Pallas kernels, halo_call(): pl.pallas_call(functools.partial(halo_kernel, which=which), grid=(4,), in...  12 us
  transfers between devices with their start and end apart: 48, of which 14 were waited for; matrix products, arithmetic and copies ran while one was open for 12% of the time, Pallas kernels for 30%

profile of v3, /device:TPU:1, one launch (start us, length us, event | category | flops | bytes accessed | tf_op | source)
XLA Modules:
  0.0 319.9 jit_solution(7390171785254331092)
XLA Ops:
  0.7 4.2 %collective-permute-start.4 = (bf16[512,768]{1,0:T(8,128)(2,1)}, bf16[512,768]{1,0:T(8,128)(2,1)S(1)}, u32[]{:S(2)}, u32[]{:S(2)}) collective-permute-start(bf16[512,768]{1,0:T(8,128)(2,1)} %bitcast.104), channel_id=1, source_target_pairs={{0,1},{1,2},{2,3},{4,5},{5,6},{6,7},{8,9},{9,10},{10,11},{12,13},{... | collective-permute-start | bytes 2359304 | tf_op jit(solution)/shard_map/ppermute | solution.py:1055
  7.2 5.0 %collective-permute-start.3 = (bf16[64,768]{1,0:T(8,128)(2,1)S(1)}, bf16[64,768]{1,0:T(8,128)(2,1)S(1)}, u32[]{:S(2)}, u32[]{:S(2)}) collective-permute-start(bf16[64,768]{1,0:T(8,128)(2,1)S(1)} %get-tuple-element.319), channel_id=1, source_target_pairs={{0,2},{1,3},{4,6},{5,7},{8,10},{9,11},{12,14},{13,15},{16,18},{17,... | collective-permute-start | bytes 294920 | tf_op jit(solution)/shard_map/ppermute | solution.py:1055
  22.4 1.7 fusion.hot_ref
  25.4 8.8 %qkv_own.1 = (bf16[1792,768]{1,0:T(8,128)(2,1)}, bf16[1792,768]{1,0:T(8,128)(2,1)}, bf16[1792,768]{1,0:T(8,128)(2,1)}, f32[512,768]{1,0:T(8,128)}, f32[512,768]{1,0:T(8,128)}, /*index=5*/bf16[768,2304]{1,0:T(8,128)(2,1)}) custom-call(bf16[512,768]{1,0:T(8,128)(2,1)} %bitcast.106, bf16[1792,128]{1,0:T(8,128)(2,1)} %fusion.hot_ref, f32[6,768]{1,0:T(8,128)} %stack.113.vec_ref, ...), custom_call_target="tpu_custom_call" | custom-call | flops 9200000000 | bytes 24000000 | tf_op jit(solution)/shard_map/qkv_own/pallas_call | solution.py:144
  34.8 3.0 collective-permute-start.1
  40.5 12.0 %halo.1 = (bf16[1792,768]{1,0:T(8,128)(2,1)}, bf16[1792,768]{1,0:T(8,128)(2,1)}, bf16[1792,768]{1,0:T(8,128)(2,1)}) custom-call(bf16[64,768]{1,0:T(8,128)(2,1)} %copy-done.35, bf16[512,768]{1,0:T(8,128)(2,1)} %copy-done.28, bf16[512,768]{1,0:T(8,128)(2,1)} %copy-done.29, ...), custom_call_target="tpu_custom_call", output_to_operand_aliasing={{0}: (9, {}), {1}: (10, {}), {2}: (11, {})} | custom-call | flops 13799999488 | bytes 36000000 | tf_op jit(solution)/shard_map/halo/pallas_call | solution.py:204
  52.5 8.0 %attention_forward.2 = (f32[512,768]{1,0:T(8,128)}, bf16[512,768]{1,0:T(8,128)(2,1)}, f32[3,4,1,512]{3,2,1,0:T(1,128)}) custom-call(s32[4,5]{1,0:T(4,128)} %stack.119.bound_ref, bf16[1792,768]{1,0:T(8,128)(2,1)} %get-tuple-element.130.q_ref, bf16[1792,768]{1,0:T(8,128)(2,1)} %get-tuple-element.131.k_ref, bf16[1792,768]{1,0:T(8,128)(2,1)} %get-tuple-element.132.v_ref, ...), custom_call_target="tpu_custom_call" | custom-call | flops 9200000000 | bytes 24000000 | tf_op jit(solution)/shard_map/attention_forward/pallas_call | solution.py:319
  60.8 3.0 collective-permute-start.7
  63.8 8.0 %attention_forward.3 = (f32[512,768]{1,0:T(8,128)}, bf16[512,768]{1,0:T(8,128)(2,1)}, f32[3,4,1,512]{3,2,1,0:T(1,128)}) custom-call(s32[4,5]{1,0:T(4,128)} %stack.119.bound_ref, bf16[1792,768]{1,0:T(8,128)(2,1)} %get-tuple-element.130.q_ref, bf16[1792,768]{1,0:T(8,128)(2,1)} %get-tuple-element.131.k_ref, ...), custom_call_target="tpu_custom_call", output_to_operand_aliasing={{0}: (6, {}), {1}: (7, {}), {2}: (8, {})} | custom-call | flops 9200000000 | bytes 24000000 | tf_op jit(solution)/shard_map/attention_forward/pallas_call | solution.py:319
  71.8 11.7 %middle_own.1 = (f32[512,768]{1,0:T(8,128)}, bf16[512,768]{1,0:T(8,128)(2,1)}, f32[512,768]{1,0:T(8,128)}, f32[512,768]{1,0:T(8,128)}, f32[1,768]{1,0:T(1,128)},...) custom-call(s32[2]{0:T(128)} %pad_add_fusion.1.place_ref, bf16[512,768]{1,0:T(8,128)(2,1)} %bitcast.107, ...), custom_call_target="tpu_custom_call" | custom-call | flops 13799999488 | bytes 36000000 | tf_op jit(solution)/shard_map/middle_own/pallas_call | solution.py:623
  83.5 1.8 collective-permute-done.8.refs_2_
  87.3 10.2 %collective-permute-done.9.refs_3_ = bf16[3,192,768]{2,1,0:T(8,128)(2,1)S(1)} collective-permute-done((bf16[3,192,768]{2,1,0:T(8,128)(2,1)S(1)}, bf16[3,192,768]{2,1,0:T(8,128)(2,1)S(1)}, u32[]{:S(2)}, u32[]{:S(2)}) %collective-permute-start.9) | collective-permute-done | bytes 884768 | tf_op jit(solution)/shard_map/ppermute | solution.py:1055
  97.5 1.8 collective-permute-start.13
  102.4 23.3 %middle.1 = (bf16[512,768]{1,0:T(8,128)(2,1)}, f32[512,768]{1,0:T(8,128)}, bf16[560,768]{1,0:T(8,128)(2,1)}, bf16[80,768]{1,0:T(8,128)(2,1)}, bf16[80,768]{1,0:T...) custom-call(s32[2]{0:T(128)} %pad_add_fusion.1.place_ref, ...), custom_call_target="tpu_custom_call" | custom-call | flops 23000000512 | bytes 60000000 | tf_op jit(solution)/shard_map/middle/pallas_call | solution.py:792
  127.4 5.3 %collective-permute-start.15 = (bf16[560,768]{1,0:T(8,128)(2,1)}, bf16[560,768]{1,0:T(8,128)(2,1)}, u32[]{:S(2)}, u32[]{:S(2)}) collective-permute-start(bf16[560,768]{1,0:T(8,128)(2,1)} %get-tuple-element.162.do_ref), channel_id=1, source_target_pairs={{0,1},{1,2},{2,3},{4,5},{5,6},{6,7},{8,9},{9,10},{10,11},{12,13},{... | collective-permute-start | bytes 2580488 | tf_op jit(solution)/shard_map/ppermute | solution.py:1055
  134.0 2.8 collective-permute-start.14
  138.1 3.8 %add_convert_fusion = bf16[2,576,768]{2,1,0:T(8,128)(2,1)} fusion(bf16[4,864,768]{2,1,0:T(8,128)(2,1)} %collective-permute-done.18, bf16[4,864,768]{2,1,0:T(8,128)(2,1)} %get-tuple-element.164), kind=kLoop, calls=%fused_computation | loop fusion | flops 3538944 | bytes 5308416 | tf_op jit(solution)/shard_map/convert_element_type | solution.py:1247
  141.9 22.9 %attention_backward_own.1 = (f32[512,768]{1,0:T(8,128)}, f32[512,768]{1,0:T(8,128)}, f32[512,768]{1,0:T(8,128)}) custom-call(s32[4,5]{1,0:T(4,128)} %stack.119.bound_ref, bf16[1792,768]{1,0:T(8,128)(2,1)} %get-tuple-element.130.q_ref, bf16[560,768]{1,0:T(8,128)(2,1)} %get-tuple-element.162.do_ref, bf16[1792,768]{1,0:T(8,128)(2,1)} %get-tuple-element.131.k_ref, ...), custom_call_target="tpu_custom_call" | custom-call | flops 23000000512 | bytes 60000000 | tf_op jit(solution)/shard_map/attention_backward_own/pallas_call | solution.py:407
  164.8 2.3 add_convert_fusion.2
  168.7 3.2 %collective-permute-start.21 = (bf16[576,768]{1,0:T(8,128)(2,1)S(1)}, bf16[576,768]{1,0:T(8,128)(2,1)}, u32[]{:S(2)}, u32[]{:S(2)}) collective-permute-start(bf16[576,768]{1,0:T(8,128)(2,1)S(1)} %fusion.1), channel_id=1, source_target_pairs={{0,16},{4,12},{8,24},{12,4},{16,0},{20,28},{24,8},{28,20},{1,17},{... | collective-permute-start | bytes 2654216 | tf_op jit(solution)/shard_map/ppermute | solution.py:1055
  172.5 12.0 %attention_backward_halo.1 = (f32[512,768]{1,0:T(8,128)}, f32[512,768]{1,0:T(8,128)}) custom-call(s32[14,2]{1,0:T(8,128)} %copy.93.bound_ref, bf16[1792,768]{1,0:T(8,128)(2,1)} %get-tuple-element.130.q_ref, bf16[80,768]{1,0:T(8,128)(2,1)} %copy-done.33, bf16[560,768]{1,0:T(8,128)(2,1)} %collective-permute-done.15.near_l, ...), custom_call_target="tpu_custom_call" | custom-call | flops 12650000384 | bytes 33000000 | tf_op jit(solution)/shard_map/attention_backward_halo/pallas_call | solution.py:495
  184.6 7.6 %collective-permute-done.21 = bf16[576,768]{1,0:T(8,128)(2,1)} collective-permute-done((bf16[576,768]{1,0:T(8,128)(2,1)S(1)}, bf16[576,768]{1,0:T(8,128)(2,1)}, u32[]{:S(2)}, u32[]{:S(2)}) %collective-permute-start.21) | collective-permute-done | bytes 884768 | tf_op jit(solution)/shard_map/ppermute | solution.py:1055
  192.1 2.3 fusion.5
  194.4 2.1 fusion.7
  196.5 10.6 %turn_back.1 = (bf16[3,512,768]{2,1,0:T(8,128)(2,1)}, f32[3,768]{1,0:T(4,128)}, f32[8,384]{1,0:T(8,128)}, bf16[4,96,2304]{2,1,0:T(8,128)(2,1)}, bf16[4,96,2304]{2,1,0:T(8,128)(2,1)}) custom-call(s32[2]{0:T(128)} %pad_add_fusion.1.place_ref, bf16[512,768]{1,0:T(8,128)(2,1)} %bitcast.108, f32[6,768]{1,0:T(8,128)} %stack.113.vec_ref, ...), custom_call_target="tpu_custom_call" | custom-call | flops 10350000128 | bytes 27000000 | tf_op jit(solution)/shard_map/turn_back/pallas_call | solution.py:887
  207.8 7.6 %collective-permute-start.30 = (bf16[192,768]{1,0:T(8,128)(2,1)}, bf16[192,768]{1,0:T(8,128)(2,1)}, u32[]{:S(2)}, u32[]{:S(2)}) collective-permute-start(bf16[192,768]{1,0:T(8,128)(2,1)} %get-tuple-element.316), channel_id=1, source_target_pairs={{0,2},{1,3},{2,0},{3,1},{4,6},{5,7},{6,4},{7,5},{8,10},{9,11},{10,... | collective-permute-start | bytes 884744 | tf_op jit(solution)/shard_map/ppermute | solution.py:1055
  215.3 3.0 add_convert_fusion.1
  219.0 2.1 fusion.4
  221.1 1.6 collective-permute-start.31
  222.7 7.2 %input_grad.1 = (f32[512,768]{1,0:T(8,128)}, f32[84,128]{1,0:T(8,128)}) custom-call(s32[2]{0:T(128)} %pad_add_fusion.1.place_ref, bf16[512,768]{1,0:T(8,128)(2,1)} %bitcast.109, f32[6,768]{1,0:T(8,128)} %stack.113.vec_ref, bf16[3,512,768]{2,1,0:T(8,128)(2,1)} %get-tuple-element.192.d_ref, bf16[768,2304]{1,0:T(8,128)(2,1)} %w_ref.3, ...), custom_call_target="tpu_custom_call" | custom-call | flops 8049999872 | bytes 21000000 | tf_op jit(solution)/shard_map/input_grad/pallas_call | solution.py:949
  232.0 1.6 collective-permute-start.25
  233.6 7.2 %collective-permute-done.30 = bf16[192,768]{1,0:T(8,128)(2,1)} collective-permute-done((bf16[192,768]{1,0:T(8,128)(2,1)}, bf16[192,768]{1,0:T(8,128)(2,1)}, u32[]{:S(2)}, u32[]{:S(2)}) %collective-permute-start.30) | collective-permute-done | bytes 294944 | tf_op jit(solution)/shard_map/ppermute | solution.py:1055
  240.9 1.7 collective-permute-start.32
  244.7 1.6 collective-permute-done.33
  248.8 3.2 collective-permute-start.28
  252.0 1.6 fusion.3
  254.7 5.3 %collective-permute-done.27 = bf16[24,3072]{1,0:T(8,128)(2,1)S(1)} collective-permute-done((bf16[24,3072]{1,0:T(8,128)(2,1)S(1)}, bf16[24,3072]{1,0:T(8,128)(2,1)S(1)}, u32[]{:S(2)}, u32[]{:S(2)}) %collective-permute-start.27) | collective-permute-done | bytes 147488 | tf_op jit(solution)/shard_map/ppermute | solution.py:1055
  260.9 4.4 %collective-permute-start.35 = (bf16[24,3072]{1,0:T(8,128)(2,1)S(1)}, bf16[24,3072]{1,0:T(8,128)(2,1)S(1)}, u32[]{:S(2)}, u32[]{:S(2)}) collective-permute-start(bf16[24,3072]{1,0:T(8,128)(2,1)S(1)} %add_convert_fusion.6), channel_id=1, source_target_pairs={{0,1},{1,2},{2,3},{3,0},{4,5},{5,6},{6,7},{7,4},{8,9},{9,10},{10,1... | collective-permute-start | bytes 442376 | tf_op jit(solution)/shard_map/ppermute | solution.py:1055
  265.3 2.1 collective-permute-start.37
  268.1 7.8 %collective-permute-done.36 = bf16[24,3072]{1,0:T(8,128)(2,1)S(1)} collective-permute-done((bf16[24,3072]{1,0:T(8,128)(2,1)S(1)}, bf16[24,3072]{1,0:T(8,128)(2,1)S(1)}, u32[]{:S(2)}, u32[]{:S(2)}) %collective-permute-start.36) | collective-permute-done | bytes 147488 | tf_op jit(solution)/shard_map/ppermute | solution.py:1055
  278.4 2.8 collective-permute-start.43
  281.2 5.0 %collective-permute-done.38 = bf16[4,24,3072]{2,1,0:T(8,128)(2,1)S(1)} collective-permute-done((bf16[4,24,3072]{2,1,0:T(8,128)(2,1)S(1)}, bf16[4,24,3072]{2,1,0:T(8,128)(2,1)S(1)}, u32[]{:S(2)}, u32[]{:S(2)}) %collective-permute-start.38) | collective-permute-done | bytes 589856 | tf_op jit(solution)/shard_map/ppermute | solution.py:1055
  289.3 6.1 %assemble.2 = (f32[768,768]{1,0:T(8,128)}, f32[768,768]{1,0:T(8,128)}, f32[8,128]{1,0:T(8,128)}) custom-call(s32[2]{0:T(128)} %pad_add_fusion.1.place_ref, bf16[2,192,768]{2,1,0:T(8,128)(2,1)} %copy-done.3, bf16[2,192,768]{2,1,0:T(8,128)(2,1)} %copy-done.30, bf16[2,192,768]{2,1,0:T(8,128)(2,1)} %copy-done.31, bf16[2,192,768]{2,1,0:T(8,128)(2,1)} %copy-done.32), custom_call_target="tpu_custom_call" | custom-call | flops 6899999744 | bytes 18000000 | tf_op jit(solution)/shard_map/assemble/pallas_call | solution.py:1038
  296.1 2.4 collective-permute-start.44
  298.4 1.8 collective-permute-done.44
  301.3 3.3 %collective-permute-start.46 = (bf16[2,4,24,3072]{3,2,1,0:T(8,128)(2,1)S(1)}, bf16[2,4,24,3072]{3,2,1,0:T(8,128)(2,1)}, u32[]{:S(2)}, u32[]{:S(2)}) collective-permute-start(bf16[2,4,24,3072]{3,2,1,0:T(8,128)(2,1)S(1)} %pad_maximum_fusion.1.refs_0_), channel_id=1, source_target_pairs={{0,4},{4,0},{1,5},{5,1},{2,6},{6,2},{3,7},{7,3},{8,12},{12,8},{9,1... | collective-permute-start | bytes 3538952 | tf_op jit(solution)/shard_map/ppermute | solution.py:1055
  304.8 3.1 collective-permute-start.47
  310.5 8.1 %assemble.3 = (f32[768,2304]{1,0:T(8,128)}, f32[768,768]{1,0:T(8,128)}, f32[8,128]{1,0:T(8,128)}, f32[2,128]{1,0:T(2,128)}) custom-call(s32[2]{0:T(128)} %pad_add_fusion.1.place_ref, bf16[2,4,24,3072]{3,2,1,0:T(8,128)(2,1)} %copy-done.1, bf16[2,4,24,3072]{3,2,1,0:T(8,128)(2,1)} %copy-done.20, bf16[2,4,24,3072]{3,2,1,0:T(8,128)(2,1)} %collective-permute-done.46.refs_2_, ...), custom_call_target="tpu_custom_call" | custom-call | flops 6899999744 | bytes 18000000 | tf_op jit(solution)/shard_map/assemble/pallas_call | solution.py:1038
  (244 shorter events, 50.4 us)
Async XLA Ops:
  0.7 38.3 %collective-permute-start.4 = (bf16[512,768]{1,0:T(8,128)(2,1)}, bf16[512,768]{1,0:T(8,128)(2,1)S(1)}, u32[]{:S(2)}, u32[]{:S(2)}) collective-permute-start(bf16[512,768]{1,0:T(8,128)(2,1)} %bitcast.104), channel_id=1, source_target_pairs={{0,1},{1,2},{2,3},{4,5},{5,6},{6,7},{8,9},{9,10},{10,11},{12,13},{... | collective-permute-start | bytes 2359304 | tf_op jit(solution)/shard_map/ppermute | solution.py:1055
  4.9 34.1 %collective-permute-start.5 = (bf16[512,768]{1,0:T(8,128)(2,1)}, bf16[512,768]{1,0:T(8,128)(2,1)S(1)}, u32[]{:S(2)}, u32[]{:S(2)}) collective-permute-start(bf16[512,768]{1,0:T(8,128)(2,1)} %bitcast.105), channel_id=1, source_target_pairs={{1,0},{2,1},{3,2},{5,4},{6,5},{7,6},{9,8},{10,9},{11,10},{13,12},{... | collective-permute-start | bytes 2359304 | tf_op jit(solution)/shard_map/ppermute | solution.py:1055
  7.2 27.6 %collective-permute-start.3 = (bf16[64,768]{1,0:T(8,128)(2,1)S(1)}, bf16[64,768]{1,0:T(8,128)(2,1)S(1)}, u32[]{:S(2)}, u32[]{:S(2)}) collective-permute-start(bf16[64,768]{1,0:T(8,128)(2,1)S(1)} %get-tuple-element.319), channel_id=1, source_target_pairs={{0,2},{1,3},{4,6},{5,7},{8,10},{9,11},{12,14},{13,15},{16,18},{17,... | collective-permute-start | bytes 294920 | tf_op jit(solution)/shard_map/ppermute | solution.py:1055
  12.2 25.7 %collective-permute-start.6 = (bf16[64,768]{1,0:T(8,128)(2,1)S(1)}, bf16[64,768]{1,0:T(8,128)(2,1)S(1)}, u32[]{:S(2)}, u32[]{:S(2)}) collective-permute-start(bf16[64,768]{1,0:T(8,128)(2,1)S(1)} %get-tuple-element.318), channel_id=1, source_target_pairs={{2,0},{3,1},{6,4},{7,5},{10,8},{11,9},{14,12},{15,13},{18,16},{19,... | collective-permute-start | bytes 294920 | tf_op jit(solution)/shard_map/ppermute | solution.py:1055
  15.6 44.9 %collective-permute-start = (bf16[208,768]{1,0:T(8,128)(2,1)S(1)}, bf16[208,768]{1,0:T(8,128)(2,1)S(1)}, u32[]{:S(2)}, u32[]{:S(2)}) collective-permute-start(bf16[208,768]{1,0:T(8,128)(2,1)S(1)} %pad_maximum_fusion.5), channel_id=1, source_target_pairs={{0,1},{1,2},{2,3},{3,0},{4,5},{5,6},{6,7},{7,4},{8,9},{9,10},{10,1... | collective-permute-start | bytes 958472 | tf_op jit(solution)/shard_map/ppermute | solution.py:1055
  34.8 25.7 %collective-permute-start.1 = (bf16[208,768]{1,0:T(8,128)(2,1)S(1)}, bf16[208,768]{1,0:T(8,128)(2,1)S(1)}, u32[]{:S(2)}, u32[]{:S(2)}) collective-permute-start(bf16[208,768]{1,0:T(8,128)(2,1)S(1)} %pad_maximum_fusion.5), channel_id=1, source_target_pairs={{0,2},{1,3},{2,0},{3,1},{4,6},{5,7},{6,4},{7,5},{8,10},{9,11},{10,... | collective-permute-start | bytes 958472 | tf_op jit(solution)/shard_map/ppermute | solution.py:1055
  37.8 22.7 %collective-permute-start.2 = (bf16[208,768]{1,0:T(8,128)(2,1)S(1)}, bf16[208,768]{1,0:T(8,128)(2,1)S(1)}, u32[]{:S(2)}, u32[]{:S(2)}) collective-permute-start(bf16[208,768]{1,0:T(8,128)(2,1)S(1)} %pad_maximum_fusion.5), channel_id=1, source_target_pairs={{0,3},{1,0},{2,1},{3,2},{4,7},{5,4},{6,5},{7,6},{8,11},{9,8},{10,9... | collective-permute-start | bytes 958472 | tf_op jit(solution)/shard_map/ppermute | solution.py:1055
  60.8 22.7 %collective-permute-start.7 = (bf16[3,192,768]{2,1,0:T(8,128)(2,1)S(1)}, bf16[3,192,768]{2,1,0:T(8,128)(2,1)S(1)}, u32[]{:S(2)}, u32[]{:S(2)}) collective-permute-start(bf16[3,192,768]{2,1,0:T(8,128)(2,1)S(1)} %pad_maximum_fusion.2.refs_0_), channel_id=1, source_target_pairs={{0,8},{4,20},{8,0},{12,28},{16,24},{20,4},{24,16},{28,12},{1,9},{5... | collective-permute-start | bytes 2654216 | tf_op jit(solution)/shard_map/ppermute | solution.py:1055
  63.8 21.5 %collective-permute-start.8 = (bf16[3,192,768]{2,1,0:T(8,128)(2,1)S(1)}, bf16[3,192,768]{2,1,0:T(8,128)(2,1)S(1)}, u32[]{:S(2)}, u32[]{:S(2)}) collective-permute-start(bf16[3,192,768]{2,1,0:T(8,128)(2,1)S(1)} %pad_maximum_fusion.2.refs_0_), channel_id=1, source_target_pairs={{0,16},{4,12},{8,24},{12,4},{16,0},{20,28},{24,8},{28,20},{1,17},{... | collective-permute-start | bytes 2654216 | tf_op jit(solution)/shard_map/ppermute | solution.py:1055
  85.3 12.2 %collective-permute-start.9 = (bf16[3,192,768]{2,1,0:T(8,128)(2,1)S(1)}, bf16[3,192,768]{2,1,0:T(8,128)(2,1)S(1)}, u32[]{:S(2)}, u32[]{:S(2)}) collective-permute-start(bf16[3,192,768]{2,1,0:T(8,128)(2,1)S(1)} %collective-permute-done.7.refs_1_), channel_id=1, source_target_pairs={{0,16},{4,12},{8,24},{12,4},{16,0},{20,28},{24,8},{28,20},{1,17},{... | collective-permute-start | bytes 2654216 | tf_op jit(solution)/shard_map/ppermute | solution.py:1055
  86.8 13.4 %collective-permute-start.10 = (bf16[3,192,768]{2,1,0:T(8,128)(2,1)S(1)}, bf16[3,192,768]{2,1,0:T(8,128)(2,1)S(1)}, u32[]{:S(2)}, u32[]{:S(2)}) collective-permute-start(bf16[3,192,768]{2,1,0:T(8,128)(2,1)S(1)} %pad_maximum_fusion.2.refs_0_), channel_id=1, source_target_pairs={{0,4},{4,0},{1,5},{5,1},{2,6},{6,2},{3,7},{7,3},{8,12},{12,8},{9,1... | collective-permute-start | bytes 2654216 | tf_op jit(solution)/shard_map/ppermute | solution.py:1055
  86.8 13.4 %collective-permute-start.11 = (bf16[3,192,768]{2,1,0:T(8,128)(2,1)S(1)}, bf16[3,192,768]{2,1,0:T(8,128)(2,1)S(1)}, u32[]{:S(2)}, u32[]{:S(2)}) collective-permute-start(bf16[3,192,768]{2,1,0:T(8,128)(2,1)S(1)} %collective-permute-done.7.refs_1_), channel_id=1, source_target_pairs={{0,4},{4,0},{1,5},{5,1},{2,6},{6,2},{3,7},{7,3},{8,12},{12,8},{9,1... | collective-permute-start | bytes 2654216 | tf_op jit(solution)/shard_map/ppermute | solution.py:1055
  87.3 12.9 %collective-permute-start.12 = (bf16[3,192,768]{2,1,0:T(8,128)(2,1)S(1)}, bf16[3,192,768]{2,1,0:T(8,128)(2,1)S(1)}, u32[]{:S(2)}, u32[]{:S(2)}) collective-permute-start(bf16[3,192,768]{2,1,0:T(8,128)(2,1)S(1)} %collective-permute-done.8.refs_2_), channel_id=1, source_target_pairs={{0,4},{4,0},{1,5},{5,1},{2,6},{6,2},{3,7},{7,3},{8,12},{12,8},{9,1... | collective-permute-start | bytes 2654216 | tf_op jit(solution)/shard_map/ppermute | solution.py:1055
  97.5 3.8 %collective-permute-start.13 = (bf16[3,192,768]{2,1,0:T(8,128)(2,1)S(1)}, bf16[3,192,768]{2,1,0:T(8,128)(2,1)S(1)}, u32[]{:S(2)}, u32[]{:S(2)}) collective-permute-start(bf16[3,192,768]{2,1,0:T(8,128)(2,1)S(1)} %collective-permute-done.9.refs_3_), channel_id=1, source_target_pairs={{0,4},{4,0},{1,5},{5,1},{2,6},{6,2},{3,7},{7,3},{8,12},{12,8},{9,1... | collective-permute-start | bytes 2654216 | tf_op jit(solution)/shard_map/ppermute | solution.py:1055
  125.7 12.5 %collective-permute-start.18 = (bf16[4,864,768]{2,1,0:T(8,128)(2,1)}, bf16[4,864,768]{2,1,0:T(8,128)(2,1)}, u32[]{:S(2)}, u32[]{:S(2)}) collective-permute-start(bf16[4,864,768]{2,1,0:T(8,128)(2,1)} %get-tuple-element.165), channel_id=1, source_target_pairs={{0,4},{4,0},{1,5},{5,1},{2,6},{6,2},{3,7},{7,3},{8,12},{12,8},{9,1... | collective-permute-start | bytes 15925256 | tf_op jit(solution)/shard_map/ppermute | solution.py:1055
  127.4 44.5 %collective-permute-start.15 = (bf16[560,768]{1,0:T(8,128)(2,1)}, bf16[560,768]{1,0:T(8,128)(2,1)}, u32[]{:S(2)}, u32[]{:S(2)}) collective-permute-start(bf16[560,768]{1,0:T(8,128)(2,1)} %get-tuple-element.162.do_ref), channel_id=1, source_target_pairs={{0,1},{1,2},{2,3},{4,5},{5,6},{6,7},{8,9},{9,10},{10,11},{12,13},{... | collective-permute-start | bytes 2580488 | tf_op jit(solution)/shard_map/ppermute | solution.py:1055
  132.7 39.2 %collective-permute-start.16 = (bf16[560,768]{1,0:T(8,128)(2,1)}, bf16[560,768]{1,0:T(8,128)(2,1)}, u32[]{:S(2)}, u32[]{:S(2)}) collective-permute-start(bf16[560,768]{1,0:T(8,128)(2,1)} %get-tuple-element.162.do_ref), channel_id=1, source_target_pairs={{1,0},{2,1},{3,2},{5,4},{6,5},{7,6},{9,8},{10,9},{11,10},{13,12},{... | collective-permute-start | bytes 2580488 | tf_op jit(solution)/shard_map/ppermute | solution.py:1055
  134.0 34.6 %collective-permute-start.14 = (bf16[80,768]{1,0:T(8,128)(2,1)}, bf16[80,768]{1,0:T(8,128)(2,1)S(1)}, u32[]{:S(2)}, u32[]{:S(2)}) collective-permute-start(bf16[80,768]{1,0:T(8,128)(2,1)} %get-tuple-element.161), channel_id=1, source_target_pairs={{0,2},{1,3},{4,6},{5,7},{8,10},{9,11},{12,14},{13,15},{16,18},{17,... | collective-permute-start | bytes 368648 | tf_op jit(solution)/shard_map/ppermute | solution.py:1055
  136.8 35.1 %collective-permute-start.17 = (bf16[80,768]{1,0:T(8,128)(2,1)}, bf16[80,768]{1,0:T(8,128)(2,1)S(1)}, u32[]{:S(2)}, u32[]{:S(2)}) collective-permute-start(bf16[80,768]{1,0:T(8,128)(2,1)} %get-tuple-element.163), channel_id=1, source_target_pairs={{2,0},{3,1},{6,4},{7,5},{10,8},{11,9},{14,12},{15,13},{18,16},{19,... | collective-permute-start | bytes 368648 | tf_op jit(solution)/shard_map/ppermute | solution.py:1055
  141.9 25.2 %collective-permute-start.19 = (bf16[2,576,768]{2,1,0:T(8,128)(2,1)}, bf16[2,576,768]{2,1,0:T(8,128)(2,1)S(1)}, u32[]{:S(2)}, u32[]{:S(2)}) collective-permute-start(bf16[2,576,768]{2,1,0:T(8,128)(2,1)} %add_convert_fusion), channel_id=1, source_target_pairs={{0,8},{4,20},{8,0},{12,28},{16,24},{20,4},{24,16},{28,12},{1,9},{5... | collective-permute-start | bytes 5308424 | tf_op jit(solution)/shard_map/ppermute | solution.py:1055
  167.1 17.4 %collective-permute-start.20 = (bf16[2,288,768]{2,1,0:T(8,128)(2,1)}, bf16[2,288,768]{2,1,0:T(8,128)(2,1)}, u32[]{:S(2)}, u32[]{:S(2)}) collective-permute-start(bf16[2,288,768]{2,1,0:T(8,128)(2,1)} %add_convert_fusion.2), channel_id=1, source_target_pairs={{0,8},{4,20},{8,0},{12,28},{16,24},{20,4},{24,16},{28,12},{1,9},{5... | collective-permute-start | bytes 2654216 | tf_op jit(solution)/shard_map/ppermute | solution.py:1055
  168.7 23.5 %collective-permute-start.21 = (bf16[576,768]{1,0:T(8,128)(2,1)S(1)}, bf16[576,768]{1,0:T(8,128)(2,1)}, u32[]{:S(2)}, u32[]{:S(2)}) collective-permute-start(bf16[576,768]{1,0:T(8,128)(2,1)S(1)} %fusion.1), channel_id=1, source_target_pairs={{0,16},{4,12},{8,24},{12,4},{16,0},{20,28},{24,8},{28,20},{1,17},{... | collective-permute-start | bytes 2654216 | tf_op jit(solution)/shard_map/ppermute | solution.py:1055
  207.2 8.1 %collective-permute-start.23 = (bf16[4,96,2304]{2,1,0:T(8,128)(2,1)}, bf16[4,96,2304]{2,1,0:T(8,128)(2,1)S(1)}, u32[]{:S(2)}, u32[]{:S(2)}) collective-permute-start(bf16[4,96,2304]{2,1,0:T(8,128)(2,1)} %get-tuple-element.190), channel_id=1, source_target_pairs={{0,4},{4,0},{1,5},{5,1},{2,6},{6,2},{3,7},{7,3},{8,12},{12,8},{9,1... | collective-permute-start | bytes 5308424 | tf_op jit(solution)/shard_map/ppermute | solution.py:1055
  207.7 11.3 %collective-permute-start.22 = (bf16[288,768]{1,0:T(8,128)(2,1)}, bf16[288,768]{1,0:T(8,128)(2,1)S(1)}, u32[]{:S(2)}, u32[]{:S(2)}) collective-permute-start(bf16[288,768]{1,0:T(8,128)(2,1)} %fusion.7), channel_id=1, source_target_pairs={{0,16},{4,12},{8,24},{12,4},{16,0},{20,28},{24,8},{28,20},{1,17},{... | collective-permute-start | bytes 1327112 | tf_op jit(solution)/shard_map/ppermute | solution.py:1055
  207.7 25.9 %collective-permute-start.29 = (bf16[192,768]{1,0:T(8,128)(2,1)}, bf16[192,768]{1,0:T(8,128)(2,1)S(1)}, u32[]{:S(2)}, u32[]{:S(2)}) collective-permute-start(bf16[192,768]{1,0:T(8,128)(2,1)} %get-tuple-element.317), channel_id=1, source_target_pairs={{0,3},{1,0},{2,1},{3,2},{4,7},{5,4},{6,5},{7,6},{8,11},{9,8},{10,9... | collective-permute-start | bytes 884744 | tf_op jit(solution)/shard_map/ppermute | solution.py:1055
  207.8 33.1 %collective-permute-start.30 = (bf16[192,768]{1,0:T(8,128)(2,1)}, bf16[192,768]{1,0:T(8,128)(2,1)}, u32[]{:S(2)}, u32[]{:S(2)}) collective-permute-start(bf16[192,768]{1,0:T(8,128)(2,1)} %get-tuple-element.316), channel_id=1, source_target_pairs={{0,2},{1,3},{2,0},{3,1},{4,6},{5,7},{6,4},{7,5},{8,10},{9,11},{10,... | collective-permute-start | bytes 884744 | tf_op jit(solution)/shard_map/ppermute | solution.py:1055
  218.3 12.4 %collective-permute-start.24 = (bf16[2,96,2304]{2,1,0:T(8,128)(2,1)}, bf16[2,96,2304]{2,1,0:T(8,128)(2,1)S(1)}, u32[]{:S(2)}, u32[]{:S(2)}) collective-permute-start(bf16[2,96,2304]{2,1,0:T(8,128)(2,1)} %add_convert_fusion.1), channel_id=1, source_target_pairs={{0,8},{4,20},{8,0},{12,28},{16,24},{20,4},{24,16},{28,12},{1,9},{5... | collective-permute-start | bytes 2654216 | tf_op jit(solution)/shard_map/ppermute | solution.py:1055
  221.1 19.8 %collective-permute-start.31 = (bf16[192,768]{1,0:T(8,128)(2,1)}, bf16[192,768]{1,0:T(8,128)(2,1)}, u32[]{:S(2)}, u32[]{:S(2)}) collective-permute-start(bf16[192,768]{1,0:T(8,128)(2,1)} %fusion.4), channel_id=1, source_target_pairs={{0,1},{1,2},{2,3},{3,0},{4,5},{5,6},{6,7},{7,4},{8,9},{9,10},{10,1... | collective-permute-start | bytes 884744 | tf_op jit(solution)/shard_map/ppermute | solution.py:1055
  232.0 15.1 %collective-permute-start.25 = (bf16[96,2304]{1,0:T(8,128)(2,1)S(1)}, bf16[96,2304]{1,0:T(8,128)(2,1)}, u32[]{:S(2)}, u32[]{:S(2)}) collective-permute-start(bf16[96,2304]{1,0:T(8,128)(2,1)S(1)} %fusion.8), channel_id=1, source_target_pairs={{0,16},{4,12},{8,24},{12,4},{16,0},{20,28},{24,8},{28,20},{1,17},{... | collective-permute-start | bytes 1327112 | tf_op jit(solution)/shard_map/ppermute | solution.py:1055
  240.9 2.6 collective-permute-start.32
  243.5 2.9 collective-permute-start.33
  246.4 7.2 %collective-permute-start.34 = (f32[84,128]{1,0:T(8,128)S(1)}, f32[84,128]{1,0:T(8,128)S(1)}, u32[]{:S(2)}, u32[]{:S(2)}) collective-permute-start(f32[84,128]{1,0:T(8,128)S(1)} %add.364), channel_id=1, source_target_pairs={{0,16},{16,0},{1,17},{17,1},{2,18},{18,2},{3,19},{19,3},{4,20},{20... | collective-permute-start | bytes 129032 | tf_op jit(solution)/shard_map/ppermute | solution.py:1055
  248.7 6.1 %collective-permute-start.26 = (bf16[24,3072]{1,0:T(8,128)(2,1)S(1)}, bf16[24,3072]{1,0:T(8,128)(2,1)S(1)}, u32[]{:S(2)}, u32[]{:S(2)}) collective-permute-start(bf16[24,3072]{1,0:T(8,128)(2,1)S(1)} %get-tuple-element.323), channel_id=1, source_target_pairs={{0,1},{1,2},{2,3},{3,0},{4,5},{5,6},{6,7},{7,4},{8,9},{9,10},{10,1... | collective-permute-start | bytes 442376 | tf_op jit(solution)/shard_map/ppermute | solution.py:1055
  248.7 11.2 %collective-permute-start.27 = (bf16[24,3072]{1,0:T(8,128)(2,1)S(1)}, bf16[24,3072]{1,0:T(8,128)(2,1)S(1)}, u32[]{:S(2)}, u32[]{:S(2)}) collective-permute-start(bf16[24,3072]{1,0:T(8,128)(2,1)S(1)} %get-tuple-element.324), channel_id=1, source_target_pairs={{0,2},{1,3},{2,0},{3,1},{4,6},{5,7},{6,4},{7,5},{8,10},{9,11},{10,... | collective-permute-start | bytes 442376 | tf_op jit(solution)/shard_map/ppermute | solution.py:1055
  248.8 11.2 %collective-permute-start.28 = (bf16[24,3072]{1,0:T(8,128)(2,1)S(1)}, bf16[24,3072]{1,0:T(8,128)(2,1)S(1)}, u32[]{:S(2)}, u32[]{:S(2)}) collective-permute-start(bf16[24,3072]{1,0:T(8,128)(2,1)S(1)} %get-tuple-element.322), channel_id=1, source_target_pairs={{0,3},{1,0},{2,1},{3,2},{4,7},{5,4},{6,5},{7,6},{8,11},{9,8},{10,9... | collective-permute-start | bytes 442376 | tf_op jit(solution)/shard_map/ppermute | solution.py:1055
  260.1 7.3 %collective-permute-start.40 = (bf16[192,768]{1,0:T(8,128)(2,1)S(1)}, bf16[192,768]{1,0:T(8,128)(2,1)S(1)}, u32[]{:S(2)}, u32[]{:S(2)}) collective-permute-start(bf16[192,768]{1,0:T(8,128)(2,1)S(1)} %fusion.3), channel_id=1, source_target_pairs={{0,8},{4,20},{8,0},{12,28},{16,24},{20,4},{24,16},{28,12},{1,9},{5... | collective-permute-start | bytes 884744 | tf_op jit(solution)/shard_map/ppermute | solution.py:1055
  260.9 7.2 %collective-permute-start.35 = (bf16[24,3072]{1,0:T(8,128)(2,1)S(1)}, bf16[24,3072]{1,0:T(8,128)(2,1)S(1)}, u32[]{:S(2)}, u32[]{:S(2)}) collective-permute-start(bf16[24,3072]{1,0:T(8,128)(2,1)S(1)} %add_convert_fusion.6), channel_id=1, source_target_pairs={{0,1},{1,2},{2,3},{3,0},{4,5},{5,6},{6,7},{7,4},{8,9},{9,10},{10,1... | collective-permute-start | bytes 442376 | tf_op jit(solution)/shard_map/ppermute | solution.py:1055
  265.3 10.6 %collective-permute-start.36 = (bf16[24,3072]{1,0:T(8,128)(2,1)S(1)}, bf16[24,3072]{1,0:T(8,128)(2,1)S(1)}, u32[]{:S(2)}, u32[]{:S(2)}) collective-permute-start(bf16[24,3072]{1,0:T(8,128)(2,1)S(1)} %add_convert_fusion.6), channel_id=1, source_target_pairs={{0,2},{1,3},{2,0},{3,1},{4,6},{5,7},{6,4},{7,5},{8,10},{9,11},{10,... | collective-permute-start | bytes 442376 | tf_op jit(solution)/shard_map/ppermute | solution.py:1055
  265.3 10.6 %collective-permute-start.37 = (bf16[24,3072]{1,0:T(8,128)(2,1)S(1)}, bf16[24,3072]{1,0:T(8,128)(2,1)S(1)}, u32[]{:S(2)}, u32[]{:S(2)}) collective-permute-start(bf16[24,3072]{1,0:T(8,128)(2,1)S(1)} %add_convert_fusion.6), channel_id=1, source_target_pairs={{0,3},{1,0},{2,1},{3,2},{4,7},{5,4},{6,5},{7,6},{8,11},{9,8},{10,9... | collective-permute-start | bytes 442376 | tf_op jit(solution)/shard_map/ppermute | solution.py:1055
  267.5 10.9 %collective-permute-start.41 = (bf16[2,192,768]{2,1,0:T(8,128)(2,1)S(1)}, bf16[2,192,768]{2,1,0:T(8,128)(2,1)S(1)}, u32[]{:S(2)}, u32[]{:S(2)}) collective-permute-start(bf16[2,192,768]{2,1,0:T(8,128)(2,1)S(1)} %pad_maximum_fusion.4.refs_0_), channel_id=1, source_target_pairs={{0,16},{4,12},{8,24},{12,4},{16,0},{20,28},{24,8},{28,20},{1,17},{... | collective-permute-start | bytes 1769480 | tf_op jit(solution)/shard_map/ppermute | solution.py:1055
  276.0 10.1 %collective-permute-start.38 = (bf16[4,24,3072]{2,1,0:T(8,128)(2,1)S(1)}, bf16[4,24,3072]{2,1,0:T(8,128)(2,1)S(1)}, u32[]{:S(2)}, u32[]{:S(2)}) collective-permute-start(bf16[4,24,3072]{2,1,0:T(8,128)(2,1)S(1)} %get-tuple-element.321), channel_id=1, source_target_pairs={{0,8},{4,20},{8,0},{12,28},{16,24},{20,4},{24,16},{28,12},{1,9},{5... | collective-permute-start | bytes 1769480 | tf_op jit(solution)/shard_map/ppermute | solution.py:1055
  277.3 10.3 %collective-permute-start.42 = (bf16[2,192,768]{2,1,0:T(8,128)(2,1)S(1)}, bf16[2,192,768]{2,1,0:T(8,128)(2,1)S(1)}, u32[]{:S(2)}, u32[]{:S(2)}) collective-permute-start(bf16[2,192,768]{2,1,0:T(8,128)(2,1)S(1)} %pad_maximum_fusion.4.refs_0_), channel_id=1, source_target_pairs={{0,4},{4,0},{1,5},{5,1},{2,6},{6,2},{3,7},{7,3},{8,12},{12,8},{9,1... | collective-permute-start | bytes 1769480 | tf_op jit(solution)/shard_map/ppermute | solution.py:1055
  278.4 9.2 %collective-permute-start.43 = (bf16[2,192,768]{2,1,0:T(8,128)(2,1)S(1)}, bf16[2,192,768]{2,1,0:T(8,128)(2,1)S(1)}, u32[]{:S(2)}, u32[]{:S(2)}) collective-permute-start(bf16[2,192,768]{2,1,0:T(8,128)(2,1)S(1)} %collective-permute-done.41.refs_1_), channel_id=1, source_target_pairs={{0,4},{4,0},{1,5},{5,1},{2,6},{6,2},{3,7},{7,3},{8,12},{12,8},{9,1... | collective-permute-start | bytes 1769480 | tf_op jit(solution)/shard_map/ppermute | solution.py:1055
  286.3 18.5 %collective-permute-start.39 = (bf16[2,4,24,3072]{3,2,1,0:T(8,128)(2,1)S(1)}, bf16[2,4,24,3072]{3,2,1,0:T(8,128)(2,1)S(1)}, u32[]{:S(2)}, u32[]{:S(2)}) collective-permute-start(bf16[2,4,24,3072]{3,2,1,0:T(8,128)(2,1)S(1)} %pad_maximum_fusion.1.refs_0_), channel_id=1, source_target_pairs={{0,16},{4,12},{8,24},{12,4},{16,0},{20,28},{24,8},{28,20},{1,17},{... | collective-permute-start | bytes 3538952 | tf_op jit(solution)/shard_map/ppermute | solution.py:1055
  296.1 4.1 %collective-permute-start.44 = (f32[92,128]{1,0:T(8,128)S(1)}, f32[92,128]{1,0:T(8,128)S(1)}, u32[]{:S(2)}, u32[]{:S(2)}) collective-permute-start(f32[92,128]{1,0:T(8,128)S(1)} %pad_maximum_fusion.6), channel_id=1, source_target_pairs={{0,1},{1,0},{2,3},{3,2},{4,5},{5,4},{6,7},{7,6},{8,9},{9,8},{10,11... | collective-permute-start | bytes 141320 | tf_op jit(solution)/shard_map/ppermute | solution.py:1055
  300.9 3.8 %collective-permute-start.45 = (f32[92,128]{1,0:T(8,128)S(1)}, f32[92,128]{1,0:T(8,128)S(1)}, u32[]{:S(2)}, u32[]{:S(2)}) collective-permute-start(f32[92,128]{1,0:T(8,128)S(1)} %fusion.39), channel_id=1, source_target_pairs={{0,2},{1,3},{2,0},{3,1},{4,6},{5,7},{6,4},{7,5},{8,10},{9,11},{10,... | collective-permute-start | bytes 141320 | tf_op jit(solution)/shard_map/ppermute | solution.py:1055
  301.3 9.1 %collective-permute-start.46 = (bf16[2,4,24,3072]{3,2,1,0:T(8,128)(2,1)S(1)}, bf16[2,4,24,3072]{3,2,1,0:T(8,128)(2,1)}, u32[]{:S(2)}, u32[]{:S(2)}) collective-permute-start(bf16[2,4,24,3072]{3,2,1,0:T(8,128)(2,1)S(1)} %pad_maximum_fusion.1.refs_0_), channel_id=1, source_target_pairs={{0,4},{4,0},{1,5},{5,1},{2,6},{6,2},{3,7},{7,3},{8,12},{12,8},{9,1... | collective-permute-start | bytes 3538952 | tf_op jit(solution)/shard_map/ppermute | solution.py:1055
  304.8 5.7 %collective-permute-start.47 = (bf16[2,4,24,3072]{3,2,1,0:T(8,128)(2,1)S(1)}, bf16[2,4,24,3072]{3,2,1,0:T(8,128)(2,1)}, u32[]{:S(2)}, u32[]{:S(2)}) collective-permute-start(bf16[2,4,24,3072]{3,2,1,0:T(8,128)(2,1)S(1)} %collective-permute-done.39.refs_1_), channel_id=1, source_target_pairs={{0,4},{4,0},{1,5},{5,1},{2,6},{6,2},{3,7},{7,3},{8,12},{12,8},{9,1... | collective-permute-start | bytes 3538952 | tf_op jit(solution)/shard_map/ppermute | solution.py:1055
  (40 other events, 347.5 us)
